TPU v7x, 32 devices: a whole 2x2x4 slice. The times are simulated.
32 devices in a mesh: groups: 2 (over x), src: 16 (over z, y, core).
Axes of the slice: x: 2, y: 2, z: 4, core: 2. Of those that a mesh axis runs over, the one named last changes fastest.
Arguments:
- source_feats: float32 [3072, 128], P(('groups', 'src')), parts along dimension 0, may hold values from -5 to 5, as said below
- target_feats: float32 [4096, 128], P(('groups', 'src')), parts along dimension 0, may hold values from -5 to 5, as said below
- log_a: float32 [3072], P(('groups', 'src')), parts along dimension 0, may hold values from -1 to 1
- log_b: float32 [4096], P(('groups', 'src')), parts along dimension 0, may hold values from -1 to 1
Outputs:
- f_pot: float32 [3072], P(('groups', 'src')), parts along dimension 0
- g_pot: float32 [4096], P(('groups', 'src')), parts along dimension 0
- src_moved: float32 [3072, 128], P(('groups', 'src')), parts along dimension 0
- tgt_moved: float32 [4096, 128], P(('groups', 'src')), parts along dimension 0
There are 2 independent parts, one for each index of `groups`. A program takes and returns all parts, laid end to end along the dimension named above; each array names one. Nothing has to cross between parts.
Inputs may be any that keep to these rules, and one draw needn't show every extreme that they name: `source_feats`: entries are real-valued features. `target_feats`: entries are real-valued features.
All inputs are finite; a program needn't handle non-finite values.
Results may differ from a plain program's by a relative error of at most 0.0003.
Values sent between devices are 32-bit elements; how exact they have to be, the bound alone decides.
No kernel may reach another device: no remote copies, remote signals or barrier semaphores. Data moves between devices by JAX's collectives and lax.ppermute only.
A program may use at most 128 MiB of HBM per device.

v0:
```python
import jax
import jax.numpy as jnp
from jax import lax
from jax.sharding import PartitionSpec as P

ITERS = 3


EPS = 0.05


def merged(part, axis, combine):
    gathered = jax.tree.map(lambda a: lax.all_gather(a, axis), part)

    def take(source):
        return jax.tree.map(lambda a: lax.dynamic_index_in_dim(a, source, 0, False), gathered)

    return lax.fori_loop(
        1, lax.axis_size(axis), lambda source, state: combine(state, take(source)), take(0)
    )


def pair_cost(rows, cols, rows_sq, cols_sq, width):
    inner = jnp.dot(
        rows, cols.T, precision=lax.Precision.HIGHEST, preferred_element_type=jnp.float32
    )
    return (rows_sq[:, None] + cols_sq[None, :] - 2.0 * inner) / width


def row_update(cost, g_pot, log_mass):
    scores = (g_pot[None, :] - cost) / EPS
    top = jnp.max(scores, axis=1)
    total = jnp.sum(jnp.exp(scores - top[:, None]), axis=1)
    return EPS * log_mass - EPS * (top + jnp.log(total))


def combine_pairs(first, second):
    top = jnp.maximum(first[0], second[0])
    total = first[1] * jnp.exp(first[0] - top) + second[1] * jnp.exp(second[0] - top)
    return (top, total)


def per_device(source_feats, target_feats, log_a, log_b):
    width = source_feats.shape[1]
    rows = target_feats.shape[0]
    tgt_all, log_b_all = (
        lax.all_gather(target_feats, "src", axis=0, tiled=True),
        lax.all_gather(log_b, "src", axis=0, tiled=True),
    )
    sq_src = jnp.sum(source_feats * source_feats, axis=1)
    sq_tgt = jnp.sum(tgt_all * tgt_all, axis=1)
    cost = pair_cost(source_feats, tgt_all, sq_src, sq_tgt, width)
    g_pot = jnp.zeros((tgt_all.shape[0],), jnp.float32)
    f_pot = jnp.zeros((source_feats.shape[0],), jnp.float32)
    for step in range(ITERS):
        f_pot = row_update(cost, g_pot, log_a)
        scores = (f_pot[:, None] - cost) / EPS
        local_top = jnp.max(scores, axis=0)
        local_total = jnp.sum(jnp.exp(scores - local_top[None, :]), axis=0)
        top, total = merged((local_top, local_total), "src", combine_pairs)
        g_pot = EPS * log_b_all - EPS * (top + jnp.log(total))
    plan = jnp.exp((f_pot[:, None] + g_pot[None, :] - cost) / EPS)
    carried = jnp.dot(
        plan, tgt_all, precision=lax.Precision.HIGHEST, preferred_element_type=jnp.float32
    )
    src_moved = carried / jnp.sum(plan, axis=1)[:, None]
    own_start = lax.axis_index("src") * rows
    g_own = lax.dynamic_slice_in_dim(g_pot, own_start, rows)
    gathered = lax.psum_scatter(
        lax.dot_general(
            plan,
            source_feats,
            (((0,), (0,)), ((), ())),
            precision=lax.Precision.HIGHEST,
            preferred_element_type=jnp.float32,
        ),
        "src",
        scatter_dimension=0,
        tiled=True,
    )
    tgt_moved = gathered / jnp.exp(log_b)[:, None]
    return (f_pot, g_own, src_moved, tgt_moved)


def solution(mesh):
    return jax.shard_map(
        per_device,
        mesh=mesh,
        in_specs=(
            P(("groups", "src"), None),
            P(("groups", "src"), None),
            P(("groups", "src")),
            P(("groups", "src")),
        ),
        out_specs=(
            P(("groups", "src")),
            P(("groups", "src")),
            P(("groups", "src"), None),
            P(("groups", "src"), None),
        ),
        check_vma=False,
    )
```

profile of v0, /device:TPU:0, one launch (start us, length us, event | category | flops | bytes accessed | tf_op | source)
XLA Modules:
  0.0 241.7 jit_solution(13964520722538550230)
XLA Ops:
  7.2 0.0 copy-start.4
  7.2 0.0 all-gather.9.cloned.1.call-start
  7.2 0.7 all-gather.9.cloned.1.call-update
  7.9 0.0 reduce-scatter.2.cloned.1.call-start
  8.0 0.0 copy-start.7
  8.0 0.6 copy-done.7
  8.6 23.0 %all-gather.6 = f32[16,1,128]{2,1,0:T(1,128)S(1)} all-gather(f32[1,1,128]{2,1,0:T(1,128)S(1)} %bitcast.33), channel_id=1, replica_groups=mesh['groups'=2,'src'=16] {'src'}, dimensions={0}, use_global_device_ids=true | all-gather | bytes 8704 | tf_op jit(solution)/shard_map/all_gather | solution.py:48
  31.6 0.0 copy-done.4
  31.6 0.1 multiply_reduce_fusion.1
  31.7 19.1 %all-gather.9.cloned.1.call-done = f32[2048,128]{1,0:T(8,128)} async-done(((f32[128,128]{1,0:T(8,128)}), f32[2048,128]{1,0:T(8,128)}) %all-gather.9.cloned.1.call-update) | async-done | bytes 1048592 | tf_op jit(solution)/shard_map/all_gather | solution.py:47
  50.8 1.7 multiply_reduce_fusion
  52.5 1.4 fusion.2
  53.9 0.0 copy-start.6
  53.9 0.3 exponential_reduce_fusion.5
  54.2 0.4 copy-done.6
  54.6 0.2 fusion.3
  54.7 19.7 %all-gather = f32[32768]{0:T(1024)S(1)} all-gather(f32[2048]{0:T(1024)S(1)} %fusion.3), channel_id=2, replica_groups=mesh['groups'=2,'src'=16] {'src'}, dimensions={0}, use_global_device_ids=true | all-gather | bytes 139264 | tf_op jit(solution)/shard_map/all_gather | solution.py:13
  74.4 0.2 exponential_reduce_fusion.4
  74.7 0.4 copy-done.1
  75.1 17.8 %all-gather.1 = f32[32768]{0:T(1024)S(1)} all-gather(f32[2048]{0:T(1024)S(1)} %exponential_reduce_fusion.4), channel_id=3, replica_groups=mesh['groups'=2,'src'=16] {'src'}, dimensions={0}, use_global_device_ids=true | all-gather | bytes 139264 | tf_op jit(solution)/shard_map/all_gather | solution.py:13
  92.9 0.7 slice-done
  93.6 1.0 while.51
  94.6 0.2 fusion.4
  94.8 0.3 exponential_reduce_fusion.3
  95.1 0.2 fusion.5
  95.2 19.1 %all-gather.2 = f32[32768]{0:T(1024)S(1)} all-gather(f32[2048]{0:T(1024)S(1)} %fusion.5), channel_id=4, replica_groups=mesh['groups'=2,'src'=16] {'src'}, dimensions={0}, use_global_device_ids=true | all-gather | bytes 139264 | tf_op jit(solution)/shard_map/all_gather | solution.py:13
  114.4 0.2 exponential_reduce_fusion.2
  114.6 0.4 copy-done.2
  115.0 17.8 %all-gather.3 = f32[32768]{0:T(1024)S(1)} all-gather(f32[2048]{0:T(1024)S(1)} %exponential_reduce_fusion.2), channel_id=5, replica_groups=mesh['groups'=2,'src'=16] {'src'}, dimensions={0}, use_global_device_ids=true | all-gather | bytes 139264 | tf_op jit(solution)/shard_map/all_gather | solution.py:13
  132.9 0.7 slice-done.1
  133.5 1.0 while.52
  134.5 0.2 fusion.6
  134.7 0.3 exponential_reduce_fusion.1
  135.0 0.0 copy-start.5
  135.0 0.2 fusion.7
  135.2 19.1 %all-gather.4 = f32[32768]{0:T(1024)S(1)} all-gather(f32[2048]{0:T(1024)S(1)} %fusion.7), channel_id=6, replica_groups=mesh['groups'=2,'src'=16] {'src'}, dimensions={0}, use_global_device_ids=true | all-gather | bytes 139264 | tf_op jit(solution)/shard_map/all_gather | solution.py:13
  154.3 0.2 exponential_reduce_fusion
  154.6 0.4 copy-done.3
  155.0 17.8 %all-gather.5 = f32[32768]{0:T(1024)S(1)} all-gather(f32[2048]{0:T(1024)S(1)} %exponential_reduce_fusion), channel_id=7, replica_groups=mesh['groups'=2,'src'=16] {'src'}, dimensions={0}, use_global_device_ids=true | all-gather | bytes 139264 | tf_op jit(solution)/shard_map/all_gather | solution.py:13
  172.8 0.7 slice-done.2
  173.5 1.0 while.53
  174.5 2.9 %fusion.8 = f32[2048,128]{1,0:T(8,128)} fusion(f32[96,128]{1,0:T(8,128)S(1)} %copy-done.4, f32[96,2048]{1,0:T(8,128)S(1)} %get-tuple-element.452, f32[2048]{0:T(1024)S(1)} %multiply_subtract_fusion, f32[96]{0:T(128)S(1)} %multiply_subtract_fusion.3), kind=kOutput, calls=%fused_computation.33 | convolution fusion | flops 302579712 | bytes 1892736 | tf_op jit(solution)/shard_map/dot_general | solution.py:70
  177.4 0.0 reduce-scatter.2.cloned.1.call-update
  177.4 0.6 dynamic_slice.88
  178.0 0.3 fusion.9
  178.3 1.7 convolution_divide_fusion
  180.1 53.3 %reduce-scatter.2.cloned.1.call-done = f32[128,128]{1,0:T(8,128)} async-done(((f32[2048,128]{1,0:T(8,128)}), f32[128,128]{1,0:T(8,128)}) %reduce-scatter.2.cloned.1.call-update) | async-done | bytes 65552 | tf_op jit(solution)/shard_map/reduce_scatter | solution.py:69
  233.3 1.6 broadcast_divide_fusion
  (116 shorter events, 1.8 us)
Async XLA Ops:
  7.2 24.4 %copy-start.4 = (f32[96,128]{1,0:T(8,128)S(1)}, f32[96,128]{1,0:T(8,128)}, u32[]{:S(2)}) copy-start(f32[96,128]{1,0:T(8,128)} %param.10) | copy-start | bytes 147460
  7.2 43.7 %all-gather.9.cloned.1.call-start = ((), (), s32[]{:S(2)}) async-start(), calls=%async_computation.1 | async-start | bytes 1114112 | tf_op jit(solution)/shard_map/all_gather | solution.py:47
  7.9 225.4 %reduce-scatter.2.cloned.1.call-start = ((), (), s32[]{:S(2)}) async-start(), calls=%async_computation.2 | async-start | bytes 1114112 | tf_op jit(solution)/shard_map/reduce_scatter | solution.py:69
  8.0 0.7 copy-start.7
  50.8 1.7 copy-start
  53.9 0.7 copy-start.6
  74.4 0.6 copy-start.1
  92.9 0.7 slice-start
  114.4 0.6 copy-start.2
  132.8 0.7 slice-start.1
  135.0 43.3 %copy-start.5 = (f32[96]{0:T(128)}, f32[96]{0:T(128)S(1)}, u32[]{:S(2)}) copy-start(f32[96]{0:T(128)S(1)} %multiply_subtract_fusion.3) | copy-start | bytes 1156
  154.3 0.6 copy-start.3
  172.8 0.7 slice-start.2
Sparse Core Ops, SparseCore 0:
  10.2 40.6 all-gather.8
  177.5 55.7 reduce-scatter.1
where the time goes:
time: 242 us
  blocking collectives  134 us (55%)
  waiting for transfers between devices  73.1 us (30%)
  between operations  14.2 us (6%)
  other arithmetic  6.74 us (3%)
  matrix products  5.96 us (2%)
  local copies, waits for them, and re-layouts  5.86 us (2%)
    all_gather x6, blocking collectives, merged(): gathered = jax.tree.map(lambda a: lax.all_gather(a, axis), part)  111 us
    reduce_scatter x1, waiting for transfers between devices, per_device(): lax.psum_scatter(lax.dot_general(plan, source_feats, (((0,), (0,)), ((),...  53.3 us
    all_gather x1, blocking collectives, per_device(): lax.all_gather(log_b, 'src', axis=0, tiled=True)  23 us
    all_gather x1, waiting for transfers between devices, per_device(): lax.all_gather(target_feats, 'src', axis=0, tiled=True)  19.1 us
  transfers between devices with their start and end apart: 2, of which 2 were waited for; matrix products, arithmetic and copies ran while one was open for 1% of the time, Pallas kernels for 0%

commit v1 on v0

--- a/solution.py
+++ b/solution.py
@@ -1,12 +1,242 @@
+import functools
+
 import jax
 import jax.numpy as jnp
 from jax import lax
+from jax.experimental import pallas as pl
+from jax.experimental.pallas import tpu as pltpu
 from jax.sharding import PartitionSpec as P
 
 ITERS = 3
-
-
 EPS = 0.05
+LN2 = 0.6931471805599453
+LOG2E = 1.4426950408889634
+SAFE = 2.0**30
+REPLICATED_BYTES = 24 * 2**20
+HI = lax.Precision.HIGHEST
+
+
+def split3(a):
+    first = a.astype(jnp.bfloat16)
+    rest = a - first.astype(jnp.float32)
+    second = rest.astype(jnp.bfloat16)
+    third = (rest - second.astype(jnp.float32)).astype(jnp.bfloat16)
+    return first, second, third
+
+
+def nt_dot(a, b, precision=None):
+    return lax.dot_general(
+        a, b, (((1,), (1,)), ((), ())), precision=precision, preferred_element_type=jnp.float32
+    )
+
+
+def whole_group_kernel(n, s_dev, t_dev, blk, *refs):
+    pieces = refs[: -13]
+    f_ref, g_ref, sm_ref, tm_ref = refs[-13:-9]
+    e_ref, xs, ys, la_col, u_col, fm, rows_p, cols_p, acc = refs[-9:]
+    feat = pieces[0].shape[1]
+    rows = s_dev + t_dev + 8
+    k = LOG2E / (feat * EPS)
+    sources, targets = n * s_dev, n * t_dev
+
+    blocks = [(ref, at) for ref in pieces for at in range(0, ref.shape[0], rows)]
+    las, lbs, g1s = [], [], []
+    ones = jnp.ones((8, feat), jnp.float32)
+    for d, (ref, at) in enumerate(blocks):
+        x1, x2, x3 = split3(ref[at : at + s_dev, :] * (2.0 * k))
+        xs[d * s_dev : (d + 1) * s_dev, :] = jnp.concatenate([x1, x1, x2, x2, x1, x3], 1)
+        y = ref[at + s_dev : at + s_dev + t_dev, :]
+        y1, y2, y3 = split3(y)
+        ys[d * t_dev : (d + 1) * t_dev, :] = jnp.concatenate([y1, y2, y1, y2, y3, y1], 1)
+        g1s.append(nt_dot(ones, y * y, HI)[0:1, :])
+        lbs.append(ref[at + s_dev + t_dev : at + s_dev + t_dev + 1, :])
+        las.append(ref[at + s_dev + t_dev + 1 : at + s_dev + t_dev + 2, :])
+    g1 = jnp.concatenate(g1s, 1) * (-k)
+    mass_b = jnp.exp(jnp.concatenate(lbs, 1))
+    la_t = jnp.exp(jnp.concatenate(las, 0)).T
+    for d in range(n):
+        la_col[d * s_dev : (d + 1) * s_dev, :] = la_t[:s_dev, d : d + 1]
+
+    steps = sources // blk
+
+    def at_block(i):
+        return pl.ds(pl.multiple_of(i * blk, blk), blk)
+
+    def column_part(e, u):
+        return jnp.sum((e * u).reshape(blk // 8, 8, targets), axis=0)
+
+    def first(i, state):
+        low, high = state
+        s = at_block(i)
+        t = nt_dot(xs[s, :], ys[...]) + g1
+        top = jnp.max(t, axis=1, keepdims=True)
+        e = jnp.exp2(t - top)
+        e_ref[s, :] = e
+        r = jnp.sum(e, axis=1, keepdims=True)
+        u = la_col[s, :] / r
+        fm[s, :] = top
+        acc[...] += column_part(e, u)
+        return low, high
+
+    def later(v, i, state):
+        low, high = state
+        s = at_block(i)
+        e = e_ref[s, :]
+        r = jnp.sum(e * v, axis=1, keepdims=True)
+        u = la_col[s, :] / r
+        u_col[s, :] = u
+        acc[...] += column_part(e, u)
+        return jnp.minimum(low, r), jnp.maximum(high, r)
+
+    v = None
+    low, high = jnp.ones((blk, 1), jnp.float32), jnp.ones((blk, 1), jnp.float32)
+    worst_low, worst_high = jnp.ones((1, targets), jnp.float32), jnp.ones((1, targets), jnp.float32)
+    for step in range(ITERS):
+        acc[...] = jnp.zeros_like(acc)
+        body = first if step == 0 else functools.partial(later, v)
+        low, high = lax.fori_loop(0, steps, body, (low, high))
+        total = jnp.sum(acc[...], axis=0, keepdims=True)
+        worst_low = jnp.minimum(worst_low, total)
+        worst_high = jnp.maximum(worst_high, total)
+        v = mass_b / total
+    safe = (
+        (jnp.min(low) > 1.0 / SAFE)
+        & (jnp.max(high) < SAFE)
+        & (jnp.min(worst_low) > 1.0 / SAFE)
+        & (jnp.max(worst_high) < SAFE)
+    )
+
+    x_own = pieces[0][0:s_dev, :]
+    sq_own = k * jnp.sum(x_own * x_own, axis=1, keepdims=True)
+
+    @pl.when(safe)
+    def _():
+        u_own = u_col[0:s_dev, :]
+        f_ref[...] = EPS * jnp.log(u_own) + (EPS * LN2) * (sq_own - fm[0:s_dev, :])
+        g_ref[...] = EPS * jnp.log(v[:, 0:t_dev])
+        rows_p[...] = e_ref[0:s_dev, :] * v
+        cols_p[...] = e_ref[:, 0:t_dev] * u_col[...] * (1.0 / total[:, 0:t_dev])
+
+    @pl.when(jnp.logical_not(safe))
+    def _():
+        log_b = jnp.log2(mass_b)
+
+        def inner(i, carry):
+            s = at_block(i)
+            e_ref[s, :] = nt_dot(xs[s, :], ys[...])
+            return carry
+
+        lax.fori_loop(0, steps, inner, 0)
+
+        def potentials(step, g):
+            def row(i, carry):
+                s = at_block(i)
+                t = e_ref[s, :] + g
+                top = jnp.max(t, axis=1, keepdims=True)
+                total = jnp.sum(jnp.exp2(t - top), axis=1, keepdims=True)
+                fm[s, :] = jnp.log2(la_col[s, :]) - top - jnp.log2(total)
+                return carry
+
+            lax.fori_loop(0, steps, row, 0)
+
+            def column_top(i, top):
+                s = at_block(i)
+                return jnp.maximum(top, jnp.max(e_ref[s, :] + fm[s, :], axis=0, keepdims=True))
+
+            top = lax.fori_loop(0, steps, column_top, jnp.full((1, targets), -jnp.inf, jnp.float32))
+
+            def column_total(i, total):
+                s = at_block(i)
+                e = jnp.exp2(e_ref[s, :] + fm[s, :] - top)
+                return total + jnp.sum(e, axis=0, keepdims=True)
+
+            total = lax.fori_loop(0, steps, column_total, jnp.zeros((1, targets), jnp.float32))
+            return log_b - top - jnp.log2(total)
+
+        g = lax.fori_loop(0, ITERS, potentials, g1)
+        f_ref[...] = (EPS * LN2) * (fm[0:s_dev, :] + sq_own)
+        g_ref[...] = (EPS * LN2) * (g[:, 0:t_dev] - g1[:, 0:t_dev])
+        rows_p[...] = jnp.exp2(e_ref[0:s_dev, :] + fm[0:s_dev, :] + g)
+        own = jnp.exp2(e_ref[:, 0:t_dev] + fm[...] + g[:, 0:t_dev])
+        cols_p[...] = own * (1.0 / mass_b[:, 0:t_dev])
+
+    plan_rows = rows_p[...]
+    mass = jnp.sum(plan_rows, axis=1, keepdims=True)
+    p1, p2, p3 = split3(plan_rows)
+    y1, y2, y3 = ys[:, 0:feat], ys[:, feat : 2 * feat], ys[:, 4 * feat : 5 * feat]
+
+    def nn(a, b):
+        return jnp.dot(a, b, preferred_element_type=jnp.float32)
+
+    moved = nn(p1, y1) + ((nn(p1, y2) + nn(p2, y1)) + (nn(p2, y2) + nn(p1, y3) + nn(p3, y1)))
+    sm_ref[...] = moved / mass
+
+    def tn(a, b):
+        return lax.dot_general(a, b, (((0,), (0,)), ((), ())), preferred_element_type=jnp.float32)
+
+    q1, q2, q3 = split3(cols_p[...])
+    x1, x2, x3 = xs[:, 0:feat], xs[:, 2 * feat : 3 * feat], xs[:, 5 * feat : 6 * feat]
+    moved = tn(q1, x1) + ((tn(q1, x2) + tn(q2, x1)) + (tn(q2, x2) + tn(q1, x3) + tn(q3, x1)))
+    tm_ref[...] = moved * (1.0 / (2.0 * k))
+
+
+def exchange(block, axis):
+    n = lax.axis_size(axis)
+
+    def swap(a, bits):
+        return lax.ppermute(a, axis, [(i, i ^ bits) for i in range(n)])
+
+    far = [swap(block, bits) for bits in range(4, n, 4)]
+    line = [block] + far
+    side = [swap(a, 2) for a in line]
+    mine = jnp.concatenate(line + side, axis=0)
+    return [mine, swap(mine, 1)]
+
+
+def per_device_whole(source_feats, target_feats, log_a, log_b):
+    n = lax.axis_size("src")
+    s_dev, feat = source_feats.shape
+    t_dev = target_feats.shape[0]
+    block = jnp.concatenate(
+        [
+            source_feats,
+            target_feats,
+            log_b[None, :],
+            jnp.pad(log_a, (0, feat - s_dev))[None, :],
+            jnp.zeros((6, feat), jnp.float32),
+        ],
+        axis=0,
+    )
+    pieces = exchange(block, "src")
+    sources, targets = n * s_dev, n * t_dev
+    blk = 256
+    f32, b16 = jnp.float32, jnp.bfloat16
+    vmem = pl.BlockSpec(memory_space=pltpu.VMEM)
+    f_pot, g_pot, src_moved, tgt_moved = pl.pallas_call(
+        functools.partial(whole_group_kernel, n, s_dev, t_dev, blk),
+        out_shape=[
+            jax.ShapeDtypeStruct((s_dev, 1), f32),
+            jax.ShapeDtypeStruct((1, t_dev), f32),
+            jax.ShapeDtypeStruct((s_dev, feat), f32),
+            jax.ShapeDtypeStruct((t_dev, feat), f32),
+        ],
+        in_specs=[vmem] * len(pieces),
+        out_specs=[vmem] * 4,
+        scratch_shapes=[
+            pltpu.VMEM((sources, targets), f32),
+            pltpu.VMEM((sources, 6 * feat), b16),
+            pltpu.VMEM((targets, 6 * feat), b16),
+            pltpu.VMEM((sources, 1), f32),
+            pltpu.VMEM((sources, 1), f32),
+            pltpu.VMEM((sources, 1), f32),
+            pltpu.VMEM((s_dev, targets), f32),
+            pltpu.VMEM((sources, t_dev), f32),
+            pltpu.VMEM((8, targets), f32),
+        ],
+        compiler_params=pltpu.CompilerParams(vmem_limit_bytes=56 * 2**20),
+        name="whole_group",
+    )(*pieces)
+    return f_pot.reshape(s_dev), g_pot.reshape(t_dev), src_moved, tgt_moved
 
 
 def merged(part, axis, combine):
@@ -21,9 +251,7 @@
 
 
 def pair_cost(rows, cols, rows_sq, cols_sq, width):
-    inner = jnp.dot(
-        rows, cols.T, precision=lax.Precision.HIGHEST, preferred_element_type=jnp.float32
-    )
+    inner = jnp.dot(rows, cols.T, precision=HI, preferred_element_type=jnp.float32)
     return (rows_sq[:, None] + cols_sq[None, :] - 2.0 * inner) / width
 
 
@@ -40,7 +268,7 @@
     return (top, total)
 
 
-def per_device(source_feats, target_feats, log_a, log_b):
+def per_device_rows(source_feats, target_feats, log_a, log_b):
     width = source_feats.shape[1]
     rows = target_feats.shape[0]
     tgt_all, log_b_all = (
@@ -60,9 +288,7 @@
         top, total = merged((local_top, local_total), "src", combine_pairs)
         g_pot = EPS * log_b_all - EPS * (top + jnp.log(total))
     plan = jnp.exp((f_pot[:, None] + g_pot[None, :] - cost) / EPS)
-    carried = jnp.dot(
-        plan, tgt_all, precision=lax.Precision.HIGHEST, preferred_element_type=jnp.float32
-    )
+    carried = jnp.dot(plan, tgt_all, precision=HI, preferred_element_type=jnp.float32)
     src_moved = carried / jnp.sum(plan, axis=1)[:, None]
     own_start = lax.axis_index("src") * rows
     g_own = lax.dynamic_slice_in_dim(g_pot, own_start, rows)
@@ -71,7 +297,7 @@
             plan,
             source_feats,
             (((0,), (0,)), ((), ())),
-            precision=lax.Precision.HIGHEST,
+            precision=HI,
             preferred_element_type=jnp.float32,
         ),
         "src",
@@ -82,21 +308,24 @@
     return (f_pot, g_own, src_moved, tgt_moved)
 
 
+def per_device(source_feats, target_feats, log_a, log_b):
+    n = lax.axis_size("src")
+    s_dev, feat = source_feats.shape
+    t_dev = target_feats.shape[0]
+    fits = 4 * n * s_dev * n * t_dev <= REPLICATED_BYTES
+    shaped = n >= 4 and n & (n - 1) == 0 and s_dev % 16 == 0 and s_dev <= feat == t_dev
+    if fits and shaped and (n * s_dev) % 256 == 0:
+        return per_device_whole(source_feats, target_feats, log_a, log_b)
+    return per_device_rows(source_feats, target_feats, log_a, log_b)
+
+
 def solution(mesh):
+    both = P(("groups", "src"), None)
+    line = P(("groups", "src"))
     return jax.shard_map(
         per_device,
         mesh=mesh,
-        in_specs=(
-            P(("groups", "src"), None),
-            P(("groups", "src"), None),
-            P(("groups", "src")),
-            P(("groups", "src")),
-        ),
-        out_specs=(
-            P(("groups", "src")),
-            P(("groups", "src")),
-            P(("groups", "src"), None),
-            P(("groups", "src"), None),
-        ),
+        in_specs=(both, both, line, line),
+        out_specs=(line, line, both, both),
         check_vma=False,
     )

time: 242 us -> 78.6 us (0.32)
  blocking collectives: 134 us -> 0 us
  waiting for transfers between devices: 73.1 us -> 13.3 us
  Pallas kernels: 0 us -> 47.5 us
  between operations: 14.2 us -> 0.67 us
  starting transfers between devices: 0.08 us -> 11.3 us
  matrix products: 5.96 us -> 0 us
  other arithmetic: 6.74 us -> 1.43 us
    all_gather x7 -> x0, blocking collectives: 134 us -> none  [the longest x6 111 us: merged(): gathered = jax.tree.map(lambda a: lax.all_gather(a, axis), part)]
    reduce_scatter x1 -> x0, waiting for transfers between devices: 53.3 us -> none  [per_device(): lax.psum_scatter(lax.dot_general(plan, source_feats, (((0,), (0,)), ((),...]
    pallas_call x0 -> x1, Pallas kernels: none -> 47.5 us  [per_device_whole(): pl.pallas_call(functools.partial(whole_group_kernel, n, s_dev, t_dev, blk...]
    all_gather x1 -> x0, waiting for transfers between devices: 19.1 us -> none  [per_device(): lax.all_gather(target_feats, 'src', axis=0, tiled=True)]
    ppermute x0 -> x8, waiting for transfers between devices: none -> 13.3 us  [swap(): return lax.ppermute(a, axis, [(i, i ^ bits) for i in range(n)])]
    ppermute x0 -> x8, starting transfers between devices: none -> 11.3 us  [swap(): return lax.ppermute(a, axis, [(i, i ^ bits) for i in range(n)])]
    dot_general x3 -> x0, matrix products: 5.96 us -> none  [the longest x1 2.88 us: per_device(): lax.dot_general(plan, source_feats, (((0,), (0,)), ((), ())), precision=l...]
    reduce_sum x9 -> x0, other arithmetic: 3.66 us -> none  [the longest x1 1.65 us: per_device(): sq_tgt = jnp.sum(tgt_all * tgt_all, axis=1)]
  transfers between devices with their start and end apart: 2 -> 8, of which waited for: 2 -> 5; matrix products, arithmetic and copies ran while one was open for 1% -> 0% of each run, Pallas kernels for 0% -> 0%
where the time goes in v1:
time: 78.6 us; the launch traced here: 78.3 us
  Pallas kernels  47.5 us (60%)
  waiting for transfers between devices  13.3 us (17%)
  starting transfers between devices  11.3 us (14%)
  local copies, waits for them, and re-layouts  4.14 us (5%)
  other arithmetic  1.43 us (2%)
    pallas_call x1, Pallas kernels, per_device_whole(): pl.pallas_call(functools.partial(whole_group_kernel, n, s_dev, t_dev, blk...  47.5 us
    ppermute x8, waiting for transfers between devices, swap(): return lax.ppermute(a, axis, [(i, i ^ bits) for i in range(n)])  13.3 us
    ppermute x8, starting transfers between devices, swap(): return lax.ppermute(a, axis, [(i, i ^ bits) for i in range(n)])  11.3 us
    concatenate x1, local copies, waits for them, and re-layouts, per_device_whole(): jnp.concatenate([source_feats, target_feats, log_b[None, :], jnp.pad(log_...  1.74 us
    unnamed x10, local copies, waits for them, and re-layouts  1.67 us
  transfers between devices with their start and end apart: 8, of which 5 were waited for; matrix products, arithmetic and copies ran while one was open for 0% of the time, Pallas kernels for 0%

profile of v1, /device:TPU:0, one launch (start us, length us, event | category | flops | bytes accessed | tf_op | source)
XLA Modules:
  0.0 78.3 jit_solution(8708085640232599994)
XLA Ops:
  0.6 0.7 pad_bitcast_fusion
  1.3 0.0 copy-start.4
  1.3 0.7 copy-done.4
  1.9 0.0 copy-start.2
  1.9 0.0 copy-start.3
  1.9 1.7 %concatenate.7 = f32[232,128]{1,0:T(8,128)S(1)} concatenate(f32[96,128]{1,0:T(8,128)} %param.4, f32[128,128]{1,0:T(8,128)} %param.5, f32[1,128]{1,0:T(1,128)S(1)} %bitcast.4, f32[1,128]{1,0:T(1,128)S(1)} %pad_bitcast_fusion, f32[6,128]{1,0:T(8,128)S(1)} %broadcast_in_dim.11), dimensions={0} | concatenate | bytes 237568 | tf_op jit(solution)/shard_map/concatenate | solution.py:200
  3.7 5.1 %collective-permute-start.2 = (f32[232,128]{1,0:T(8,128)S(1)}, f32[232,128]{1,0:T(8,128)S(1)}, u32[]{:S(2)}, u32[]{:S(2)}) collective-permute-start(f32[232,128]{1,0:T(8,128)S(1)} %concatenate.7), channel_id=1, source_target_pairs={{0,12},{1,13},{2,14},{3,15},{4,8},{5,9},{6,10},{7,11},{8,4},{9,5},... | collective-permute-start | bytes 356360 | tf_op jit(solution)/shard_map/ppermute | solution.py:187
  8.8 0.0 collective-permute-start.1
  8.8 0.6 collective-permute-start
  9.4 1.7 %collective-permute-start.3 = (f32[232,128]{1,0:T(8,128)S(1)}, f32[232,128]{1,0:T(8,128)S(1)}, u32[]{:S(2)}, u32[]{:S(2)}) collective-permute-start(f32[232,128]{1,0:T(8,128)S(1)} %concatenate.7), channel_id=1, source_target_pairs={{0,2},{1,3},{2,0},{3,1},{4,6},{5,7},{6,4},{7,5},{8,10},{9,11},{10,... | collective-permute-start | bytes 356360 | tf_op jit(solution)/shard_map/ppermute | solution.py:187
  11.1 1.9 %collective-permute-done.2 = f32[232,128]{1,0:T(8,128)S(1)} collective-permute-done((f32[232,128]{1,0:T(8,128)S(1)}, f32[232,128]{1,0:T(8,128)S(1)}, u32[]{:S(2)}, u32[]{:S(2)}) %collective-permute-start.2) | collective-permute-done | bytes 118816 | tf_op jit(solution)/shard_map/ppermute | solution.py:187
  13.0 1.7 %collective-permute-start.6 = (f32[232,128]{1,0:T(8,128)S(1)}, f32[232,128]{1,0:T(8,128)S(1)}, u32[]{:S(2)}, u32[]{:S(2)}) collective-permute-start(f32[232,128]{1,0:T(8,128)S(1)} %collective-permute-done.2), channel_id=1, source_target_pairs={{0,2},{1,3},{2,0},{3,1},{4,6},{5,7},{6,4},{7,5},{8,10},{9,11},{10,... | collective-permute-start | bytes 356360 | tf_op jit(solution)/shard_map/ppermute | solution.py:187
  14.7 4.1 %collective-permute-done.1 = f32[232,128]{1,0:T(8,128)S(1)} collective-permute-done((f32[232,128]{1,0:T(8,128)S(1)}, f32[232,128]{1,0:T(8,128)S(1)}, u32[]{:S(2)}, u32[]{:S(2)}) %collective-permute-start.1) | collective-permute-done | bytes 118816 | tf_op jit(solution)/shard_map/ppermute | solution.py:187
  18.8 1.5 %collective-permute-start.5 = (f32[232,128]{1,0:T(8,128)S(1)}, f32[232,128]{1,0:T(8,128)S(1)}, u32[]{:S(2)}, u32[]{:S(2)}) collective-permute-start(f32[232,128]{1,0:T(8,128)S(1)} %collective-permute-done.1), channel_id=1, source_target_pairs={{0,2},{1,3},{2,0},{3,1},{4,6},{5,7},{6,4},{7,5},{8,10},{9,11},{10,... | collective-permute-start | bytes 356360 | tf_op jit(solution)/shard_map/ppermute | solution.py:187
  20.3 0.0 collective-permute-done
  20.3 0.5 collective-permute-start.4
  20.9 0.0 collective-permute-done.3
  20.9 0.0 collective-permute-done.6
  20.9 3.5 %collective-permute-done.5 = f32[232,128]{1,0:T(8,128)S(1)} collective-permute-done((f32[232,128]{1,0:T(8,128)S(1)}, f32[232,128]{1,0:T(8,128)S(1)}, u32[]{:S(2)}, u32[]{:S(2)}) %collective-permute-start.5) | collective-permute-done | bytes 118816 | tf_op jit(solution)/shard_map/ppermute | solution.py:187
  24.4 1.3 %collective-permute-done.4 = f32[232,128]{1,0:T(8,128)S(1)} collective-permute-done((f32[232,128]{1,0:T(8,128)S(1)}, f32[232,128]{1,0:T(8,128)S(1)}, u32[]{:S(2)}, u32[]{:S(2)}) %collective-permute-start.4) | collective-permute-done | bytes 118816 | tf_op jit(solution)/shard_map/ppermute | solution.py:187
  25.6 0.0 copy-done.2
  25.7 0.0 copy-done.3
  25.7 0.1 concatenate.8.refs_0_
  25.7 0.0 copy-start
  25.7 0.1 collective-permute-start.7
  25.8 2.5 %collective-permute-done.7.refs_1_ = f32[1856,128]{1,0:T(8,128)S(1)} collective-permute-done((f32[1856,128]{1,0:T(8,128)S(1)}, f32[1856,128]{1,0:T(8,128)S(1)}, u32[]{:S(2)}, u32[]{:S(2)}) %collective-permute-start.7) | collective-permute-done | bytes 950304 | tf_op jit(solution)/shard_map/ppermute | solution.py:187
  28.3 0.0 copy-done
  28.3 0.0 copy-start.1
  28.3 1.0 %copy-done.1 = f32[1856,128]{1,0:T(8,128)} copy-done((f32[1856,128]{1,0:T(8,128)}, f32[1856,128]{1,0:T(8,128)S(1)}, u32[]{:S(2)}) %copy-start.1) | copy-done | bytes 950296
  29.3 47.5 %whole_group.1 = (f32[96,1]{1,0:T(8,128)}, f32[1,128]{1,0:T(1,128)}, f32[96,128]{1,0:T(8,128)}, f32[128,128]{1,0:T(8,128)}) custom-call(f32[1856,128]{1,0:T(8,128)} %copy-done, f32[1856,128]{1,0:T(8,128)} %copy-done.1), custom_call_target="tpu_custom_call" | custom-call | tf_op jit(solution)/shard_map/whole_group/pallas_call | solution.py:215
  76.9 1.4 %reduce = f32[96]{0:T(128)} reduce(f32[96,1]{1,0:T(8,128)} %get-tuple-element.8, f32[]{:T(128)} %constant.6), dimensions={1}, to_apply=%get-tuple-element.8.reduce_sub_computation | reduce | bytes 772 | tf_op jit(solution)/shard_map/whole_group/pallas_call | solution.py:215
  (1 shorter events, 0.0 us)
Async XLA Ops:
  1.3 0.7 copy-start.4
  1.9 23.7 %copy-start.2 = (f32[128,128]{1,0:T(8,128)S(1)}, f32[128,128]{1,0:T(8,128)}, u32[]{:S(2)}) copy-start(f32[128,128]{1,0:T(8,128)} %param.5) | copy-start | bytes 196612
  1.9 23.7 %copy-start.3 = (f32[96,128]{1,0:T(8,128)S(1)}, f32[96,128]{1,0:T(8,128)}, u32[]{:S(2)}) copy-start(f32[96,128]{1,0:T(8,128)} %param.4) | copy-start | bytes 147460
  3.7 9.3 %collective-permute-start.2 = (f32[232,128]{1,0:T(8,128)S(1)}, f32[232,128]{1,0:T(8,128)S(1)}, u32[]{:S(2)}, u32[]{:S(2)}) collective-permute-start(f32[232,128]{1,0:T(8,128)S(1)} %concatenate.7), channel_id=1, source_target_pairs={{0,12},{1,13},{2,14},{3,15},{4,8},{5,9},{6,10},{7,11},{8,4},{9,5},... | collective-permute-start | bytes 356360 | tf_op jit(solution)/shard_map/ppermute | solution.py:187
  8.8 10.0 %collective-permute-start.1 = (f32[232,128]{1,0:T(8,128)S(1)}, f32[232,128]{1,0:T(8,128)S(1)}, u32[]{:S(2)}, u32[]{:S(2)}) collective-permute-start(f32[232,128]{1,0:T(8,128)S(1)} %concatenate.7), channel_id=1, source_target_pairs={{0,8},{1,9},{2,10},{3,11},{4,12},{5,13},{6,14},{7,15},{8,0},{9,1},... | collective-permute-start | bytes 356360 | tf_op jit(solution)/shard_map/ppermute | solution.py:187
  8.8 11.5 %collective-permute-start = (f32[232,128]{1,0:T(8,128)S(1)}, f32[232,128]{1,0:T(8,128)S(1)}, u32[]{:S(2)}, u32[]{:S(2)}) collective-permute-start(f32[232,128]{1,0:T(8,128)S(1)} %concatenate.7), channel_id=1, source_target_pairs={{0,4},{1,5},{2,6},{3,7},{4,0},{5,1},{6,2},{7,3},{8,12},{9,13},{10,... | collective-permute-start | bytes 356360 | tf_op jit(solution)/shard_map/ppermute | solution.py:187
  9.4 11.4 %collective-permute-start.3 = (f32[232,128]{1,0:T(8,128)S(1)}, f32[232,128]{1,0:T(8,128)S(1)}, u32[]{:S(2)}, u32[]{:S(2)}) collective-permute-start(f32[232,128]{1,0:T(8,128)S(1)} %concatenate.7), channel_id=1, source_target_pairs={{0,2},{1,3},{2,0},{3,1},{4,6},{5,7},{6,4},{7,5},{8,10},{9,11},{10,... | collective-permute-start | bytes 356360 | tf_op jit(solution)/shard_map/ppermute | solution.py:187
  13.0 7.9 %collective-permute-start.6 = (f32[232,128]{1,0:T(8,128)S(1)}, f32[232,128]{1,0:T(8,128)S(1)}, u32[]{:S(2)}, u32[]{:S(2)}) collective-permute-start(f32[232,128]{1,0:T(8,128)S(1)} %collective-permute-done.2), channel_id=1, source_target_pairs={{0,2},{1,3},{2,0},{3,1},{4,6},{5,7},{6,4},{7,5},{8,10},{9,11},{10,... | collective-permute-start | bytes 356360 | tf_op jit(solution)/shard_map/ppermute | solution.py:187
  18.8 5.6 %collective-permute-start.5 = (f32[232,128]{1,0:T(8,128)S(1)}, f32[232,128]{1,0:T(8,128)S(1)}, u32[]{:S(2)}, u32[]{:S(2)}) collective-permute-start(f32[232,128]{1,0:T(8,128)S(1)} %collective-permute-done.1), channel_id=1, source_target_pairs={{0,2},{1,3},{2,0},{3,1},{4,6},{5,7},{6,4},{7,5},{8,10},{9,11},{10,... | collective-permute-start | bytes 356360 | tf_op jit(solution)/shard_map/ppermute | solution.py:187
  20.3 5.3 %collective-permute-start.4 = (f32[232,128]{1,0:T(8,128)S(1)}, f32[232,128]{1,0:T(8,128)S(1)}, u32[]{:S(2)}, u32[]{:S(2)}) collective-permute-start(f32[232,128]{1,0:T(8,128)S(1)} %collective-permute-done), channel_id=1, source_target_pairs={{0,2},{1,3},{2,0},{3,1},{4,6},{5,7},{6,4},{7,5},{8,10},{9,11},{10,... | collective-permute-start | bytes 356360 | tf_op jit(solution)/shard_map/ppermute | solution.py:187
  25.7 2.6 %copy-start = (f32[1856,128]{1,0:T(8,128)}, f32[1856,128]{1,0:T(8,128)S(1)}, u32[]{:S(2)}) copy-start(f32[1856,128]{1,0:T(8,128)S(1)} %concatenate.8.refs_0_) | copy-start | bytes 2850820
  25.7 2.6 %collective-permute-start.7 = (f32[1856,128]{1,0:T(8,128)S(1)}, f32[1856,128]{1,0:T(8,128)S(1)}, u32[]{:S(2)}, u32[]{:S(2)}) collective-permute-start(f32[1856,128]{1,0:T(8,128)S(1)} %concatenate.8.refs_0_), channel_id=1, source_target_pairs={{0,1},{1,0},{2,3},{3,2},{4,5},{5,4},{6,7},{7,6},{8,9},{9,8},{10,11... | collective-permute-start | bytes 2850824 | tf_op jit(solution)/shard_map/ppermute | solution.py:187
  28.3 1.0 %copy-start.1 = (f32[1856,128]{1,0:T(8,128)}, f32[1856,128]{1,0:T(8,128)S(1)}, u32[]{:S(2)}) copy-start(f32[1856,128]{1,0:T(8,128)S(1)} %collective-permute-done.7.refs_1_) | copy-start | bytes 2850820

commit v2 on v1

--- a/solution.py
+++ b/solution.py
@@ -12,6 +12,8 @@
 LN2 = 0.6931471805599453
 LOG2E = 1.4426950408889634
 SAFE = 2.0**30
+WIDE = 2.0**60
+PARTS = 8
 REPLICATED_BYTES = 24 * 2**20
 HI = lax.Precision.HIGHEST
 
@@ -31,88 +33,107 @@
 
 
 def whole_group_kernel(n, s_dev, t_dev, blk, *refs):
-    pieces = refs[: -13]
-    f_ref, g_ref, sm_ref, tm_ref = refs[-13:-9]
-    e_ref, xs, ys, la_col, u_col, fm, rows_p, cols_p, acc = refs[-9:]
+    pieces = refs[:-14]
+    f_ref, g_ref, sm_ref, tm_ref = refs[-14:-10]
+    e_ref, xs, ys, la_col, u_col, rows_p, cols_p, acc, mb0, mb1 = refs[-10:]
     feat = pieces[0].shape[1]
     rows = s_dev + t_dev + 8
     k = LOG2E / (feat * EPS)
     sources, targets = n * s_dev, n * t_dev
 
     blocks = [(ref, at) for ref in pieces for at in range(0, ref.shape[0], rows)]
-    las, lbs, g1s = [], [], []
-    ones = jnp.ones((8, feat), jnp.float32)
+    center = sum(
+        jnp.sum(ref[at + s_dev : at + s_dev + t_dev, :].reshape(t_dev // 8, 8, feat), axis=0)
+        for ref, at in blocks
+    )
+    center = jnp.sum(center, axis=0, keepdims=True) * (1.0 / targets)
+    las, lbs, norms = [], [], []
+    ones = jnp.ones((8, 3 * feat), jnp.bfloat16)
     for d, (ref, at) in enumerate(blocks):
-        x1, x2, x3 = split3(ref[at : at + s_dev, :] * (2.0 * k))
+        x1, x2, x3 = split3((ref[at : at + s_dev, :] - center) * (2.0 * k))
         xs[d * s_dev : (d + 1) * s_dev, :] = jnp.concatenate([x1, x1, x2, x2, x1, x3], 1)
-        y = ref[at + s_dev : at + s_dev + t_dev, :]
+        y = ref[at + s_dev : at + s_dev + t_dev, :] - center
         y1, y2, y3 = split3(y)
         ys[d * t_dev : (d + 1) * t_dev, :] = jnp.concatenate([y1, y2, y1, y2, y3, y1], 1)
-        g1s.append(nt_dot(ones, y * y, HI)[0:1, :])
+        norms.append(nt_dot(ones, jnp.concatenate(split3(y * y), 1))[0:1, :])
         lbs.append(ref[at + s_dev + t_dev : at + s_dev + t_dev + 1, :])
         las.append(ref[at + s_dev + t_dev + 1 : at + s_dev + t_dev + 2, :])
-    g1 = jnp.concatenate(g1s, 1) * (-k)
+    norm = jnp.concatenate(norms, 1) * k
+    shift = jnp.mean(norm, axis=1, keepdims=True)
+    g1 = shift - norm
     mass_b = jnp.exp(jnp.concatenate(lbs, 1))
     la_t = jnp.exp(jnp.concatenate(las, 0)).T
     for d in range(n):
         la_col[d * s_dev : (d + 1) * s_dev, :] = la_t[:s_dev, d : d + 1]
 
     steps = sources // blk
-
-    def at_block(i):
-        return pl.ds(pl.multiple_of(i * blk, blk), blk)
+    parts = PARTS
+    chunk, sub = targets // parts, blk // parts
 
     def column_part(e, u):
-        return jnp.sum((e * u).reshape(blk // 8, 8, targets), axis=0)
-
-    def first(i, state):
-        low, high = state
-        s = at_block(i)
-        t = nt_dot(xs[s, :], ys[...]) + g1
-        top = jnp.max(t, axis=1, keepdims=True)
-        e = jnp.exp2(t - top)
+        return jnp.sum((e * u).reshape(e.shape[0] // 8, 8, targets), axis=0)
+
+    def product(dst, i, part):
+        cols = slice(part * chunk, (part + 1) * chunk)
+        dst[:, cols] = nt_dot(xs[i * blk : (i + 1) * blk, :], ys[cols, :])
+
+    lows, highs = [], []
+
+    def absorb(src, i, part):
+        s = slice(i * blk + part * sub, i * blk + (part + 1) * sub)
+        e = jnp.exp2(src[part * sub : (part + 1) * sub, :] + g1)
         e_ref[s, :] = e
         r = jnp.sum(e, axis=1, keepdims=True)
-        u = la_col[s, :] / r
-        fm[s, :] = top
-        acc[...] += column_part(e, u)
-        return low, high
-
-    def later(v, i, state):
-        low, high = state
-        s = at_block(i)
-        e = e_ref[s, :]
-        r = jnp.sum(e * v, axis=1, keepdims=True)
-        u = la_col[s, :] / r
-        u_col[s, :] = u
-        acc[...] += column_part(e, u)
-        return jnp.minimum(low, r), jnp.maximum(high, r)
-
-    v = None
-    low, high = jnp.ones((blk, 1), jnp.float32), jnp.ones((blk, 1), jnp.float32)
-    worst_low, worst_high = jnp.ones((1, targets), jnp.float32), jnp.ones((1, targets), jnp.float32)
-    for step in range(ITERS):
+        lows.append(jnp.min(r))
+        highs.append(jnp.max(r))
+        acc[...] += column_part(e, la_col[s, :] / r)
+
+    def column_end():
+        total = jnp.sum(acc[...], axis=0, keepdims=True)
+        lows.append(jnp.min(total))
+        highs.append(jnp.max(total) * (WIDE / SAFE))
+        return total
+
+    acc[...] = jnp.zeros_like(acc)
+    bufs = (mb0, mb1)
+    for part in range(parts):
+        product(bufs[0], 0, part)
+    for i in range(steps):
+        for part in range(parts):
+            if i + 1 < steps:
+                product(bufs[(i + 1) % 2], i + 1, part)
+            absorb(bufs[i % 2], i, part)
+    total = column_end()
+
+    for _ in range(1, ITERS):
+        v = mass_b / total
         acc[...] = jnp.zeros_like(acc)
-        body = first if step == 0 else functools.partial(later, v)
-        low, high = lax.fori_loop(0, steps, body, (low, high))
-        total = jnp.sum(acc[...], axis=0, keepdims=True)
-        worst_low = jnp.minimum(worst_low, total)
-        worst_high = jnp.maximum(worst_high, total)
-        v = mass_b / total
-    safe = (
-        (jnp.min(low) > 1.0 / SAFE)
-        & (jnp.max(high) < SAFE)
-        & (jnp.min(worst_low) > 1.0 / SAFE)
-        & (jnp.max(worst_high) < SAFE)
-    )
-
-    x_own = pieces[0][0:s_dev, :]
+        for i in range(steps):
+            s = slice(i * blk, (i + 1) * blk)
+            e = e_ref[s, :]
+            r = jnp.sum(e * v, axis=1, keepdims=True)
+            lows.append(jnp.min(r))
+            highs.append(jnp.max(r))
+            u = la_col[s, :] / r
+            u_col[s, :] = u
+            acc[...] += column_part(e, u)
+        total = column_end()
+    v = mass_b / total
+    safe = (functools.reduce(jnp.minimum, lows) > 1.0 / SAFE) & (
+        functools.reduce(jnp.maximum, highs) < WIDE
+    )
+
+    x_own = pieces[0][0:s_dev, :] - center
     sq_own = k * jnp.sum(x_own * x_own, axis=1, keepdims=True)
+
+    def put_f(f):
+        wide = jnp.broadcast_to(f, (s_dev, feat))
+        wide = jnp.concatenate([wide, jnp.zeros((feat - s_dev, feat), jnp.float32)], 0)
+        f_ref[...] = wide.T[0:1, 0:s_dev]
 
     @pl.when(safe)
     def _():
-        u_own = u_col[0:s_dev, :]
-        f_ref[...] = EPS * jnp.log(u_own) + (EPS * LN2) * (sq_own - fm[0:s_dev, :])
+        put_f(EPS * jnp.log(u_col[0:s_dev, :]) + (EPS * LN2) * (sq_own + shift))
         g_ref[...] = EPS * jnp.log(v[:, 0:t_dev])
         rows_p[...] = e_ref[0:s_dev, :] * v
         cols_p[...] = e_ref[:, 0:t_dev] * u_col[...] * (1.0 / total[:, 0:t_dev])
@@ -120,6 +141,9 @@
     @pl.when(jnp.logical_not(safe))
     def _():
         log_b = jnp.log2(mass_b)
+
+        def at_block(i):
+            return pl.ds(pl.multiple_of(i * blk, blk), blk)
 
         def inner(i, carry):
             s = at_block(i)
@@ -134,50 +158,48 @@
                 t = e_ref[s, :] + g
                 top = jnp.max(t, axis=1, keepdims=True)
                 total = jnp.sum(jnp.exp2(t - top), axis=1, keepdims=True)
-                fm[s, :] = jnp.log2(la_col[s, :]) - top - jnp.log2(total)
+                u_col[s, :] = jnp.log2(la_col[s, :]) - top - jnp.log2(total)
                 return carry
 
             lax.fori_loop(0, steps, row, 0)
 
             def column_top(i, top):
                 s = at_block(i)
-                return jnp.maximum(top, jnp.max(e_ref[s, :] + fm[s, :], axis=0, keepdims=True))
+                return jnp.maximum(top, jnp.max(e_ref[s, :] + u_col[s, :], axis=0, keepdims=True))
 
             top = lax.fori_loop(0, steps, column_top, jnp.full((1, targets), -jnp.inf, jnp.float32))
 
             def column_total(i, total):
                 s = at_block(i)
-                e = jnp.exp2(e_ref[s, :] + fm[s, :] - top)
+                e = jnp.exp2(e_ref[s, :] + u_col[s, :] - top)
                 return total + jnp.sum(e, axis=0, keepdims=True)
 
             total = lax.fori_loop(0, steps, column_total, jnp.zeros((1, targets), jnp.float32))
             return log_b - top - jnp.log2(total)
 
-        g = lax.fori_loop(0, ITERS, potentials, g1)
-        f_ref[...] = (EPS * LN2) * (fm[0:s_dev, :] + sq_own)
-        g_ref[...] = (EPS * LN2) * (g[:, 0:t_dev] - g1[:, 0:t_dev])
-        rows_p[...] = jnp.exp2(e_ref[0:s_dev, :] + fm[0:s_dev, :] + g)
-        own = jnp.exp2(e_ref[:, 0:t_dev] + fm[...] + g[:, 0:t_dev])
+        g = lax.fori_loop(0, ITERS, potentials, -norm)
+        put_f((EPS * LN2) * (u_col[0:s_dev, :] + sq_own))
+        g_ref[...] = (EPS * LN2) * (g[:, 0:t_dev] + norm[:, 0:t_dev])
+        rows_p[...] = jnp.exp2(e_ref[0:s_dev, :] + u_col[0:s_dev, :] + g)
+        own = jnp.exp2(e_ref[:, 0:t_dev] + u_col[...] + g[:, 0:t_dev])
         cols_p[...] = own * (1.0 / mass_b[:, 0:t_dev])
 
     plan_rows = rows_p[...]
     mass = jnp.sum(plan_rows, axis=1, keepdims=True)
-    p1, p2, p3 = split3(plan_rows)
-    y1, y2, y3 = ys[:, 0:feat], ys[:, feat : 2 * feat], ys[:, 4 * feat : 5 * feat]
+    p1, p2, _ = split3(plan_rows)
+    y1, y2 = ys[:, 0:feat], ys[:, feat : 2 * feat]
 
     def nn(a, b):
         return jnp.dot(a, b, preferred_element_type=jnp.float32)
 
-    moved = nn(p1, y1) + ((nn(p1, y2) + nn(p2, y1)) + (nn(p2, y2) + nn(p1, y3) + nn(p3, y1)))
-    sm_ref[...] = moved / mass
+    sm_ref[...] = (nn(p1, y1) + (nn(p1, y2) + nn(p2, y1))) / mass + center
 
     def tn(a, b):
         return lax.dot_general(a, b, (((0,), (0,)), ((), ())), preferred_element_type=jnp.float32)
 
-    q1, q2, q3 = split3(cols_p[...])
-    x1, x2, x3 = xs[:, 0:feat], xs[:, 2 * feat : 3 * feat], xs[:, 5 * feat : 6 * feat]
-    moved = tn(q1, x1) + ((tn(q1, x2) + tn(q2, x1)) + (tn(q2, x2) + tn(q1, x3) + tn(q3, x1)))
-    tm_ref[...] = moved * (1.0 / (2.0 * k))
+    q1, q2, _ = split3(cols_p[...])
+    x1, x2 = xs[:, 0:feat], xs[:, 2 * feat : 3 * feat]
+    tm_ref[...] = (tn(q1, x1) + (tn(q1, x2) + tn(q2, x1))) * (1.0 / (2.0 * k)) + center
 
 
 def exchange(block, axis):
@@ -215,7 +237,7 @@
     f_pot, g_pot, src_moved, tgt_moved = pl.pallas_call(
         functools.partial(whole_group_kernel, n, s_dev, t_dev, blk),
         out_shape=[
-            jax.ShapeDtypeStruct((s_dev, 1), f32),
+            jax.ShapeDtypeStruct((1, s_dev), f32),
             jax.ShapeDtypeStruct((1, t_dev), f32),
             jax.ShapeDtypeStruct((s_dev, feat), f32),
             jax.ShapeDtypeStruct((t_dev, feat), f32),
@@ -228,12 +250,13 @@
             pltpu.VMEM((targets, 6 * feat), b16),
             pltpu.VMEM((sources, 1), f32),
             pltpu.VMEM((sources, 1), f32),
-            pltpu.VMEM((sources, 1), f32),
             pltpu.VMEM((s_dev, targets), f32),
             pltpu.VMEM((sources, t_dev), f32),
             pltpu.VMEM((8, targets), f32),
+            pltpu.VMEM((blk, targets), f32),
+            pltpu.VMEM((blk, targets), f32),
         ],
-        compiler_params=pltpu.CompilerParams(vmem_limit_bytes=56 * 2**20),
+        compiler_params=pltpu.CompilerParams(vmem_limit_bytes=36 * 2**20),
         name="whole_group",
     )(*pieces)
     return f_pot.reshape(s_dev), g_pot.reshape(t_dev), src_moved, tgt_moved

time: 78.6 us -> 68.8 us (0.88)
  Pallas kernels: 47.5 us -> 40.2 us
  other arithmetic: 1.43 us -> 0 us
  local copies, waits for them, and re-layouts: 4.14 us -> 3.13 us
    pallas_call x1, Pallas kernels: 47.5 us -> 40.2 us  [per_device_whole(): pl.pallas_call(functools.partial(whole_group_kernel, n, s_dev, t_dev, blk...]
    pallas_call x1 -> x0, other arithmetic: 1.43 us -> none  [per_device_whole(): pl.pallas_call(functools.partial(whole_group_kernel, n, s_dev, t_dev, blk...]
    unnamed x10 -> x6, local copies, waits for them, and re-layouts: 1.67 us -> 0.66 us
where the time goes in v2:
time: 68.8 us; the launch traced here: 68.5 us
  Pallas kernels  40.2 us (58%)
  waiting for transfers between devices  13.3 us (19%)
  starting transfers between devices  11.3 us (16%)
  local copies, waits for them, and re-layouts  3.13 us (5%)
    pallas_call x1, Pallas kernels, per_device_whole(): pl.pallas_call(functools.partial(whole_group_kernel, n, s_dev, t_dev, blk...  40.2 us
    ppermute x8, waiting for transfers between devices, swap(): return lax.ppermute(a, axis, [(i, i ^ bits) for i in range(n)])  13.3 us
    ppermute x8, starting transfers between devices, swap(): return lax.ppermute(a, axis, [(i, i ^ bits) for i in range(n)])  11.3 us
    concatenate x1, local copies, waits for them, and re-layouts, per_device_whole(): jnp.concatenate([source_feats, target_feats, log_b[None, :], jnp.pad(log_...  1.74 us
  transfers between devices with their start and end apart: 8, of which 5 were waited for; matrix products, arithmetic and copies ran while one was open for 0% of the time, Pallas kernels for 0%

profile of v2, /device:TPU:0, one launch (start us, length us, event | category | flops | bytes accessed | tf_op | source)
XLA Modules:
  0.0 68.5 jit_solution(4457722402914604282)
XLA Ops:
  0.6 0.7 pad_bitcast_fusion
  1.3 0.0 copy-start.2
  1.3 0.7 copy-done.2
  1.9 0.0 copy-start
  1.9 0.0 copy-start.1
  1.9 1.7 %concatenate.7 = f32[232,128]{1,0:T(8,128)S(1)} concatenate(f32[96,128]{1,0:T(8,128)} %param.4, f32[128,128]{1,0:T(8,128)} %param.5, f32[1,128]{1,0:T(1,128)S(1)} %bitcast.5, f32[1,128]{1,0:T(1,128)S(1)} %pad_bitcast_fusion, f32[6,128]{1,0:T(8,128)S(1)} %broadcast_in_dim.11), dimensions={0} | concatenate | bytes 237568 | tf_op jit(solution)/shard_map/concatenate | solution.py:222
  3.7 5.1 %collective-permute-start.2 = (f32[232,128]{1,0:T(8,128)S(1)}, f32[232,128]{1,0:T(8,128)S(1)}, u32[]{:S(2)}, u32[]{:S(2)}) collective-permute-start(f32[232,128]{1,0:T(8,128)S(1)} %concatenate.7), channel_id=1, source_target_pairs={{0,12},{1,13},{2,14},{3,15},{4,8},{5,9},{6,10},{7,11},{8,4},{9,5},... | collective-permute-start | bytes 356360 | tf_op jit(solution)/shard_map/ppermute | solution.py:209
  8.8 0.0 collective-permute-start.1
  8.8 0.6 collective-permute-start
  9.4 1.7 %collective-permute-start.3 = (f32[232,128]{1,0:T(8,128)S(1)}, f32[232,128]{1,0:T(8,128)S(1)}, u32[]{:S(2)}, u32[]{:S(2)}) collective-permute-start(f32[232,128]{1,0:T(8,128)S(1)} %concatenate.7), channel_id=1, source_target_pairs={{0,2},{1,3},{2,0},{3,1},{4,6},{5,7},{6,4},{7,5},{8,10},{9,11},{10,... | collective-permute-start | bytes 356360 | tf_op jit(solution)/shard_map/ppermute | solution.py:209
  11.1 1.9 %collective-permute-done.2 = f32[232,128]{1,0:T(8,128)S(1)} collective-permute-done((f32[232,128]{1,0:T(8,128)S(1)}, f32[232,128]{1,0:T(8,128)S(1)}, u32[]{:S(2)}, u32[]{:S(2)}) %collective-permute-start.2) | collective-permute-done | bytes 118816 | tf_op jit(solution)/shard_map/ppermute | solution.py:209
  13.0 1.7 %collective-permute-start.6 = (f32[232,128]{1,0:T(8,128)S(1)}, f32[232,128]{1,0:T(8,128)S(1)}, u32[]{:S(2)}, u32[]{:S(2)}) collective-permute-start(f32[232,128]{1,0:T(8,128)S(1)} %collective-permute-done.2), channel_id=1, source_target_pairs={{0,2},{1,3},{2,0},{3,1},{4,6},{5,7},{6,4},{7,5},{8,10},{9,11},{10,... | collective-permute-start | bytes 356360 | tf_op jit(solution)/shard_map/ppermute | solution.py:209
  14.7 4.1 %collective-permute-done.1 = f32[232,128]{1,0:T(8,128)S(1)} collective-permute-done((f32[232,128]{1,0:T(8,128)S(1)}, f32[232,128]{1,0:T(8,128)S(1)}, u32[]{:S(2)}, u32[]{:S(2)}) %collective-permute-start.1) | collective-permute-done | bytes 118816 | tf_op jit(solution)/shard_map/ppermute | solution.py:209
  18.8 1.5 %collective-permute-start.5 = (f32[232,128]{1,0:T(8,128)S(1)}, f32[232,128]{1,0:T(8,128)S(1)}, u32[]{:S(2)}, u32[]{:S(2)}) collective-permute-start(f32[232,128]{1,0:T(8,128)S(1)} %collective-permute-done.1), channel_id=1, source_target_pairs={{0,2},{1,3},{2,0},{3,1},{4,6},{5,7},{6,4},{7,5},{8,10},{9,11},{10,... | collective-permute-start | bytes 356360 | tf_op jit(solution)/shard_map/ppermute | solution.py:209
  20.3 0.0 collective-permute-done
  20.3 0.5 collective-permute-start.4
  20.9 0.0 collective-permute-done.3
  20.9 0.0 collective-permute-done.6
  20.9 3.5 %collective-permute-done.5 = f32[232,128]{1,0:T(8,128)S(1)} collective-permute-done((f32[232,128]{1,0:T(8,128)S(1)}, f32[232,128]{1,0:T(8,128)S(1)}, u32[]{:S(2)}, u32[]{:S(2)}) %collective-permute-start.5) | collective-permute-done | bytes 118816 | tf_op jit(solution)/shard_map/ppermute | solution.py:209
  24.4 1.3 %collective-permute-done.4 = f32[232,128]{1,0:T(8,128)S(1)} collective-permute-done((f32[232,128]{1,0:T(8,128)S(1)}, f32[232,128]{1,0:T(8,128)S(1)}, u32[]{:S(2)}, u32[]{:S(2)}) %collective-permute-start.4) | collective-permute-done | bytes 118816 | tf_op jit(solution)/shard_map/ppermute | solution.py:209
  25.6 0.0 copy-done
  25.7 0.0 copy-done.1
  25.7 0.1 concatenate.8.refs_0_
  25.7 0.1 collective-permute-start.7
  25.8 2.5 %collective-permute-done.7.refs_1_ = f32[1856,128]{1,0:T(8,128)S(1)} collective-permute-done((f32[1856,128]{1,0:T(8,128)S(1)}, f32[1856,128]{1,0:T(8,128)S(1)}, u32[]{:S(2)}, u32[]{:S(2)}) %collective-permute-start.7) | collective-permute-done | bytes 950304 | tf_op jit(solution)/shard_map/ppermute | solution.py:209
  28.3 40.2 %whole_group.1 = (f32[1,96]{1,0:T(1,128)}, f32[1,128]{1,0:T(1,128)}, f32[96,128]{1,0:T(8,128)}, f32[128,128]{1,0:T(8,128)}) custom-call(f32[1856,128]{1,0:T(8,128)S(1)} %concatenate.8.refs_0_, f32[1856,128]{1,0:T(8,128)S(1)} %collective-permute-done.7.refs_1_), custom_call_target="tpu_custom_call" | custom-call | tf_op jit(solution)/shard_map/whole_group/pallas_call | solution.py:237
  (1 shorter events, 0.0 us)
Async XLA Ops:
  1.3 0.7 copy-start.2
  1.9 23.7 %copy-start = (f32[128,128]{1,0:T(8,128)S(1)}, f32[128,128]{1,0:T(8,128)}, u32[]{:S(2)}) copy-start(f32[128,128]{1,0:T(8,128)} %param.5) | copy-start | bytes 196612
  1.9 23.7 %copy-start.1 = (f32[96,128]{1,0:T(8,128)S(1)}, f32[96,128]{1,0:T(8,128)}, u32[]{:S(2)}) copy-start(f32[96,128]{1,0:T(8,128)} %param.4) | copy-start | bytes 147460
  3.7 9.3 %collective-permute-start.2 = (f32[232,128]{1,0:T(8,128)S(1)}, f32[232,128]{1,0:T(8,128)S(1)}, u32[]{:S(2)}, u32[]{:S(2)}) collective-permute-start(f32[232,128]{1,0:T(8,128)S(1)} %concatenate.7), channel_id=1, source_target_pairs={{0,12},{1,13},{2,14},{3,15},{4,8},{5,9},{6,10},{7,11},{8,4},{9,5},... | collective-permute-start | bytes 356360 | tf_op jit(solution)/shard_map/ppermute | solution.py:209
  8.8 10.0 %collective-permute-start.1 = (f32[232,128]{1,0:T(8,128)S(1)}, f32[232,128]{1,0:T(8,128)S(1)}, u32[]{:S(2)}, u32[]{:S(2)}) collective-permute-start(f32[232,128]{1,0:T(8,128)S(1)} %concatenate.7), channel_id=1, source_target_pairs={{0,8},{1,9},{2,10},{3,11},{4,12},{5,13},{6,14},{7,15},{8,0},{9,1},... | collective-permute-start | bytes 356360 | tf_op jit(solution)/shard_map/ppermute | solution.py:209
  8.8 11.5 %collective-permute-start = (f32[232,128]{1,0:T(8,128)S(1)}, f32[232,128]{1,0:T(8,128)S(1)}, u32[]{:S(2)}, u32[]{:S(2)}) collective-permute-start(f32[232,128]{1,0:T(8,128)S(1)} %concatenate.7), channel_id=1, source_target_pairs={{0,4},{1,5},{2,6},{3,7},{4,0},{5,1},{6,2},{7,3},{8,12},{9,13},{10,... | collective-permute-start | bytes 356360 | tf_op jit(solution)/shard_map/ppermute | solution.py:209
  9.4 11.4 %collective-permute-start.3 = (f32[232,128]{1,0:T(8,128)S(1)}, f32[232,128]{1,0:T(8,128)S(1)}, u32[]{:S(2)}, u32[]{:S(2)}) collective-permute-start(f32[232,128]{1,0:T(8,128)S(1)} %concatenate.7), channel_id=1, source_target_pairs={{0,2},{1,3},{2,0},{3,1},{4,6},{5,7},{6,4},{7,5},{8,10},{9,11},{10,... | collective-permute-start | bytes 356360 | tf_op jit(solution)/shard_map/ppermute | solution.py:209
  13.0 7.9 %collective-permute-start.6 = (f32[232,128]{1,0:T(8,128)S(1)}, f32[232,128]{1,0:T(8,128)S(1)}, u32[]{:S(2)}, u32[]{:S(2)}) collective-permute-start(f32[232,128]{1,0:T(8,128)S(1)} %collective-permute-done.2), channel_id=1, source_target_pairs={{0,2},{1,3},{2,0},{3,1},{4,6},{5,7},{6,4},{7,5},{8,10},{9,11},{10,... | collective-permute-start | bytes 356360 | tf_op jit(solution)/shard_map/ppermute | solution.py:209
  18.8 5.6 %collective-permute-start.5 = (f32[232,128]{1,0:T(8,128)S(1)}, f32[232,128]{1,0:T(8,128)S(1)}, u32[]{:S(2)}, u32[]{:S(2)}) collective-permute-start(f32[232,128]{1,0:T(8,128)S(1)} %collective-permute-done.1), channel_id=1, source_target_pairs={{0,2},{1,3},{2,0},{3,1},{4,6},{5,7},{6,4},{7,5},{8,10},{9,11},{10,... | collective-permute-start | bytes 356360 | tf_op jit(solution)/shard_map/ppermute | solution.py:209
  20.3 5.3 %collective-permute-start.4 = (f32[232,128]{1,0:T(8,128)S(1)}, f32[232,128]{1,0:T(8,128)S(1)}, u32[]{:S(2)}, u32[]{:S(2)}) collective-permute-start(f32[232,128]{1,0:T(8,128)S(1)} %collective-permute-done), channel_id=1, source_target_pairs={{0,2},{1,3},{2,0},{3,1},{4,6},{5,7},{6,4},{7,5},{8,10},{9,11},{10,... | collective-permute-start | bytes 356360 | tf_op jit(solution)/shard_map/ppermute | solution.py:209
  25.7 2.6 %collective-permute-start.7 = (f32[1856,128]{1,0:T(8,128)S(1)}, f32[1856,128]{1,0:T(8,128)S(1)}, u32[]{:S(2)}, u32[]{:S(2)}) collective-permute-start(f32[1856,128]{1,0:T(8,128)S(1)} %concatenate.8.refs_0_), channel_id=1, source_target_pairs={{0,1},{1,0},{2,3},{3,2},{4,5},{5,4},{6,7},{7,6},{8,9},{9,8},{10,11... | collective-permute-start | bytes 2850824 | tf_op jit(solution)/shard_map/ppermute | solution.py:209

commit v3 on v2

--- a/solution.py
+++ b/solution.py
@@ -26,6 +26,11 @@
     return first, second, third
 
 
+def split2(a):
+    first = a.astype(jnp.bfloat16)
+    return first, (a - first.astype(jnp.float32)).astype(jnp.bfloat16)
+
+
 def nt_dot(a, b, precision=None):
     return lax.dot_general(
         a, b, (((1,), (1,)), ((), ())), precision=precision, preferred_element_type=jnp.float32
@@ -50,11 +55,11 @@
     las, lbs, norms = [], [], []
     ones = jnp.ones((8, 3 * feat), jnp.bfloat16)
     for d, (ref, at) in enumerate(blocks):
-        x1, x2, x3 = split3((ref[at : at + s_dev, :] - center) * (2.0 * k))
-        xs[d * s_dev : (d + 1) * s_dev, :] = jnp.concatenate([x1, x1, x2, x2, x1, x3], 1)
+        x1, x2 = split2((ref[at : at + s_dev, :] - center) * (2.0 * k))
+        xs[d * s_dev : (d + 1) * s_dev, :] = jnp.concatenate([x1, x1, x2, x2], 1)
         y = ref[at + s_dev : at + s_dev + t_dev, :] - center
-        y1, y2, y3 = split3(y)
-        ys[d * t_dev : (d + 1) * t_dev, :] = jnp.concatenate([y1, y2, y1, y2, y3, y1], 1)
+        y1, y2 = split2(y)
+        ys[d * t_dev : (d + 1) * t_dev, :] = jnp.concatenate([y1, y2, y1, y2], 1)
         norms.append(nt_dot(ones, jnp.concatenate(split3(y * y), 1))[0:1, :])
         lbs.append(ref[at + s_dev + t_dev : at + s_dev + t_dev + 1, :])
         las.append(ref[at + s_dev + t_dev + 1 : at + s_dev + t_dev + 2, :])
@@ -70,6 +75,12 @@
     parts = PARTS
     chunk, sub = targets // parts, blk // parts
 
+    def least(values):
+        return functools.reduce(jnp.minimum, values)
+
+    def most(values):
+        return functools.reduce(jnp.maximum, values)
+
     def column_part(e, u):
         return jnp.sum((e * u).reshape(e.shape[0] // 8, 8, targets), axis=0)
 
@@ -77,21 +88,19 @@
         cols = slice(part * chunk, (part + 1) * chunk)
         dst[:, cols] = nt_dot(xs[i * blk : (i + 1) * blk, :], ys[cols, :])
 
-    lows, highs = [], []
+    sums, ends = [], []
 
     def absorb(src, i, part):
         s = slice(i * blk + part * sub, i * blk + (part + 1) * sub)
         e = jnp.exp2(src[part * sub : (part + 1) * sub, :] + g1)
         e_ref[s, :] = e
         r = jnp.sum(e, axis=1, keepdims=True)
-        lows.append(jnp.min(r))
-        highs.append(jnp.max(r))
+        sums.append(r)
         acc[...] += column_part(e, la_col[s, :] / r)
 
     def column_end():
         total = jnp.sum(acc[...], axis=0, keepdims=True)
-        lows.append(jnp.min(total))
-        highs.append(jnp.max(total) * (WIDE / SAFE))
+        ends.append(total)
         return total
 
     acc[...] = jnp.zeros_like(acc)
@@ -112,16 +121,15 @@
             s = slice(i * blk, (i + 1) * blk)
             e = e_ref[s, :]
             r = jnp.sum(e * v, axis=1, keepdims=True)
-            lows.append(jnp.min(r))
-            highs.append(jnp.max(r))
+            sums.extend(r[p * sub : (p + 1) * sub, :] for p in range(parts))
             u = la_col[s, :] / r
             u_col[s, :] = u
             acc[...] += column_part(e, u)
         total = column_end()
     v = mass_b / total
-    safe = (functools.reduce(jnp.minimum, lows) > 1.0 / SAFE) & (
-        functools.reduce(jnp.maximum, highs) < WIDE
-    )
+    low = jnp.minimum(jnp.min(least(sums)), jnp.min(least(ends)))
+    high = jnp.maximum(jnp.max(most(sums)), jnp.max(most(ends)) * (WIDE / SAFE))
+    safe = (low > 1.0 / SAFE) & (high < WIDE)
 
     x_own = pieces[0][0:s_dev, :] - center
     sq_own = k * jnp.sum(x_own * x_own, axis=1, keepdims=True)
@@ -186,7 +194,7 @@
 
     plan_rows = rows_p[...]
     mass = jnp.sum(plan_rows, axis=1, keepdims=True)
-    p1, p2, _ = split3(plan_rows)
+    p1, p2 = split2(plan_rows)
     y1, y2 = ys[:, 0:feat], ys[:, feat : 2 * feat]
 
     def nn(a, b):
@@ -197,7 +205,7 @@
     def tn(a, b):
         return lax.dot_general(a, b, (((0,), (0,)), ((), ())), preferred_element_type=jnp.float32)
 
-    q1, q2, _ = split3(cols_p[...])
+    q1, q2 = split2(cols_p[...])
     x1, x2 = xs[:, 0:feat], xs[:, 2 * feat : 3 * feat]
     tm_ref[...] = (tn(q1, x1) + (tn(q1, x2) + tn(q2, x1))) * (1.0 / (2.0 * k)) + center
 
@@ -208,27 +216,57 @@
     def swap(a, bits):
         return lax.ppermute(a, axis, [(i, i ^ bits) for i in range(n)])
 
-    far = [swap(block, bits) for bits in range(4, n, 4)]
-    line = [block] + far
-    side = [swap(a, 2) for a in line]
-    mine = jnp.concatenate(line + side, axis=0)
-    return [mine, swap(mine, 1)]
+    step = [swap(block, 4)]
+    for bits in range(8, n, 8):
+        jump = swap(block, bits)
+        step += [jump, swap(jump, 4)]
+    line = jnp.concatenate([block] + step, axis=0)
+    side = jnp.concatenate([swap(a, 2) for a in [block] + step], axis=0)
+    return [line, swap(line, 1), side, swap(side, 1)]
+
+
+def pack_kernel(x_ref, y_ref, la_ref, lb_ref, out_ref, la_row, lb_row, sems):
+    s_dev, t_dev = x_ref.shape[0], y_ref.shape[0]
+    rows = s_dev + t_dev
+    copies = [
+        pltpu.make_async_copy(src, dst, sems.at[i])
+        for i, (src, dst) in enumerate(
+            (
+                (x_ref, out_ref.at[0:s_dev, :]),
+                (y_ref, out_ref.at[s_dev:rows, :]),
+                (la_ref, la_row),
+                (lb_ref, lb_row),
+            )
+        )
+    ]
+    for copy in copies:
+        copy.start()
+    out_ref[rows:, :] = jnp.zeros((8, x_ref.shape[1]), jnp.float32)
+    copies[2].wait()
+    out_ref[rows + 1 : rows + 2, 0:s_dev] = la_row[...].reshape(1, s_dev)
+    copies[3].wait()
+    out_ref[rows : rows + 1, :] = lb_row[...].reshape(1, t_dev)
+    copies[0].wait()
+    copies[1].wait()
 
 
 def per_device_whole(source_feats, target_feats, log_a, log_b):
     n = lax.axis_size("src")
     s_dev, feat = source_feats.shape
     t_dev = target_feats.shape[0]
-    block = jnp.concatenate(
-        [
-            source_feats,
-            target_feats,
-            log_b[None, :],
-            jnp.pad(log_a, (0, feat - s_dev))[None, :],
-            jnp.zeros((6, feat), jnp.float32),
+    block = pl.pallas_call(
+        pack_kernel,
+        out_shape=jax.ShapeDtypeStruct((s_dev + t_dev + 8, feat), jnp.float32),
+        in_specs=[pl.BlockSpec(memory_space=pltpu.HBM)] * 4,
+        out_specs=pl.BlockSpec(memory_space=pltpu.VMEM),
+        scratch_shapes=[
+            pltpu.VMEM((s_dev,), jnp.float32),
+            pltpu.VMEM((t_dev,), jnp.float32),
+            pltpu.SemaphoreType.DMA((4,)),
         ],
-        axis=0,
-    )
+        compiler_params=pltpu.CompilerParams(vmem_limit_bytes=60 * 2**20),
+        name="pack",
+    )(source_feats, target_feats, log_a, log_b)
     pieces = exchange(block, "src")
     sources, targets = n * s_dev, n * t_dev
     blk = 256
@@ -246,8 +284,8 @@
         out_specs=[vmem] * 4,
         scratch_shapes=[
             pltpu.VMEM((sources, targets), f32),
-            pltpu.VMEM((sources, 6 * feat), b16),
-            pltpu.VMEM((targets, 6 * feat), b16),
+            pltpu.VMEM((sources, 4 * feat), b16),
+            pltpu.VMEM((targets, 4 * feat), b16),
             pltpu.VMEM((sources, 1), f32),
             pltpu.VMEM((sources, 1), f32),
             pltpu.VMEM((s_dev, targets), f32),

time: 68.8 us -> 61.7 us (0.90)
  local copies, waits for them, and re-layouts: 3.13 us -> 0.04 us
  waiting for transfers between devices: 13.3 us -> 11 us
  Pallas kernels: 40.2 us -> 38.1 us
    pallas_call x1, Pallas kernels: 40.2 us -> 36.6 us  [per_device_whole(): pl.pallas_call(functools.partial(whole_group_kernel, n, s_dev, t_dev, blk...]
    ppermute x8 -> x9, waiting for transfers between devices: 13.3 us -> 11 us  [swap(): return lax.ppermute(a, axis, [(i, i ^ bits) for i in range(n)])]
    concatenate x2 -> x1, local copies, waits for them, and re-layouts: 1.81 us -> 0.01 us  [exchange(): side = jnp.concatenate([swap(a, 2) for a in [block] + step], axis=0)]
    pallas_call x0 -> x1, Pallas kernels: none -> 1.55 us  [per_device_whole(): pl.pallas_call(pack_kernel, out_shape=jax.ShapeDtypeStruct((s_dev + t_dev...]
    ppermute x8 -> x9, starting transfers between devices: 11.3 us -> 11.7 us  [swap(): return lax.ppermute(a, axis, [(i, i ^ bits) for i in range(n)])]
  transfers between devices with their start and end apart: 8 -> 9, of which waited for: 5 -> 5; matrix products, arithmetic and copies ran while one was open for 0% -> 0% of each run, Pallas kernels for 0% -> 0%
where the time goes in v3:
time: 61.7 us; the launch traced here: 61.6 us
  Pallas kernels  38.1 us (62%)
  starting transfers between devices  11.7 us (19%)
  waiting for transfers between devices  11 us (18%)
  between operations  0.71 us (1%)
    pallas_call x1, Pallas kernels, per_device_whole(): pl.pallas_call(functools.partial(whole_group_kernel, n, s_dev, t_dev, blk...  36.6 us
    ppermute x9, starting transfers between devices, swap(): return lax.ppermute(a, axis, [(i, i ^ bits) for i in range(n)])  11.7 us
    ppermute x9, waiting for transfers between devices, swap(): return lax.ppermute(a, axis, [(i, i ^ bits) for i in range(n)])  11 us
    pallas_call x1, Pallas kernels, per_device_whole(): pl.pallas_call(pack_kernel, out_shape=jax.ShapeDtypeStruct((s_dev + t_dev...  1.55 us
  transfers between devices with their start and end apart: 9, of which 5 were waited for; matrix products, arithmetic and copies ran while one was open for 0% of the time, Pallas kernels for 0%

profile of v3, /device:TPU:0, one launch (start us, length us, event | category | flops | bytes accessed | tf_op | source)
XLA Modules:
  0.0 61.6 jit_solution(13329376798317288396)
XLA Ops:
  0.6 1.5 %pack.1 = f32[232,128]{1,0:T(8,128)} custom-call(f32[96,128]{1,0:T(8,128)} %x_ref.1, f32[128,128]{1,0:T(8,128)} %y_ref.1, f32[96]{0:T(128)} %la_ref.1, f32[128]{0:T(128)} %lb_ref.1), custom_call_target="tpu_custom_call" | custom-call | tf_op jit(solution)/shard_map/pack/pallas_call | solution.py:257
  2.2 0.0 copy-start
  2.2 4.1 %collective-permute-start.1 = (f32[232,128]{1,0:T(8,128)}, f32[232,128]{1,0:T(8,128)S(1)}, u32[]{:S(2)}, u32[]{:S(2)}) collective-permute-start(f32[232,128]{1,0:T(8,128)} %pack.1), channel_id=1, source_target_pairs={{0,8},{1,9},{2,10},{3,11},{4,12},{5,13},{6,14},{7,15},{8,0},{9,1},... | collective-permute-start | bytes 356360 | tf_op jit(solution)/shard_map/ppermute | solution.py:217
  6.3 1.6 %collective-permute-start = (f32[232,128]{1,0:T(8,128)}, f32[232,128]{1,0:T(8,128)S(1)}, u32[]{:S(2)}, u32[]{:S(2)}) collective-permute-start(f32[232,128]{1,0:T(8,128)} %pack.1), channel_id=1, source_target_pairs={{0,4},{1,5},{2,6},{3,7},{4,0},{5,1},{6,2},{7,3},{8,12},{9,13},{10,... | collective-permute-start | bytes 356360 | tf_op jit(solution)/shard_map/ppermute | solution.py:217
  7.9 1.5 %collective-permute-start.4 = (f32[232,128]{1,0:T(8,128)}, f32[232,128]{1,0:T(8,128)S(1)}, u32[]{:S(2)}, u32[]{:S(2)}) collective-permute-start(f32[232,128]{1,0:T(8,128)} %pack.1), channel_id=1, source_target_pairs={{0,2},{1,3},{2,0},{3,1},{4,6},{5,7},{6,4},{7,5},{8,10},{9,11},{10,... | collective-permute-start | bytes 356360 | tf_op jit(solution)/shard_map/ppermute | solution.py:217
  9.4 3.0 %collective-permute-done.1 = f32[232,128]{1,0:T(8,128)S(1)} collective-permute-done((f32[232,128]{1,0:T(8,128)}, f32[232,128]{1,0:T(8,128)S(1)}, u32[]{:S(2)}, u32[]{:S(2)}) %collective-permute-start.1) | collective-permute-done | bytes 118816 | tf_op jit(solution)/shard_map/ppermute | solution.py:217
  12.4 0.7 %collective-permute-start.2 = (f32[232,128]{1,0:T(8,128)S(1)}, f32[232,128]{1,0:T(8,128)S(1)}, u32[]{:S(2)}, u32[]{:S(2)}) collective-permute-start(f32[232,128]{1,0:T(8,128)S(1)} %collective-permute-done.1), channel_id=1, source_target_pairs={{0,4},{1,5},{2,6},{3,7},{4,0},{5,1},{6,2},{7,3},{8,12},{9,13},{10,... | collective-permute-start | bytes 356360 | tf_op jit(solution)/shard_map/ppermute | solution.py:217
  13.1 1.5 %collective-permute-start.6 = (f32[232,128]{1,0:T(8,128)S(1)}, f32[232,128]{1,0:T(8,128)S(1)}, u32[]{:S(2)}, u32[]{:S(2)}) collective-permute-start(f32[232,128]{1,0:T(8,128)S(1)} %collective-permute-done.1), channel_id=1, source_target_pairs={{0,2},{1,3},{2,0},{3,1},{4,6},{5,7},{6,4},{7,5},{8,10},{9,11},{10,... | collective-permute-start | bytes 356360 | tf_op jit(solution)/shard_map/ppermute | solution.py:217
  14.6 0.0 collective-permute-done
  14.6 0.5 collective-permute-start.5
  15.1 0.0 collective-permute-done.4
  15.2 2.1 %collective-permute-done.2 = f32[232,128]{1,0:T(8,128)S(1)} collective-permute-done((f32[232,128]{1,0:T(8,128)S(1)}, f32[232,128]{1,0:T(8,128)S(1)}, u32[]{:S(2)}, u32[]{:S(2)}) %collective-permute-start.2) | collective-permute-done | bytes 118816 | tf_op jit(solution)/shard_map/ppermute | solution.py:217
  17.2 0.0 copy-done
  17.3 0.1 collective-permute-start.3
  17.3 1.6 %collective-permute-start.7 = (f32[232,128]{1,0:T(8,128)S(1)}, f32[232,128]{1,0:T(8,128)S(1)}, u32[]{:S(2)}, u32[]{:S(2)}) collective-permute-start(f32[232,128]{1,0:T(8,128)S(1)} %collective-permute-done.2), channel_id=1, source_target_pairs={{0,2},{1,3},{2,0},{3,1},{4,6},{5,7},{6,4},{7,5},{8,10},{9,11},{10,... | collective-permute-start | bytes 356360 | tf_op jit(solution)/shard_map/ppermute | solution.py:217
  19.0 1.6 %collective-permute-done.5 = f32[232,128]{1,0:T(8,128)S(1)} collective-permute-done((f32[232,128]{1,0:T(8,128)S(1)}, f32[232,128]{1,0:T(8,128)S(1)}, u32[]{:S(2)}, u32[]{:S(2)}) %collective-permute-start.5) | collective-permute-done | bytes 118816 | tf_op jit(solution)/shard_map/ppermute | solution.py:217
  20.6 0.0 collective-permute-done.6
  20.6 2.5 %collective-permute-done.7 = f32[232,128]{1,0:T(8,128)S(1)} collective-permute-done((f32[232,128]{1,0:T(8,128)S(1)}, f32[232,128]{1,0:T(8,128)S(1)}, u32[]{:S(2)}, u32[]{:S(2)}) %collective-permute-start.7) | collective-permute-done | bytes 118816 | tf_op jit(solution)/shard_map/ppermute | solution.py:217
  23.1 0.1 collective-permute-start.8
  23.2 0.0 collective-permute-done.3.refs_1_
  23.2 1.8 %collective-permute-done.8.refs_3_ = f32[928,128]{1,0:T(8,128)S(1)} collective-permute-done((f32[928,128]{1,0:T(8,128)S(1)}, f32[928,128]{1,0:T(8,128)S(1)}, u32[]{:S(2)}, u32[]{:S(2)}) %collective-permute-start.8) | collective-permute-done | bytes 475168 | tf_op jit(solution)/shard_map/ppermute | solution.py:217
  25.0 36.6 %whole_group.1 = (f32[1,96]{1,0:T(1,128)}, f32[1,128]{1,0:T(1,128)}, f32[96,128]{1,0:T(8,128)}, f32[128,128]{1,0:T(8,128)}) custom-call(f32[928,128]{1,0:T(8,128)S(1)} %pad_maximum_fusion.refs_0_, f32[928,128]{1,0:T(8,128)S(1)} %collective-permute-done.3.refs_1_, f32[928,128]{1,0:T(8,128)S(1)} %constant_dynamic-update-slice_fusion.refs_2_, ...), custom_call_target="tpu_custom_call" | custom-call | tf_op jit(solution)/shard_map/whole_group/pallas_call | solution.py:275
  (5 shorter events, 0.1 us)
Async XLA Ops:
  2.2 15.0 %copy-start = (f32[232,128]{1,0:T(8,128)S(1)}, f32[232,128]{1,0:T(8,128)}, u32[]{:S(2)}) copy-start(f32[232,128]{1,0:T(8,128)} %pack.1) | copy-start | bytes 356356
  2.2 10.2 %collective-permute-start.1 = (f32[232,128]{1,0:T(8,128)}, f32[232,128]{1,0:T(8,128)S(1)}, u32[]{:S(2)}, u32[]{:S(2)}) collective-permute-start(f32[232,128]{1,0:T(8,128)} %pack.1), channel_id=1, source_target_pairs={{0,8},{1,9},{2,10},{3,11},{4,12},{5,13},{6,14},{7,15},{8,0},{9,1},... | collective-permute-start | bytes 356360 | tf_op jit(solution)/shard_map/ppermute | solution.py:217
  6.3 8.3 %collective-permute-start = (f32[232,128]{1,0:T(8,128)}, f32[232,128]{1,0:T(8,128)S(1)}, u32[]{:S(2)}, u32[]{:S(2)}) collective-permute-start(f32[232,128]{1,0:T(8,128)} %pack.1), channel_id=1, source_target_pairs={{0,4},{1,5},{2,6},{3,7},{4,0},{5,1},{6,2},{7,3},{8,12},{9,13},{10,... | collective-permute-start | bytes 356360 | tf_op jit(solution)/shard_map/ppermute | solution.py:217
  7.9 7.3 %collective-permute-start.4 = (f32[232,128]{1,0:T(8,128)}, f32[232,128]{1,0:T(8,128)S(1)}, u32[]{:S(2)}, u32[]{:S(2)}) collective-permute-start(f32[232,128]{1,0:T(8,128)} %pack.1), channel_id=1, source_target_pairs={{0,2},{1,3},{2,0},{3,1},{4,6},{5,7},{6,4},{7,5},{8,10},{9,11},{10,... | collective-permute-start | bytes 356360 | tf_op jit(solution)/shard_map/ppermute | solution.py:217
  12.4 4.8 %collective-permute-start.2 = (f32[232,128]{1,0:T(8,128)S(1)}, f32[232,128]{1,0:T(8,128)S(1)}, u32[]{:S(2)}, u32[]{:S(2)}) collective-permute-start(f32[232,128]{1,0:T(8,128)S(1)} %collective-permute-done.1), channel_id=1, source_target_pairs={{0,4},{1,5},{2,6},{3,7},{4,0},{5,1},{6,2},{7,3},{8,12},{9,13},{10,... | collective-permute-start | bytes 356360 | tf_op jit(solution)/shard_map/ppermute | solution.py:217
  13.1 7.5 %collective-permute-start.6 = (f32[232,128]{1,0:T(8,128)S(1)}, f32[232,128]{1,0:T(8,128)S(1)}, u32[]{:S(2)}, u32[]{:S(2)}) collective-permute-start(f32[232,128]{1,0:T(8,128)S(1)} %collective-permute-done.1), channel_id=1, source_target_pairs={{0,2},{1,3},{2,0},{3,1},{4,6},{5,7},{6,4},{7,5},{8,10},{9,11},{10,... | collective-permute-start | bytes 356360 | tf_op jit(solution)/shard_map/ppermute | solution.py:217
  14.6 5.9 %collective-permute-start.5 = (f32[232,128]{1,0:T(8,128)S(1)}, f32[232,128]{1,0:T(8,128)S(1)}, u32[]{:S(2)}, u32[]{:S(2)}) collective-permute-start(f32[232,128]{1,0:T(8,128)S(1)} %collective-permute-done), channel_id=1, source_target_pairs={{0,2},{1,3},{2,0},{3,1},{4,6},{5,7},{6,4},{7,5},{8,10},{9,11},{10,... | collective-permute-start | bytes 356360 | tf_op jit(solution)/shard_map/ppermute | solution.py:217
  17.3 5.9 %collective-permute-start.3 = (f32[928,128]{1,0:T(8,128)S(1)}, f32[928,128]{1,0:T(8,128)S(1)}, u32[]{:S(2)}, u32[]{:S(2)}) collective-permute-start(f32[928,128]{1,0:T(8,128)S(1)} %pad_maximum_fusion.refs_0_), channel_id=1, source_target_pairs={{0,1},{1,0},{2,3},{3,2},{4,5},{5,4},{6,7},{7,6},{8,9},{9,8},{10,11... | collective-permute-start | bytes 1425416 | tf_op jit(solution)/shard_map/ppermute | solution.py:217
  17.3 5.7 %collective-permute-start.7 = (f32[232,128]{1,0:T(8,128)S(1)}, f32[232,128]{1,0:T(8,128)S(1)}, u32[]{:S(2)}, u32[]{:S(2)}) collective-permute-start(f32[232,128]{1,0:T(8,128)S(1)} %collective-permute-done.2), channel_id=1, source_target_pairs={{0,2},{1,3},{2,0},{3,1},{4,6},{5,7},{6,4},{7,5},{8,10},{9,11},{10,... | collective-permute-start | bytes 356360 | tf_op jit(solution)/shard_map/ppermute | solution.py:217
  23.1 1.9 %collective-permute-start.8 = (f32[928,128]{1,0:T(8,128)S(1)}, f32[928,128]{1,0:T(8,128)S(1)}, u32[]{:S(2)}, u32[]{:S(2)}) collective-permute-start(f32[928,128]{1,0:T(8,128)S(1)} %constant_dynamic-update-slice_fusion.refs_2_), channel_id=1, source_target_pairs={{0,1},{1,0},{2,3},{3,2},{4,5},{5,4},{6,7},{7,6},{8,9},{9,8},{10,11... | collective-permute-start | bytes 1425416 | tf_op jit(solution)/shard_map/ppermute | solution.py:217

commit v4 on v0

--- a/solution.py
+++ b/solution.py
@@ -1,12 +1,404 @@
+import functools
+
 import jax
 import jax.numpy as jnp
 from jax import lax
+from jax.experimental import pallas as pl
+from jax.experimental.pallas import tpu as pltpu
 from jax.sharding import PartitionSpec as P
 
 ITERS = 3
-
-
 EPS = 0.05
+LN2 = 0.6931471805599453
+LOG2E = 1.4426950408889634
+SAFE = 2.0**30
+WIDE = 2.0**60
+PARTS = 8
+CHUNK = 256
+NEAR_VMEM = 16 * 2**20
+WHOLE_VMEM = 36 * 2**20
+REPLICATED_BYTES = 24 * 2**20
+HI = lax.Precision.HIGHEST
+
+
+def split3(a):
+    first = a.astype(jnp.bfloat16)
+    rest = a - first.astype(jnp.float32)
+    second = rest.astype(jnp.bfloat16)
+    third = (rest - second.astype(jnp.float32)).astype(jnp.bfloat16)
+    return first, second, third
+
+
+def split2(a):
+    first = a.astype(jnp.bfloat16)
+    return first, (a - first.astype(jnp.float32)).astype(jnp.bfloat16)
+
+
+def nt_dot(a, b, precision=None):
+    return lax.dot_general(
+        a, b, (((1,), (1,)), ((), ())), precision=precision, preferred_element_type=jnp.float32
+    )
+
+
+def least(values):
+    return functools.reduce(jnp.minimum, values)
+
+
+def most(values):
+    return functools.reduce(jnp.maximum, values)
+
+
+def blocks_of(pieces, rows):
+    return [(ref, at) for ref in pieces for at in range(0, ref.shape[0], rows)]
+
+
+def target_sum(blocks, s_dev, t_dev):
+    total = sum(
+        jnp.sum(ref[at + s_dev : at + s_dev + t_dev, :].reshape(t_dev // 8, 8, -1), axis=0)
+        for ref, at in blocks
+    )
+    return jnp.sum(total, axis=0, keepdims=True)
+
+
+def split_features(blocks, s_dev, t_dev, center, k, xs, ys):
+    feat = center.shape[1]
+    norms = []
+    ones = jnp.ones((8, 3 * feat), jnp.bfloat16)
+    for d, (ref, at) in enumerate(blocks):
+        x1, x2 = split2((ref[at : at + s_dev, :] - center) * (2.0 * k))
+        xs[d * s_dev : (d + 1) * s_dev, :] = jnp.concatenate([x1, x1, x2, x2], 1)
+        y = ref[at + s_dev : at + s_dev + t_dev, :] - center
+        y1, y2 = split2(y)
+        ys[d * t_dev : (d + 1) * t_dev, :] = jnp.concatenate([y1, y2, y1, y2], 1)
+        norms.append(nt_dot(ones, jnp.concatenate(split3(y * y), 1))[0:1, :])
+    return jnp.concatenate(norms, 1) * k
+
+
+def near_kernel(s_dev, t_dev, blk, *refs):
+    pieces = refs[:-8]
+    e_ref, xs, ys, r_ref, norm_ref, mid_ref, mb0, mb1 = refs[-8:]
+    feat = pieces[0].shape[1]
+    k = LOG2E / (feat * EPS)
+    blocks = blocks_of(pieces, s_dev + t_dev + 8)
+    sources, targets = len(blocks) * s_dev, len(blocks) * t_dev
+    center = target_sum(blocks, s_dev, t_dev) * (1.0 / targets)
+    norm = split_features(blocks, s_dev, t_dev, center, k, xs, ys)
+    norm_ref[...] = norm
+    shift = jnp.mean(norm, axis=1, keepdims=True)
+    mid_ref[0:1, :] = center
+    mid_ref[1:2, :] = jnp.broadcast_to(shift, (1, feat))
+    mid_ref[2:8, :] = jnp.zeros((6, feat), jnp.float32)
+    g1 = shift - norm
+    bufs = (mb0, mb1)
+    steps = sources // blk
+    bufs[0][...] = nt_dot(xs[0:blk, :], ys[...])
+    for i in range(steps):
+        if i + 1 < steps:
+            bufs[(i + 1) % 2][...] = nt_dot(xs[(i + 1) * blk : (i + 2) * blk, :], ys[...])
+        s = slice(i * blk, (i + 1) * blk)
+        e = jnp.exp2(bufs[i % 2][...] + g1)
+        e_ref[s, :] = e
+        r_ref[s, :] = jnp.sum(e, axis=1, keepdims=True)
+
+
+def whole_group_kernel(n, s_dev, t_dev, blk, *refs):
+    pieces = refs[:-22]
+    e11, xs1, ys1, r1_ref, norm_ref, mid_ref = refs[-22:-16]
+    f_ref, g_ref, sm_ref, tm_ref = refs[-16:-12]
+    e12, e21, e22, e_own, xs2, ys2, la_col, u_col, acc0, acc1, mb0, mb1 = refs[-12:]
+    feat = pieces[0].shape[1]
+    rows = s_dev + t_dev + 8
+    k = LOG2E / (feat * EPS)
+    sources, targets = n * s_dev, n * t_dev
+    half_s, half_t = sources // 2, targets // 2
+    xs, ys, accs = (xs1, xs2), (ys1, ys2), (acc0, acc1)
+
+    blocks = blocks_of(pieces, rows)
+    center = mid_ref[0:1, :]
+    shift = mid_ref[1:2, 0:1]
+    norms = (norm_ref[...], split_features(blocks[n // 2 :], s_dev, t_dev, center, k, xs2, ys2))
+    lbs = [ref[at + s_dev + t_dev : at + s_dev + t_dev + 1, :] for ref, at in blocks]
+    las = [ref[at + s_dev + t_dev + 1 : at + s_dev + t_dev + 2, :] for ref, at in blocks]
+    g1 = tuple(shift - norm for norm in norms)
+    mass_b = tuple(jnp.exp(jnp.concatenate(part, 1)) for part in (lbs[: n // 2], lbs[n // 2 :]))
+    la_t = jnp.exp(jnp.concatenate(las, 0)).T
+    for d in range(n):
+        la_col[d * s_dev : (d + 1) * s_dev, :] = la_t[:s_dev, d : d + 1]
+
+    steps = sources // blk
+    near = steps // 2
+    parts = PARTS
+    sub = blk // parts
+
+    def halves(i, first=e11):
+        at = (i % near) * blk
+        return ((first, e12) if i < near else (e21, e22)), slice(at, at + blk)
+
+    def column_part(e, u):
+        return jnp.sum((e * u).reshape(e.shape[0] // 8, 8, half_t), axis=0)
+
+    def product(dst, i, part):
+        at = (i % near) * blk
+        factor = xs[i // near][at : at + blk, :]
+        chunks = [
+            (h, slice(c, c + CHUNK))
+            for h in ((1,) if i < near else (0, 1))
+            for c in range(0, half_t, CHUNK)
+        ]
+        for h, cols in chunks[part * len(chunks) // parts : (part + 1) * len(chunks) // parts]:
+            dst[:, h * half_t + cols.start : h * half_t + cols.stop] = nt_dot(factor, ys[h][cols, :])
+
+    sums, ends = [], []
+
+    def absorb(src, i, part):
+        kept, where = halves(i)
+        local = slice(part * sub, (part + 1) * sub)
+        s = slice(where.start + local.start, where.start + local.stop)
+        e1 = jnp.exp2(src[local, half_t:] + g1[1])
+        kept[1][s, :] = e1
+        if i < near:
+            e0 = kept[0][s, :]
+            r = r1_ref[s, :] + jnp.sum(e1, axis=1, keepdims=True)
+        else:
+            e0 = jnp.exp2(src[local, :half_t] + g1[0])
+            kept[0][s, :] = e0
+            r = jnp.sum(e0 + e1, axis=1, keepdims=True)
+        sums.append(r)
+        u = la_col[i * blk + local.start : i * blk + local.stop, :] / r
+        acc0[...] += column_part(e0, u)
+        acc1[...] += column_part(e1, u)
+
+    def column_end():
+        total = tuple(jnp.sum(acc[...], axis=0, keepdims=True) for acc in accs)
+        ends.extend(total)
+        return total
+
+    def clear():
+        for acc in accs:
+            acc[...] = jnp.zeros_like(acc)
+
+    clear()
+    bufs = (mb0, mb1)
+    for part in range(parts):
+        product(bufs[0], 0, part)
+    for i in range(steps):
+        for part in range(parts):
+            if i + 1 < steps:
+                product(bufs[(i + 1) % 2], i + 1, part)
+            absorb(bufs[i % 2], i, part)
+    total = column_end()
+
+    def quarters_sum(wide, count):
+        low = wide[:count, feat:] + (wide[count:, :feat] + wide[count:, feat:])
+        return wide[:count, :feat] + low
+
+    def target_sums(plan, i):
+        at = (i % near) * blk
+        return lax.dot_general(
+            jnp.concatenate(split2(plan), 1),
+            xs[i // near][at : at + blk, feat : 3 * feat],
+            (((0,), (0,)), ((), ())),
+            preferred_element_type=jnp.float32,
+        )
+
+    def put_targets(sums_of, mass):
+        moved = quarters_sum(sum(sums_of), t_dev)
+        mass = jnp.broadcast_to(mass * (2.0 * k), (feat, t_dev)).T
+        tm_ref[...] = moved / mass + center
+
+    def put_sources(plan):
+        mass = jnp.sum(plan[0] + plan[1], axis=1, keepdims=True)
+        wide = sum(
+            jnp.dot(
+                jnp.concatenate(split2(plan[h]), 0),
+                ys[h][:, 0 : 2 * feat],
+                preferred_element_type=jnp.float32,
+            )
+            for h in (0, 1)
+        )
+        sm_ref[...] = quarters_sum(wide, s_dev) / mass + center
+
+    x_own = pieces[0][0:s_dev, :] - center
+    sq_own = k * jnp.sum(x_own * x_own, axis=1, keepdims=True)
+
+    for step in range(1, ITERS):
+        v = tuple(m / t for m, t in zip(mass_b, total))
+        clear()
+        moved_parts = []
+        for i in range(steps):
+            kept, s = halves(i)
+            e0, e1 = kept[0][s, :], kept[1][s, :]
+            r = jnp.sum(e0 * v[0] + e1 * v[1], axis=1, keepdims=True)
+            sums.extend(r[p * sub : (p + 1) * sub, :] for p in range(parts))
+            u = la_col[i * blk : (i + 1) * blk, :] / r
+            acc0[...] += column_part(e0, u)
+            acc1[...] += column_part(e1, u)
+            if step == ITERS - 1:
+                moved_parts.append(target_sums(e0[:, 0:t_dev] * u, i))
+                if i == 0:
+                    u_own = u[0:s_dev, :]
+        total = column_end()
+    v = tuple(m / t for m, t in zip(mass_b, total))
+
+    def put_f(f):
+        wide = jnp.broadcast_to(f, (s_dev, feat))
+        wide = jnp.concatenate([wide, jnp.zeros((feat - s_dev, feat), jnp.float32)], 0)
+        f_ref[...] = wide.T[0:1, 0:s_dev]
+
+    put_f(EPS * jnp.log(u_own) + (EPS * LN2) * (sq_own + shift))
+    g_ref[...] = EPS * jnp.log(v[0][:, 0:t_dev])
+    put_targets(moved_parts, total[0][:, 0:t_dev])
+    put_sources((e11[0:s_dev, :] * v[0], e12[0:s_dev, :] * v[1]))
+
+    low_r, high_r, low_c, high_c = least(sums), most(sums), least(ends), most(ends)
+    bad = jnp.max(jnp.where((low_r < 1.0 / SAFE) | (high_r > WIDE), 1.0, 0.0)) + jnp.max(
+        jnp.where((low_c < 1.0 / SAFE) | (high_c > SAFE), 1.0, 0.0)
+    )
+    finite = (jnp.max(high_r) < WIDE) & (jnp.max(high_c) < SAFE)
+
+    @pl.when(jnp.logical_not((bad == 0.0) & finite))
+    def _():
+        quarters = ((e_own, e12), (e21, e22))
+
+        def at_block(i):
+            return pl.ds(pl.multiple_of(i * blk, blk), blk)
+
+        for a in (0, 1):
+            for h in (0, 1):
+
+                def inner(i, carry):
+                    s = at_block(i)
+                    quarters[a][h][s, :] = nt_dot(xs[a][s, :], ys[h][...])
+                    return carry
+
+                lax.fori_loop(0, near, inner, 0)
+
+        def potentials(step, g):
+            for a in (0, 1):
+
+                def row(i, carry):
+                    s, line = at_block(i), at_block(i + a * near)
+                    t = [quarters[a][h][s, :] + g[h] for h in (0, 1)]
+                    top = jnp.max(jnp.maximum(t[0], t[1]), axis=1, keepdims=True)
+                    mass = jnp.sum(jnp.exp2(t[0] - top) + jnp.exp2(t[1] - top), axis=1, keepdims=True)
+                    u_col[line, :] = jnp.log2(la_col[line, :]) - top - jnp.log2(mass)
+                    return carry
+
+                lax.fori_loop(0, near, row, 0)
+
+            new = []
+            for h in (0, 1):
+                top = jnp.full((1, half_t), -jnp.inf, jnp.float32)
+                mass = jnp.zeros((1, half_t), jnp.float32)
+                for a in (0, 1):
+
+                    def column_top(i, top):
+                        t = quarters[a][h][at_block(i), :] + u_col[at_block(i + a * near), :]
+                        return jnp.maximum(top, jnp.max(t, axis=0, keepdims=True))
+
+                    top = lax.fori_loop(0, near, column_top, top)
+                for a in (0, 1):
+
+                    def column_mass(i, mass):
+                        t = quarters[a][h][at_block(i), :] + u_col[at_block(i + a * near), :]
+                        return mass + jnp.sum(jnp.exp2(t - top), axis=0, keepdims=True)
+
+                    mass = lax.fori_loop(0, near, column_mass, mass)
+                new.append(jnp.log2(mass_b[h]) - top - jnp.log2(mass))
+            return tuple(new)
+
+        g = lax.fori_loop(0, ITERS, potentials, (-norms[0], -norms[1]))
+        u_first = u_col[0:s_dev, :]
+        put_f((EPS * LN2) * (u_first + sq_own))
+        g_ref[...] = (EPS * LN2) * (g[0][:, 0:t_dev] + norms[0][:, 0:t_dev])
+        put_sources([jnp.exp2(quarters[0][h][0:s_dev, :] + u_first + g[h]) for h in (0, 1)])
+
+        def own_columns(i):
+            at = (i % near) * blk
+            inner = quarters[i // near][0][at : at + blk, 0:t_dev]
+            return jnp.exp2(inner + u_col[i * blk : (i + 1) * blk, :] + g[0][:, 0:t_dev])
+
+        mass = mass_b[0][:, 0:t_dev]
+        put_targets([target_sums(own_columns(i), i) for i in range(steps)], mass)
+
+
+def exchange(block, axis):
+    n = lax.axis_size(axis)
+
+    def swap(a, bits):
+        return lax.ppermute(a, axis, [(i, i ^ bits) for i in range(n)])
+
+    step = [swap(block, 4)]
+    for bits in range(8, n, 8):
+        jump = swap(block, bits)
+        step += [jump, swap(jump, 4)]
+    line = [block] + step
+    side = [swap(a, 2) for a in line]
+    return line + [swap(a, 1) for a in line], side + [swap(a, 1) for a in side]
+
+
+def per_device_whole(source_feats, target_feats, log_a, log_b):
+    n = lax.axis_size("src")
+    s_dev, feat = source_feats.shape
+    t_dev = target_feats.shape[0]
+    masses = jnp.concatenate([log_b, log_a, jnp.zeros((8 * feat - t_dev - s_dev,), jnp.float32)])
+    block = jnp.concatenate([source_feats, target_feats, masses.reshape(8, feat)], axis=0)
+    block = lax.optimization_barrier(block)
+    near_pieces, far_pieces = exchange(block, "src")
+    sources, targets = n * s_dev, n * t_dev
+    half_s, half_t = sources // 2, targets // 2
+    blk = 256
+    f32, b16 = jnp.float32, jnp.bfloat16
+    vmem = pl.BlockSpec(memory_space=pltpu.VMEM)
+    near = pl.pallas_call(
+        functools.partial(near_kernel, s_dev, t_dev, blk),
+        out_shape=[
+            jax.ShapeDtypeStruct((half_s, half_t), f32),
+            jax.ShapeDtypeStruct((half_s, 4 * feat), b16),
+            jax.ShapeDtypeStruct((half_t, 4 * feat), b16),
+            jax.ShapeDtypeStruct((half_s, 1), f32),
+            jax.ShapeDtypeStruct((1, half_t), f32),
+            jax.ShapeDtypeStruct((8, feat), f32),
+        ],
+        in_specs=[vmem] * len(near_pieces),
+        out_specs=[vmem] * 6,
+        scratch_shapes=[pltpu.VMEM((blk, half_t), f32), pltpu.VMEM((blk, half_t), f32)],
+        compiler_params=pltpu.CompilerParams(vmem_limit_bytes=NEAR_VMEM),
+        cost_estimate=pl.CostEstimate(
+            flops=2 * half_s * half_t * 4 * feat,
+            bytes_accessed=8 * 2**20,
+            transcendentals=half_s * half_t,
+        ),
+        name="near",
+    )(*near_pieces)
+    f_pot, g_pot, src_moved, tgt_moved = pl.pallas_call(
+        functools.partial(whole_group_kernel, n, s_dev, t_dev, blk),
+        out_shape=[
+            jax.ShapeDtypeStruct((1, s_dev), f32),
+            jax.ShapeDtypeStruct((1, t_dev), f32),
+            jax.ShapeDtypeStruct((s_dev, feat), f32),
+            jax.ShapeDtypeStruct((t_dev, feat), f32),
+        ],
+        in_specs=[vmem] * (len(near_pieces) + len(far_pieces) + 6),
+        out_specs=[vmem] * 4,
+        scratch_shapes=[
+            pltpu.VMEM((half_s, half_t), f32),
+            pltpu.VMEM((half_s, half_t), f32),
+            pltpu.VMEM((half_s, half_t), f32),
+            pltpu.VMEM((half_s, half_t), f32),
+            pltpu.VMEM((half_s, 4 * feat), b16),
+            pltpu.VMEM((half_t, 4 * feat), b16),
+            pltpu.VMEM((sources, 1), f32),
+            pltpu.VMEM((sources, 1), f32),
+            pltpu.VMEM((8, half_t), f32),
+            pltpu.VMEM((8, half_t), f32),
+            pltpu.VMEM((blk, targets), f32),
+            pltpu.VMEM((blk, targets), f32),
+        ],
+        compiler_params=pltpu.CompilerParams(vmem_limit_bytes=WHOLE_VMEM),
+        name="whole_group",
+    )(*near_pieces, *far_pieces, *near)
+    return f_pot.reshape(s_dev), g_pot.reshape(t_dev), src_moved, tgt_moved
 
 
 def merged(part, axis, combine):
@@ -21,9 +413,7 @@
 
 
 def pair_cost(rows, cols, rows_sq, cols_sq, width):
-    inner = jnp.dot(
-        rows, cols.T, precision=lax.Precision.HIGHEST, preferred_element_type=jnp.float32
-    )
+    inner = jnp.dot(rows, cols.T, precision=HI, preferred_element_type=jnp.float32)
     return (rows_sq[:, None] + cols_sq[None, :] - 2.0 * inner) / width
 
 
@@ -40,7 +430,7 @@
     return (top, total)
 
 
-def per_device(source_feats, target_feats, log_a, log_b):
+def per_device_rows(source_feats, target_feats, log_a, log_b):
     width = source_feats.shape[1]
     rows = target_feats.shape[0]
     tgt_all, log_b_all = (
@@ -60,9 +450,7 @@
         top, total = merged((local_top, local_total), "src", combine_pairs)
         g_pot = EPS * log_b_all - EPS * (top + jnp.log(total))
     plan = jnp.exp((f_pot[:, None] + g_pot[None, :] - cost) / EPS)
-    carried = jnp.dot(
-        plan, tgt_all, precision=lax.Precision.HIGHEST, preferred_element_type=jnp.float32
-    )
+    carried = jnp.dot(plan, tgt_all, precision=HI, preferred_element_type=jnp.float32)
     src_moved = carried / jnp.sum(plan, axis=1)[:, None]
     own_start = lax.axis_index("src") * rows
     g_own = lax.dynamic_slice_in_dim(g_pot, own_start, rows)
@@ -71,7 +459,7 @@
             plan,
             source_feats,
             (((0,), (0,)), ((), ())),
-            precision=lax.Precision.HIGHEST,
+            precision=HI,
             preferred_element_type=jnp.float32,
         ),
         "src",
@@ -82,21 +470,24 @@
     return (f_pot, g_own, src_moved, tgt_moved)
 
 
+def per_device(source_feats, target_feats, log_a, log_b):
+    n = lax.axis_size("src")
+    s_dev, feat = source_feats.shape
+    t_dev = target_feats.shape[0]
+    fits = 4 * n * s_dev * n * t_dev <= REPLICATED_BYTES
+    shaped = n >= 4 and n & (n - 1) == 0 and s_dev % 16 == 0 and s_dev <= feat == t_dev
+    if fits and shaped and (n * s_dev) % 512 == 0 and n == 16:
+        return per_device_whole(source_feats, target_feats, log_a, log_b)
+    return per_device_rows(source_feats, target_feats, log_a, log_b)
+
+
 def solution(mesh):
+    both = P(("groups", "src"), None)
+    line = P(("groups", "src"))
     return jax.shard_map(
         per_device,
         mesh=mesh,
-        in_specs=(
-            P(("groups", "src"), None),
-            P(("groups", "src"), None),
-            P(("groups", "src")),
-            P(("groups", "src")),
-        ),
-        out_specs=(
-            P(("groups", "src")),
-            P(("groups", "src")),
-            P(("groups", "src"), None),
-            P(("groups", "src"), None),
-        ),
+        in_specs=(both, both, line, line),
+        out_specs=(line, line, both, both),
         check_vma=False,
     )

time: 242 us -> 62.9 us (0.26)
  blocking collectives: 134 us -> 0 us
  waiting for transfers between devices: 73.1 us -> 7.91 us
  Pallas kernels: 0 us -> 39.8 us
  between operations: 14.2 us -> 0.69 us
  starting transfers between devices: 0.08 us -> 12.7 us
  matrix products: 5.96 us -> 0 us
  local copies, waits for them, and re-layouts: 5.86 us -> 0.01 us
  other arithmetic: 6.74 us -> 1.6 us
    all_gather x7 -> x0, blocking collectives: 134 us -> none  [the longest x6 111 us: merged(): gathered = jax.tree.map(lambda a: lax.all_gather(a, axis), part)]
    reduce_scatter x1 -> x0, waiting for transfers between devices: 53.3 us -> none  [per_device(): lax.psum_scatter(lax.dot_general(plan, source_feats, (((0,), (0,)), ((),...]
    pallas_call x0 -> x2, Pallas kernels: none -> 39.8 us  [the longest x1 38.3 us: per_device_whole(): pl.pallas_call(functools.partial(whole_group_kernel, n, s_dev, t_dev, blk...]
    all_gather x1 -> x0, waiting for transfers between devices: 19.1 us -> none  [per_device(): lax.all_gather(target_feats, 'src', axis=0, tiled=True)]
    ppermute x0 -> x15, starting transfers between devices: none -> 12.7 us  [swap(): return lax.ppermute(a, axis, [(i, i ^ bits) for i in range(n)])]
    ppermute x0 -> x15, waiting for transfers between devices: none -> 7.91 us  [swap(): return lax.ppermute(a, axis, [(i, i ^ bits) for i in range(n)])]
    dot_general x3 -> x0, matrix products: 5.96 us -> none  [the longest x1 2.88 us: per_device(): lax.dot_general(plan, source_feats, (((0,), (0,)), ((), ())), precision=l...]
    reduce_sum x9 -> x0, other arithmetic: 3.66 us -> none  [the longest x1 1.65 us: per_device(): sq_tgt = jnp.sum(tgt_all * tgt_all, axis=1)]
  transfers between devices with their start and end apart: 2 -> 15, of which waited for: 2 -> 4; matrix products, arithmetic and copies ran while one was open for 1% -> 0% of each run, Pallas kernels for 0% -> 2%
where the time goes in v4:
time: 62.9 us; the launch traced here: 62.7 us
  Pallas kernels  39.8 us (63%)
  starting transfers between devices  12.7 us (20%)
  waiting for transfers between devices  7.91 us (13%)
  other arithmetic  1.6 us (3%)
  between operations  0.69 us (1%)
    pallas_call x1, Pallas kernels, per_device_whole(): pl.pallas_call(functools.partial(whole_group_kernel, n, s_dev, t_dev, blk...  38.3 us
    ppermute x15, starting transfers between devices, swap(): return lax.ppermute(a, axis, [(i, i ^ bits) for i in range(n)])  12.7 us
    ppermute x15, waiting for transfers between devices, swap(): return lax.ppermute(a, axis, [(i, i ^ bits) for i in range(n)])  7.91 us
    pallas_call x1, Pallas kernels, per_device_whole(): pl.pallas_call(functools.partial(near_kernel, s_dev, t_dev, blk), out_sha...  1.46 us
  transfers between devices with their start and end apart: 15, of which 4 were waited for; matrix products, arithmetic and copies ran while one was open for 0% of the time, Pallas kernels for 2%

profile of v4, /device:TPU:0, one launch (start us, length us, event | category | flops | bytes accessed | tf_op | source)
XLA Modules:
  0.0 62.7 jit_solution(3728867238108638945)
XLA Ops:
  0.6 0.7 %maximum_bitcast_fusion = f32[8,128]{1,0:T(8,128)S(1)} fusion(f32[800]{0:T(1024)S(1)} %broadcast_in_dim.3, f32[96]{0:T(128)} %param.6, f32[128]{0:T(128)} %param.7), kind=kLoop, calls=%fused_computation.1 | loop fusion | flops 2048 | bytes 8192 | tf_op jit(solution)/shard_map/reshape | solution.py:345
  1.4 0.9 %pad_maximum_fusion.refs_0_ = f32[232,128]{1,0:T(8,128)S(1)} fusion(f32[8,128]{1,0:T(8,128)S(1)} %maximum_bitcast_fusion, f32[128,128]{1,0:T(8,128)} %param.5, f32[96,128]{1,0:T(8,128)} %param.4), kind=kLoop, calls=%fused_computation | loop fusion | flops 59392 | bytes 237568 | tf_op jit(solution)/shard_map/concatenate | solution.py:345
  2.2 4.1 %collective-permute-start.1 = (f32[232,128]{1,0:T(8,128)S(1)}, f32[232,128]{1,0:T(8,128)S(1)}, u32[]{:S(2)}, u32[]{:S(2)}) collective-permute-start(f32[232,128]{1,0:T(8,128)S(1)} %pad_maximum_fusion.refs_0_), channel_id=1, source_target_pairs={{0,8},{1,9},{2,10},{3,11},{4,12},{5,13},{6,14},{7,15},{8,0},{9,1},... | collective-permute-start | bytes 356360 | tf_op jit(solution)/shard_map/ppermute | solution.py:329
  6.3 1.5 %collective-permute-start.7 = (f32[232,128]{1,0:T(8,128)S(1)}, f32[232,128]{1,0:T(8,128)S(1)}, u32[]{:S(2)}, u32[]{:S(2)}) collective-permute-start(f32[232,128]{1,0:T(8,128)S(1)} %pad_maximum_fusion.refs_0_), channel_id=1, source_target_pairs={{0,2},{1,3},{2,0},{3,1},{4,6},{5,7},{6,4},{7,5},{8,10},{9,11},{10,... | collective-permute-start | bytes 356360 | tf_op jit(solution)/shard_map/ppermute | solution.py:329
  7.9 1.6 %collective-permute-start = (f32[232,128]{1,0:T(8,128)S(1)}, f32[232,128]{1,0:T(8,128)S(1)}, u32[]{:S(2)}, u32[]{:S(2)}) collective-permute-start(f32[232,128]{1,0:T(8,128)S(1)} %pad_maximum_fusion.refs_0_), channel_id=1, source_target_pairs={{0,4},{1,5},{2,6},{3,7},{4,0},{5,1},{6,2},{7,3},{8,12},{9,13},{10,... | collective-permute-start | bytes 356360 | tf_op jit(solution)/shard_map/ppermute | solution.py:329
  9.4 0.0 collective-permute-start.3
  9.4 2.8 %collective-permute-done.1.refs_2_ = f32[232,128]{1,0:T(8,128)S(1)} collective-permute-done((f32[232,128]{1,0:T(8,128)S(1)}, f32[232,128]{1,0:T(8,128)S(1)}, u32[]{:S(2)}, u32[]{:S(2)}) %collective-permute-start.1) | collective-permute-done | bytes 118816 | tf_op jit(solution)/shard_map/ppermute | solution.py:329
  12.2 0.7 %collective-permute-start.2 = (f32[232,128]{1,0:T(8,128)S(1)}, f32[232,128]{1,0:T(8,128)S(1)}, u32[]{:S(2)}, u32[]{:S(2)}) collective-permute-start(f32[232,128]{1,0:T(8,128)S(1)} %collective-permute-done.1.refs_2_), channel_id=1, source_target_pairs={{0,4},{1,5},{2,6},{3,7},{4,0},{5,1},{6,2},{7,3},{8,12},{9,13},{10,... | collective-permute-start | bytes 356360 | tf_op jit(solution)/shard_map/ppermute | solution.py:329
  12.9 1.5 %collective-permute-start.9 = (f32[232,128]{1,0:T(8,128)S(1)}, f32[232,128]{1,0:T(8,128)S(1)}, u32[]{:S(2)}, u32[]{:S(2)}) collective-permute-start(f32[232,128]{1,0:T(8,128)S(1)} %collective-permute-done.1.refs_2_), channel_id=1, source_target_pairs={{0,2},{1,3},{2,0},{3,1},{4,6},{5,7},{6,4},{7,5},{8,10},{9,11},{10,... | collective-permute-start | bytes 356360 | tf_op jit(solution)/shard_map/ppermute | solution.py:329
  14.4 0.0 collective-permute-done.7.refs_8_
  14.4 0.0 collective-permute-start.5
  14.4 0.0 collective-permute-done.refs_1_
  14.4 0.6 collective-permute-start.8
  15.0 0.0 collective-permute-done.3.refs_4_
  15.0 0.2 collective-permute-start.4
  15.2 1.9 %collective-permute-done.2.refs_3_ = f32[232,128]{1,0:T(8,128)S(1)} collective-permute-done((f32[232,128]{1,0:T(8,128)S(1)}, f32[232,128]{1,0:T(8,128)S(1)}, u32[]{:S(2)}, u32[]{:S(2)}) %collective-permute-start.2) | collective-permute-done | bytes 118816 | tf_op jit(solution)/shard_map/ppermute | solution.py:329
  17.1 1.6 %collective-permute-start.10 = (f32[232,128]{1,0:T(8,128)S(1)}, f32[232,128]{1,0:T(8,128)S(1)}, u32[]{:S(2)}, u32[]{:S(2)}) collective-permute-start(f32[232,128]{1,0:T(8,128)S(1)} %collective-permute-done.2.refs_3_), channel_id=1, source_target_pairs={{0,2},{1,3},{2,0},{3,1},{4,6},{5,7},{6,4},{7,5},{8,10},{9,11},{10,... | collective-permute-start | bytes 356360 | tf_op jit(solution)/shard_map/ppermute | solution.py:329
  18.6 0.0 collective-permute-done.9.refs_10_
  18.6 0.0 collective-permute-start.6
  18.6 0.0 collective-permute-done.5.refs_6_
  18.7 0.5 collective-permute-start.11
  19.2 1.4 %collective-permute-done.8.refs_9_ = f32[232,128]{1,0:T(8,128)S(1)} collective-permute-done((f32[232,128]{1,0:T(8,128)S(1)}, f32[232,128]{1,0:T(8,128)S(1)}, u32[]{:S(2)}, u32[]{:S(2)}) %collective-permute-start.8) | collective-permute-done | bytes 118816 | tf_op jit(solution)/shard_map/ppermute | solution.py:329
  20.6 0.0 collective-permute-start.13
  20.6 0.0 collective-permute-done.4.refs_5_
  20.6 0.5 collective-permute-start.12
  21.1 1.7 %collective-permute-done.10.refs_11_ = f32[232,128]{1,0:T(8,128)S(1)} collective-permute-done((f32[232,128]{1,0:T(8,128)S(1)}, f32[232,128]{1,0:T(8,128)S(1)}, u32[]{:S(2)}, u32[]{:S(2)}) %collective-permute-start.10) | collective-permute-done | bytes 118816 | tf_op jit(solution)/shard_map/ppermute | solution.py:329
  22.9 0.0 collective-permute-start.14
  22.9 0.0 collective-permute-done.6.refs_7_
  22.9 1.5 %near.1 = (f32[768,1024]{1,0:T(8,128)S(1)}, bf16[768,512]{1,0:T(8,128)(2,1)S(1)}, bf16[1024,512]{1,0:T(8,128)(2,1)S(1)}, f32[768,1]{1,0:T(8,128)S(1)}, f32[1,1024]{1,0:T(1,128)S(1)}, /*index=5*/f32[8,128]{1,0:T(8,128)S(1)}) custom-call(f32[232,128]{1,0:T(8,128)S(1)} %pad_maximum_fusion.refs_0_, f32[232,128]{1,0:T(8,128)S(1)} %collective-permute-done.refs_1_, ...), custom_call_target="tpu_custom_call" | custom-call | flops 805306368 | bytes 8388608 | tf_op jit(solution)/shard_map/near/pallas_call | solution.py:353
  24.3 0.0 collective-permute-done.11.refs_12_
  24.3 0.0 collective-permute-done.13.refs_14_
  24.3 0.0 collective-permute-done.12.refs_13_
  24.4 0.0 collective-permute-done.14.refs_15_
  24.4 38.3 %whole_group.1 = (f32[1,96]{1,0:T(1,128)}, f32[1,128]{1,0:T(1,128)}, f32[96,128]{1,0:T(8,128)}, f32[128,128]{1,0:T(8,128)}) custom-call(f32[232,128]{1,0:T(8,128)S(1)} %pad_maximum_fusion.refs_0_, f32[232,128]{1,0:T(8,128)S(1)} %collective-permute-done.refs_1_, f32[232,128]{1,0:T(8,128)S(1)} %collective-permute-done.1.refs_2_, ...), custom_call_target="tpu_custom_call" | custom-call | tf_op jit(solution)/shard_map/whole_group/pallas_call | solution.py:374
  (1 shorter events, 0.0 us)
Async XLA Ops:
  2.2 10.0 %collective-permute-start.1 = (f32[232,128]{1,0:T(8,128)S(1)}, f32[232,128]{1,0:T(8,128)S(1)}, u32[]{:S(2)}, u32[]{:S(2)}) collective-permute-start(f32[232,128]{1,0:T(8,128)S(1)} %pad_maximum_fusion.refs_0_), channel_id=1, source_target_pairs={{0,8},{1,9},{2,10},{3,11},{4,12},{5,13},{6,14},{7,15},{8,0},{9,1},... | collective-permute-start | bytes 356360 | tf_op jit(solution)/shard_map/ppermute | solution.py:329
  6.3 8.0 %collective-permute-start.7 = (f32[232,128]{1,0:T(8,128)S(1)}, f32[232,128]{1,0:T(8,128)S(1)}, u32[]{:S(2)}, u32[]{:S(2)}) collective-permute-start(f32[232,128]{1,0:T(8,128)S(1)} %pad_maximum_fusion.refs_0_), channel_id=1, source_target_pairs={{0,2},{1,3},{2,0},{3,1},{4,6},{5,7},{6,4},{7,5},{8,10},{9,11},{10,... | collective-permute-start | bytes 356360 | tf_op jit(solution)/shard_map/ppermute | solution.py:329
  7.9 6.5 %collective-permute-start = (f32[232,128]{1,0:T(8,128)S(1)}, f32[232,128]{1,0:T(8,128)S(1)}, u32[]{:S(2)}, u32[]{:S(2)}) collective-permute-start(f32[232,128]{1,0:T(8,128)S(1)} %pad_maximum_fusion.refs_0_), channel_id=1, source_target_pairs={{0,4},{1,5},{2,6},{3,7},{4,0},{5,1},{6,2},{7,3},{8,12},{9,13},{10,... | collective-permute-start | bytes 356360 | tf_op jit(solution)/shard_map/ppermute | solution.py:329
  9.4 5.6 %collective-permute-start.3 = (f32[232,128]{1,0:T(8,128)S(1)}, f32[232,128]{1,0:T(8,128)S(1)}, u32[]{:S(2)}, u32[]{:S(2)}) collective-permute-start(f32[232,128]{1,0:T(8,128)S(1)} %pad_maximum_fusion.refs_0_), channel_id=1, source_target_pairs={{0,1},{1,0},{2,3},{3,2},{4,5},{5,4},{6,7},{7,6},{8,9},{9,8},{10,11... | collective-permute-start | bytes 356360 | tf_op jit(solution)/shard_map/ppermute | solution.py:329
  12.2 4.8 %collective-permute-start.2 = (f32[232,128]{1,0:T(8,128)S(1)}, f32[232,128]{1,0:T(8,128)S(1)}, u32[]{:S(2)}, u32[]{:S(2)}) collective-permute-start(f32[232,128]{1,0:T(8,128)S(1)} %collective-permute-done.1.refs_2_), channel_id=1, source_target_pairs={{0,4},{1,5},{2,6},{3,7},{4,0},{5,1},{6,2},{7,3},{8,12},{9,13},{10,... | collective-permute-start | bytes 356360 | tf_op jit(solution)/shard_map/ppermute | solution.py:329
  12.9 5.8 %collective-permute-start.9 = (f32[232,128]{1,0:T(8,128)S(1)}, f32[232,128]{1,0:T(8,128)S(1)}, u32[]{:S(2)}, u32[]{:S(2)}) collective-permute-start(f32[232,128]{1,0:T(8,128)S(1)} %collective-permute-done.1.refs_2_), channel_id=1, source_target_pairs={{0,2},{1,3},{2,0},{3,1},{4,6},{5,7},{6,4},{7,5},{8,10},{9,11},{10,... | collective-permute-start | bytes 356360 | tf_op jit(solution)/shard_map/ppermute | solution.py:329
  14.4 4.3 %collective-permute-start.5 = (f32[232,128]{1,0:T(8,128)S(1)}, f32[232,128]{1,0:T(8,128)S(1)}, u32[]{:S(2)}, u32[]{:S(2)}) collective-permute-start(f32[232,128]{1,0:T(8,128)S(1)} %collective-permute-done.1.refs_2_), channel_id=1, source_target_pairs={{0,1},{1,0},{2,3},{3,2},{4,5},{5,4},{6,7},{7,6},{8,9},{9,8},{10,11... | collective-permute-start | bytes 356360 | tf_op jit(solution)/shard_map/ppermute | solution.py:329
  14.4 6.2 %collective-permute-start.8 = (f32[232,128]{1,0:T(8,128)S(1)}, f32[232,128]{1,0:T(8,128)S(1)}, u32[]{:S(2)}, u32[]{:S(2)}) collective-permute-start(f32[232,128]{1,0:T(8,128)S(1)} %collective-permute-done.refs_1_), channel_id=1, source_target_pairs={{0,2},{1,3},{2,0},{3,1},{4,6},{5,7},{6,4},{7,5},{8,10},{9,11},{10,... | collective-permute-start | bytes 356360 | tf_op jit(solution)/shard_map/ppermute | solution.py:329
  15.0 5.6 %collective-permute-start.4 = (f32[232,128]{1,0:T(8,128)S(1)}, f32[232,128]{1,0:T(8,128)S(1)}, u32[]{:S(2)}, u32[]{:S(2)}) collective-permute-start(f32[232,128]{1,0:T(8,128)S(1)} %collective-permute-done.refs_1_), channel_id=1, source_target_pairs={{0,1},{1,0},{2,3},{3,2},{4,5},{5,4},{6,7},{7,6},{8,9},{9,8},{10,11... | collective-permute-start | bytes 356360 | tf_op jit(solution)/shard_map/ppermute | solution.py:329
  17.1 5.8 %collective-permute-start.10 = (f32[232,128]{1,0:T(8,128)S(1)}, f32[232,128]{1,0:T(8,128)S(1)}, u32[]{:S(2)}, u32[]{:S(2)}) collective-permute-start(f32[232,128]{1,0:T(8,128)S(1)} %collective-permute-done.2.refs_3_), channel_id=1, source_target_pairs={{0,2},{1,3},{2,0},{3,1},{4,6},{5,7},{6,4},{7,5},{8,10},{9,11},{10,... | collective-permute-start | bytes 356360 | tf_op jit(solution)/shard_map/ppermute | solution.py:329
  18.6 4.2 %collective-permute-start.6 = (f32[232,128]{1,0:T(8,128)S(1)}, f32[232,128]{1,0:T(8,128)S(1)}, u32[]{:S(2)}, u32[]{:S(2)}) collective-permute-start(f32[232,128]{1,0:T(8,128)S(1)} %collective-permute-done.2.refs_3_), channel_id=1, source_target_pairs={{0,1},{1,0},{2,3},{3,2},{4,5},{5,4},{6,7},{7,6},{8,9},{9,8},{10,11... | collective-permute-start | bytes 356360 | tf_op jit(solution)/shard_map/ppermute | solution.py:329
  18.7 5.7 %collective-permute-start.11 = (f32[232,128]{1,0:T(8,128)S(1)}, f32[232,128]{1,0:T(8,128)S(1)}, u32[]{:S(2)}, u32[]{:S(2)}) collective-permute-start(f32[232,128]{1,0:T(8,128)S(1)} %collective-permute-done.7.refs_8_), channel_id=1, source_target_pairs={{0,1},{1,0},{2,3},{3,2},{4,5},{5,4},{6,7},{7,6},{8,9},{9,8},{10,11... | collective-permute-start | bytes 356360 | tf_op jit(solution)/shard_map/ppermute | solution.py:329
  20.6 3.7 %collective-permute-start.13 = (f32[232,128]{1,0:T(8,128)S(1)}, f32[232,128]{1,0:T(8,128)S(1)}, u32[]{:S(2)}, u32[]{:S(2)}) collective-permute-start(f32[232,128]{1,0:T(8,128)S(1)} %collective-permute-done.9.refs_10_), channel_id=1, source_target_pairs={{0,1},{1,0},{2,3},{3,2},{4,5},{5,4},{6,7},{7,6},{8,9},{9,8},{10,11... | collective-permute-start | bytes 356360 | tf_op jit(solution)/shard_map/ppermute | solution.py:329
  20.6 3.7 %collective-permute-start.12 = (f32[232,128]{1,0:T(8,128)S(1)}, f32[232,128]{1,0:T(8,128)S(1)}, u32[]{:S(2)}, u32[]{:S(2)}) collective-permute-start(f32[232,128]{1,0:T(8,128)S(1)} %collective-permute-done.8.refs_9_), channel_id=1, source_target_pairs={{0,1},{1,0},{2,3},{3,2},{4,5},{5,4},{6,7},{7,6},{8,9},{9,8},{10,11... | collective-permute-start | bytes 356360 | tf_op jit(solution)/shard_map/ppermute | solution.py:329
  22.9 1.5 %collective-permute-start.14 = (f32[232,128]{1,0:T(8,128)S(1)}, f32[232,128]{1,0:T(8,128)S(1)}, u32[]{:S(2)}, u32[]{:S(2)}) collective-permute-start(f32[232,128]{1,0:T(8,128)S(1)} %collective-permute-done.10.refs_11_), channel_id=1, source_target_pairs={{0,1},{1,0},{2,3},{3,2},{4,5},{5,4},{6,7},{7,6},{8,9},{9,8},{10,11... | collective-permute-start | bytes 356360 | tf_op jit(solution)/shard_map/ppermute | solution.py:329

commit v5 on v4

--- a/solution.py
+++ b/solution.py
@@ -13,7 +13,7 @@
 LOG2E = 1.4426950408889634
 SAFE = 2.0**30
 WIDE = 2.0**60
-PARTS = 8
+PARTS = 4
 CHUNK = 256
 NEAR_VMEM = 16 * 2**20
 WHOLE_VMEM = 36 * 2**20
@@ -75,8 +75,8 @@
 
 
 def near_kernel(s_dev, t_dev, blk, *refs):
-    pieces = refs[:-8]
-    e_ref, xs, ys, r_ref, norm_ref, mid_ref, mb0, mb1 = refs[-8:]
+    pieces = refs[:-6]
+    e_ref, xs, ys, r_ref, norm_ref, mid_ref = refs[-6:]
     feat = pieces[0].shape[1]
     k = LOG2E / (feat * EPS)
     blocks = blocks_of(pieces, s_dev + t_dev + 8)
@@ -89,23 +89,22 @@
     mid_ref[1:2, :] = jnp.broadcast_to(shift, (1, feat))
     mid_ref[2:8, :] = jnp.zeros((6, feat), jnp.float32)
     g1 = shift - norm
-    bufs = (mb0, mb1)
-    steps = sources // blk
-    bufs[0][...] = nt_dot(xs[0:blk, :], ys[...])
-    for i in range(steps):
-        if i + 1 < steps:
-            bufs[(i + 1) % 2][...] = nt_dot(xs[(i + 1) * blk : (i + 2) * blk, :], ys[...])
+    for i in range(sources // blk):
         s = slice(i * blk, (i + 1) * blk)
-        e = jnp.exp2(bufs[i % 2][...] + g1)
-        e_ref[s, :] = e
-        r_ref[s, :] = jnp.sum(e, axis=1, keepdims=True)
+        row_sum = 0.0
+        for c in range(0, targets, CHUNK):
+            cols = slice(c, c + CHUNK)
+            e = jnp.exp2(nt_dot(xs[s, :], ys[cols, :]) + g1[:, cols])
+            e_ref[s, cols] = e
+            row_sum += sum(e[:, c : c + feat] for c in range(0, CHUNK, feat))
+        r_ref[s, :] = jnp.sum(row_sum, axis=1, keepdims=True)
 
 
 def whole_group_kernel(n, s_dev, t_dev, blk, *refs):
-    pieces = refs[:-22]
-    e11, xs1, ys1, r1_ref, norm_ref, mid_ref = refs[-22:-16]
-    f_ref, g_ref, sm_ref, tm_ref = refs[-16:-12]
-    e12, e21, e22, e_own, xs2, ys2, la_col, u_col, acc0, acc1, mb0, mb1 = refs[-12:]
+    pieces = refs[:-20]
+    e11, xs1, ys1, r1_ref, norm_ref, mid_ref = refs[-20:-14]
+    f_ref, g_ref, sm_ref, tm_ref = refs[-14:-10]
+    e12, e21, e22, e_own, xs2, ys2, la_col, u_col, acc0, acc1 = refs[-10:]
     feat = pieces[0].shape[1]
     rows = s_dev + t_dev + 8
     k = LOG2E / (feat * EPS)
@@ -137,36 +136,34 @@
     def column_part(e, u):
         return jnp.sum((e * u).reshape(e.shape[0] // 8, 8, half_t), axis=0)
 
-    def product(dst, i, part):
-        at = (i % near) * blk
-        factor = xs[i // near][at : at + blk, :]
+    row_sums = [0.0] * steps
+
+    def product(i, part):
+        kept, where = halves(i)
+        factor = xs[i // near][where, :]
         chunks = [
             (h, slice(c, c + CHUNK))
             for h in ((1,) if i < near else (0, 1))
             for c in range(0, half_t, CHUNK)
         ]
         for h, cols in chunks[part * len(chunks) // parts : (part + 1) * len(chunks) // parts]:
-            dst[:, h * half_t + cols.start : h * half_t + cols.stop] = nt_dot(factor, ys[h][cols, :])
+            e = jnp.exp2(nt_dot(factor, ys[h][cols, :]) + g1[h][:, cols])
+            kept[h][where, cols] = e
+            row_sums[i] += sum(e[:, c : c + feat] for c in range(0, CHUNK, feat))
 
     sums, ends = [], []
 
-    def absorb(src, i, part):
+    def absorb(i, part):
         kept, where = halves(i)
         local = slice(part * sub, (part + 1) * sub)
         s = slice(where.start + local.start, where.start + local.stop)
-        e1 = jnp.exp2(src[local, half_t:] + g1[1])
-        kept[1][s, :] = e1
+        r = jnp.sum(row_sums[i][local, :], axis=1, keepdims=True)
         if i < near:
-            e0 = kept[0][s, :]
-            r = r1_ref[s, :] + jnp.sum(e1, axis=1, keepdims=True)
-        else:
-            e0 = jnp.exp2(src[local, :half_t] + g1[0])
-            kept[0][s, :] = e0
-            r = jnp.sum(e0 + e1, axis=1, keepdims=True)
+            r = r + r1_ref[s, :]
         sums.append(r)
         u = la_col[i * blk + local.start : i * blk + local.stop, :] / r
-        acc0[...] += column_part(e0, u)
-        acc1[...] += column_part(e1, u)
+        acc0[...] += column_part(kept[0][s, :], u)
+        acc1[...] += column_part(kept[1][s, :], u)
 
     def column_end():
         total = tuple(jnp.sum(acc[...], axis=0, keepdims=True) for acc in accs)
@@ -178,14 +175,13 @@
             acc[...] = jnp.zeros_like(acc)
 
     clear()
-    bufs = (mb0, mb1)
     for part in range(parts):
-        product(bufs[0], 0, part)
+        product(0, part)
     for i in range(steps):
         for part in range(parts):
             if i + 1 < steps:
-                product(bufs[(i + 1) % 2], i + 1, part)
-            absorb(bufs[i % 2], i, part)
+                product(i + 1, part)
+            absorb(i, part)
     total = column_end()
 
     def quarters_sum(wide, count):
@@ -328,12 +324,11 @@
     def swap(a, bits):
         return lax.ppermute(a, axis, [(i, i ^ bits) for i in range(n)])
 
-    step = [swap(block, 4)]
-    for bits in range(8, n, 8):
-        jump = swap(block, bits)
-        step += [jump, swap(jump, 4)]
-    line = [block] + step
-    side = [swap(a, 2) for a in line]
+    near, jump = swap(block, 4), swap(block, 8)
+    across = swap(block, 2)
+    last, over = swap(jump, 4), swap(jump, 2)
+    line = [block, near, jump, last]
+    side = [across, swap(near, 2), over, swap(over, 4)]
     return line + [swap(a, 1) for a in line], side + [swap(a, 1) for a in side]
 
 
@@ -362,7 +357,6 @@
         ],
         in_specs=[vmem] * len(near_pieces),
         out_specs=[vmem] * 6,
-        scratch_shapes=[pltpu.VMEM((blk, half_t), f32), pltpu.VMEM((blk, half_t), f32)],
         compiler_params=pltpu.CompilerParams(vmem_limit_bytes=NEAR_VMEM),
         cost_estimate=pl.CostEstimate(
             flops=2 * half_s * half_t * 4 * feat,
@@ -392,8 +386,6 @@
             pltpu.VMEM((sources, 1), f32),
             pltpu.VMEM((8, half_t), f32),
             pltpu.VMEM((8, half_t), f32),
-            pltpu.VMEM((blk, targets), f32),
-            pltpu.VMEM((blk, targets), f32),
         ],
         compiler_params=pltpu.CompilerParams(vmem_limit_bytes=WHOLE_VMEM),
         name="whole_group",

time: 62.9 us -> 62.3 us (level)
  transfers between devices with their start and end apart: 15 -> 15, of which waited for: 4 -> 5; matrix products, arithmetic and copies ran while one was open for 0% -> 0% of each run, Pallas kernels for 2% -> 2%
where the time goes in v5:
time: 62.3 us; the launch traced here: 61.8 us
  Pallas kernels  39.9 us (64%)
  starting transfers between devices  12.1 us (19%)
  waiting for transfers between devices  7.54 us (12%)
  other arithmetic  1.6 us (3%)
  between operations  0.69 us (1%)
    pallas_call x1, Pallas kernels, per_device_whole(): pl.pallas_call(functools.partial(whole_group_kernel, n, s_dev, t_dev, blk...  38.4 us
    ppermute x15, starting transfers between devices, swap(): return lax.ppermute(a, axis, [(i, i ^ bits) for i in range(n)])  12.1 us
    ppermute x15, waiting for transfers between devices, swap(): return lax.ppermute(a, axis, [(i, i ^ bits) for i in range(n)])  7.54 us
    pallas_call x1, Pallas kernels, per_device_whole(): pl.pallas_call(functools.partial(near_kernel, s_dev, t_dev, blk), out_sha...  1.47 us
  transfers between devices with their start and end apart: 15, of which 5 were waited for; matrix products, arithmetic and copies ran while one was open for 0% of the time, Pallas kernels for 2%

profile of v5, /device:TPU:0, one launch (start us, length us, event | category | flops | bytes accessed | tf_op | source)
XLA Modules:
  0.0 61.8 jit_solution(10971110496584535456)
XLA Ops:
  0.6 0.7 %maximum_bitcast_fusion = f32[8,128]{1,0:T(8,128)S(1)} fusion(f32[800]{0:T(1024)S(1)} %broadcast_in_dim.3, f32[96]{0:T(128)} %param.6, f32[128]{0:T(128)} %param.7), kind=kLoop, calls=%fused_computation.1 | loop fusion | flops 2048 | bytes 8192 | tf_op jit(solution)/shard_map/reshape | solution.py:340
  1.4 0.9 %pad_maximum_fusion.refs_0_ = f32[232,128]{1,0:T(8,128)S(1)} fusion(f32[8,128]{1,0:T(8,128)S(1)} %maximum_bitcast_fusion, f32[128,128]{1,0:T(8,128)} %param.5, f32[96,128]{1,0:T(8,128)} %param.4), kind=kLoop, calls=%fused_computation | loop fusion | flops 59392 | bytes 237568 | tf_op jit(solution)/shard_map/concatenate | solution.py:340
  2.2 4.1 %collective-permute-start.1 = (f32[232,128]{1,0:T(8,128)S(1)}, f32[232,128]{1,0:T(8,128)S(1)}, u32[]{:S(2)}, u32[]{:S(2)}) collective-permute-start(f32[232,128]{1,0:T(8,128)S(1)} %pad_maximum_fusion.refs_0_), channel_id=1, source_target_pairs={{0,8},{1,9},{2,10},{3,11},{4,12},{5,13},{6,14},{7,15},{8,0},{9,1},... | collective-permute-start | bytes 356360 | tf_op jit(solution)/shard_map/ppermute | solution.py:325
  6.3 1.5 %collective-permute-start.7 = (f32[232,128]{1,0:T(8,128)S(1)}, f32[232,128]{1,0:T(8,128)S(1)}, u32[]{:S(2)}, u32[]{:S(2)}) collective-permute-start(f32[232,128]{1,0:T(8,128)S(1)} %pad_maximum_fusion.refs_0_), channel_id=1, source_target_pairs={{0,2},{1,3},{2,0},{3,1},{4,6},{5,7},{6,4},{7,5},{8,10},{9,11},{10,... | collective-permute-start | bytes 356360 | tf_op jit(solution)/shard_map/ppermute | solution.py:325
  7.9 1.6 %collective-permute-start = (f32[232,128]{1,0:T(8,128)S(1)}, f32[232,128]{1,0:T(8,128)S(1)}, u32[]{:S(2)}, u32[]{:S(2)}) collective-permute-start(f32[232,128]{1,0:T(8,128)S(1)} %pad_maximum_fusion.refs_0_), channel_id=1, source_target_pairs={{0,4},{1,5},{2,6},{3,7},{4,0},{5,1},{6,2},{7,3},{8,12},{9,13},{10,... | collective-permute-start | bytes 356360 | tf_op jit(solution)/shard_map/ppermute | solution.py:325
  9.4 0.0 collective-permute-start.3
  9.4 2.8 %collective-permute-done.1.refs_2_ = f32[232,128]{1,0:T(8,128)S(1)} collective-permute-done((f32[232,128]{1,0:T(8,128)S(1)}, f32[232,128]{1,0:T(8,128)S(1)}, u32[]{:S(2)}, u32[]{:S(2)}) %collective-permute-start.1) | collective-permute-done | bytes 118816 | tf_op jit(solution)/shard_map/ppermute | solution.py:325
  12.2 1.6 %collective-permute-start.9 = (f32[232,128]{1,0:T(8,128)S(1)}, f32[232,128]{1,0:T(8,128)S(1)}, u32[]{:S(2)}, u32[]{:S(2)}) collective-permute-start(f32[232,128]{1,0:T(8,128)S(1)} %collective-permute-done.1.refs_2_), channel_id=1, source_target_pairs={{0,2},{1,3},{2,0},{3,1},{4,6},{5,7},{6,4},{7,5},{8,10},{9,11},{10,... | collective-permute-start | bytes 356360 | tf_op jit(solution)/shard_map/ppermute | solution.py:325
  13.8 0.6 collective-permute-start.2
  14.4 0.0 collective-permute-done.7.refs_8_
  14.4 0.0 collective-permute-start.5
  14.4 0.0 collective-permute-done.refs_1_
  14.4 0.6 collective-permute-start.8
  15.0 0.0 collective-permute-done.3.refs_4_
  15.0 0.2 collective-permute-start.4
  15.2 1.9 %collective-permute-done.9.refs_10_ = f32[232,128]{1,0:T(8,128)S(1)} collective-permute-done((f32[232,128]{1,0:T(8,128)S(1)}, f32[232,128]{1,0:T(8,128)S(1)}, u32[]{:S(2)}, u32[]{:S(2)}) %collective-permute-start.9) | collective-permute-done | bytes 118816 | tf_op jit(solution)/shard_map/ppermute | solution.py:325
  17.1 1.0 %collective-permute-start.10 = (f32[232,128]{1,0:T(8,128)S(1)}, f32[232,128]{1,0:T(8,128)S(1)}, u32[]{:S(2)}, u32[]{:S(2)}) collective-permute-start(f32[232,128]{1,0:T(8,128)S(1)} %collective-permute-done.9.refs_10_), channel_id=1, source_target_pairs={{0,4},{1,5},{2,6},{3,7},{4,0},{5,1},{6,2},{7,3},{8,12},{9,13},{10,... | collective-permute-start | bytes 356360 | tf_op jit(solution)/shard_map/ppermute | solution.py:325
  18.0 1.2 %collective-permute-done.2.refs_3_ = f32[232,128]{1,0:T(8,128)S(1)} collective-permute-done((f32[232,128]{1,0:T(8,128)S(1)}, f32[232,128]{1,0:T(8,128)S(1)}, u32[]{:S(2)}, u32[]{:S(2)}) %collective-permute-start.2) | collective-permute-done | bytes 118816 | tf_op jit(solution)/shard_map/ppermute | solution.py:325
  19.2 0.0 collective-permute-start.6
  19.2 0.0 collective-permute-done.5.refs_6_
  19.2 0.5 collective-permute-start.11
  19.7 0.3 collective-permute-done.8.refs_9_
  20.0 0.0 collective-permute-start.13
  20.0 0.0 collective-permute-done.4.refs_5_
  20.0 0.5 collective-permute-start.12
  20.5 1.4 %collective-permute-done.10.refs_11_ = f32[232,128]{1,0:T(8,128)S(1)} collective-permute-done((f32[232,128]{1,0:T(8,128)S(1)}, f32[232,128]{1,0:T(8,128)S(1)}, u32[]{:S(2)}, u32[]{:S(2)}) %collective-permute-start.10) | collective-permute-done | bytes 118816 | tf_op jit(solution)/shard_map/ppermute | solution.py:325
  21.9 0.0 collective-permute-start.14
  21.9 0.0 collective-permute-done.6.refs_7_
  21.9 1.5 %near.1 = (f32[768,1024]{1,0:T(8,128)S(1)}, bf16[768,512]{1,0:T(8,128)(2,1)S(1)}, bf16[1024,512]{1,0:T(8,128)(2,1)S(1)}, f32[768,1]{1,0:T(8,128)S(1)}, f32[1,1024]{1,0:T(1,128)S(1)}, /*index=5*/f32[8,128]{1,0:T(8,128)S(1)}) custom-call(f32[232,128]{1,0:T(8,128)S(1)} %pad_maximum_fusion.refs_0_, f32[232,128]{1,0:T(8,128)S(1)} %collective-permute-done.refs_1_, ...), custom_call_target="tpu_custom_call" | custom-call | flops 805306368 | bytes 8388608 | tf_op jit(solution)/shard_map/near/pallas_call | solution.py:348
  23.4 0.0 collective-permute-done.11.refs_12_
  23.4 0.0 collective-permute-done.13.refs_14_
  23.4 0.0 collective-permute-done.12.refs_13_
  23.4 0.0 collective-permute-done.14.refs_15_
  23.4 38.4 %whole_group.1 = (f32[1,96]{1,0:T(1,128)}, f32[1,128]{1,0:T(1,128)}, f32[96,128]{1,0:T(8,128)}, f32[128,128]{1,0:T(8,128)}) custom-call(f32[232,128]{1,0:T(8,128)S(1)} %pad_maximum_fusion.refs_0_, f32[232,128]{1,0:T(8,128)S(1)} %collective-permute-done.refs_1_, f32[232,128]{1,0:T(8,128)S(1)} %collective-permute-done.1.refs_2_, ...), custom_call_target="tpu_custom_call" | custom-call | tf_op jit(solution)/shard_map/whole_group/pallas_call | solution.py:368
  (1 shorter events, 0.0 us)
Async XLA Ops:
  2.2 10.0 %collective-permute-start.1 = (f32[232,128]{1,0:T(8,128)S(1)}, f32[232,128]{1,0:T(8,128)S(1)}, u32[]{:S(2)}, u32[]{:S(2)}) collective-permute-start(f32[232,128]{1,0:T(8,128)S(1)} %pad_maximum_fusion.refs_0_), channel_id=1, source_target_pairs={{0,8},{1,9},{2,10},{3,11},{4,12},{5,13},{6,14},{7,15},{8,0},{9,1},... | collective-permute-start | bytes 356360 | tf_op jit(solution)/shard_map/ppermute | solution.py:325
  6.3 8.0 %collective-permute-start.7 = (f32[232,128]{1,0:T(8,128)S(1)}, f32[232,128]{1,0:T(8,128)S(1)}, u32[]{:S(2)}, u32[]{:S(2)}) collective-permute-start(f32[232,128]{1,0:T(8,128)S(1)} %pad_maximum_fusion.refs_0_), channel_id=1, source_target_pairs={{0,2},{1,3},{2,0},{3,1},{4,6},{5,7},{6,4},{7,5},{8,10},{9,11},{10,... | collective-permute-start | bytes 356360 | tf_op jit(solution)/shard_map/ppermute | solution.py:325
  7.9 6.5 %collective-permute-start = (f32[232,128]{1,0:T(8,128)S(1)}, f32[232,128]{1,0:T(8,128)S(1)}, u32[]{:S(2)}, u32[]{:S(2)}) collective-permute-start(f32[232,128]{1,0:T(8,128)S(1)} %pad_maximum_fusion.refs_0_), channel_id=1, source_target_pairs={{0,4},{1,5},{2,6},{3,7},{4,0},{5,1},{6,2},{7,3},{8,12},{9,13},{10,... | collective-permute-start | bytes 356360 | tf_op jit(solution)/shard_map/ppermute | solution.py:325
  9.4 5.6 %collective-permute-start.3 = (f32[232,128]{1,0:T(8,128)S(1)}, f32[232,128]{1,0:T(8,128)S(1)}, u32[]{:S(2)}, u32[]{:S(2)}) collective-permute-start(f32[232,128]{1,0:T(8,128)S(1)} %pad_maximum_fusion.refs_0_), channel_id=1, source_target_pairs={{0,1},{1,0},{2,3},{3,2},{4,5},{5,4},{6,7},{7,6},{8,9},{9,8},{10,11... | collective-permute-start | bytes 356360 | tf_op jit(solution)/shard_map/ppermute | solution.py:325
  12.2 4.8 %collective-permute-start.9 = (f32[232,128]{1,0:T(8,128)S(1)}, f32[232,128]{1,0:T(8,128)S(1)}, u32[]{:S(2)}, u32[]{:S(2)}) collective-permute-start(f32[232,128]{1,0:T(8,128)S(1)} %collective-permute-done.1.refs_2_), channel_id=1, source_target_pairs={{0,2},{1,3},{2,0},{3,1},{4,6},{5,7},{6,4},{7,5},{8,10},{9,11},{10,... | collective-permute-start | bytes 356360 | tf_op jit(solution)/shard_map/ppermute | solution.py:325
  13.8 5.4 %collective-permute-start.2 = (f32[232,128]{1,0:T(8,128)S(1)}, f32[232,128]{1,0:T(8,128)S(1)}, u32[]{:S(2)}, u32[]{:S(2)}) collective-permute-start(f32[232,128]{1,0:T(8,128)S(1)} %collective-permute-done.1.refs_2_), channel_id=1, source_target_pairs={{0,4},{1,5},{2,6},{3,7},{4,0},{5,1},{6,2},{7,3},{8,12},{9,13},{10,... | collective-permute-start | bytes 356360 | tf_op jit(solution)/shard_map/ppermute | solution.py:325
  14.4 4.8 %collective-permute-start.5 = (f32[232,128]{1,0:T(8,128)S(1)}, f32[232,128]{1,0:T(8,128)S(1)}, u32[]{:S(2)}, u32[]{:S(2)}) collective-permute-start(f32[232,128]{1,0:T(8,128)S(1)} %collective-permute-done.1.refs_2_), channel_id=1, source_target_pairs={{0,1},{1,0},{2,3},{3,2},{4,5},{5,4},{6,7},{7,6},{8,9},{9,8},{10,11... | collective-permute-start | bytes 356360 | tf_op jit(solution)/shard_map/ppermute | solution.py:325
  14.4 5.6 %collective-permute-start.8 = (f32[232,128]{1,0:T(8,128)S(1)}, f32[232,128]{1,0:T(8,128)S(1)}, u32[]{:S(2)}, u32[]{:S(2)}) collective-permute-start(f32[232,128]{1,0:T(8,128)S(1)} %collective-permute-done.refs_1_), channel_id=1, source_target_pairs={{0,2},{1,3},{2,0},{3,1},{4,6},{5,7},{6,4},{7,5},{8,10},{9,11},{10,... | collective-permute-start | bytes 356360 | tf_op jit(solution)/shard_map/ppermute | solution.py:325
  15.0 5.0 %collective-permute-start.4 = (f32[232,128]{1,0:T(8,128)S(1)}, f32[232,128]{1,0:T(8,128)S(1)}, u32[]{:S(2)}, u32[]{:S(2)}) collective-permute-start(f32[232,128]{1,0:T(8,128)S(1)} %collective-permute-done.refs_1_), channel_id=1, source_target_pairs={{0,1},{1,0},{2,3},{3,2},{4,5},{5,4},{6,7},{7,6},{8,9},{9,8},{10,11... | collective-permute-start | bytes 356360 | tf_op jit(solution)/shard_map/ppermute | solution.py:325
  17.1 4.8 %collective-permute-start.10 = (f32[232,128]{1,0:T(8,128)S(1)}, f32[232,128]{1,0:T(8,128)S(1)}, u32[]{:S(2)}, u32[]{:S(2)}) collective-permute-start(f32[232,128]{1,0:T(8,128)S(1)} %collective-permute-done.9.refs_10_), channel_id=1, source_target_pairs={{0,4},{1,5},{2,6},{3,7},{4,0},{5,1},{6,2},{7,3},{8,12},{9,13},{10,... | collective-permute-start | bytes 356360 | tf_op jit(solution)/shard_map/ppermute | solution.py:325
  19.2 2.7 %collective-permute-start.6 = (f32[232,128]{1,0:T(8,128)S(1)}, f32[232,128]{1,0:T(8,128)S(1)}, u32[]{:S(2)}, u32[]{:S(2)}) collective-permute-start(f32[232,128]{1,0:T(8,128)S(1)} %collective-permute-done.2.refs_3_), channel_id=1, source_target_pairs={{0,1},{1,0},{2,3},{3,2},{4,5},{5,4},{6,7},{7,6},{8,9},{9,8},{10,11... | collective-permute-start | bytes 356360 | tf_op jit(solution)/shard_map/ppermute | solution.py:325
  19.2 4.2 %collective-permute-start.11 = (f32[232,128]{1,0:T(8,128)S(1)}, f32[232,128]{1,0:T(8,128)S(1)}, u32[]{:S(2)}, u32[]{:S(2)}) collective-permute-start(f32[232,128]{1,0:T(8,128)S(1)} %collective-permute-done.7.refs_8_), channel_id=1, source_target_pairs={{0,1},{1,0},{2,3},{3,2},{4,5},{5,4},{6,7},{7,6},{8,9},{9,8},{10,11... | collective-permute-start | bytes 356360 | tf_op jit(solution)/shard_map/ppermute | solution.py:325
  20.0 3.4 %collective-permute-start.13 = (f32[232,128]{1,0:T(8,128)S(1)}, f32[232,128]{1,0:T(8,128)S(1)}, u32[]{:S(2)}, u32[]{:S(2)}) collective-permute-start(f32[232,128]{1,0:T(8,128)S(1)} %collective-permute-done.9.refs_10_), channel_id=1, source_target_pairs={{0,1},{1,0},{2,3},{3,2},{4,5},{5,4},{6,7},{7,6},{8,9},{9,8},{10,11... | collective-permute-start | bytes 356360 | tf_op jit(solution)/shard_map/ppermute | solution.py:325
  20.0 3.4 %collective-permute-start.12 = (f32[232,128]{1,0:T(8,128)S(1)}, f32[232,128]{1,0:T(8,128)S(1)}, u32[]{:S(2)}, u32[]{:S(2)}) collective-permute-start(f32[232,128]{1,0:T(8,128)S(1)} %collective-permute-done.8.refs_9_), channel_id=1, source_target_pairs={{0,1},{1,0},{2,3},{3,2},{4,5},{5,4},{6,7},{7,6},{8,9},{9,8},{10,11... | collective-permute-start | bytes 356360 | tf_op jit(solution)/shard_map/ppermute | solution.py:325
  21.9 1.5 %collective-permute-start.14 = (f32[232,128]{1,0:T(8,128)S(1)}, f32[232,128]{1,0:T(8,128)S(1)}, u32[]{:S(2)}, u32[]{:S(2)}) collective-permute-start(f32[232,128]{1,0:T(8,128)S(1)} %collective-permute-done.10.refs_11_), channel_id=1, source_target_pairs={{0,1},{1,0},{2,3},{3,2},{4,5},{5,4},{6,7},{7,6},{8,9},{9,8},{10,11... | collective-permute-start | bytes 356360 | tf_op jit(solution)/shard_map/ppermute | solution.py:325

commit v6 on v5

--- a/solution.py
+++ b/solution.py
@@ -332,13 +332,49 @@
     return line + [swap(a, 1) for a in line], side + [swap(a, 1) for a in side]
 
 
+def pack_kernel(x_ref, y_ref, la_ref, lb_ref, out_ref, la_row, lb_row, sems):
+    s_dev, t_dev = x_ref.shape[0], y_ref.shape[0]
+    rows = s_dev + t_dev
+    copies = [
+        pltpu.make_async_copy(src, dst, sems.at[i])
+        for i, (src, dst) in enumerate(
+            (
+                (x_ref, out_ref.at[0:s_dev, :]),
+                (y_ref, out_ref.at[s_dev:rows, :]),
+                (la_ref, la_row),
+                (lb_ref, lb_row),
+            )
+        )
+    ]
+    for copy in copies:
+        copy.start()
+    out_ref[rows:, :] = jnp.zeros((8, x_ref.shape[1]), jnp.float32)
+    copies[2].wait()
+    out_ref[rows + 1 : rows + 2, 0:s_dev] = la_row[...].reshape(1, s_dev)
+    copies[3].wait()
+    out_ref[rows : rows + 1, :] = lb_row[...].reshape(1, t_dev)
+    copies[0].wait()
+    copies[1].wait()
+
+
 def per_device_whole(source_feats, target_feats, log_a, log_b):
     n = lax.axis_size("src")
     s_dev, feat = source_feats.shape
     t_dev = target_feats.shape[0]
-    masses = jnp.concatenate([log_b, log_a, jnp.zeros((8 * feat - t_dev - s_dev,), jnp.float32)])
-    block = jnp.concatenate([source_feats, target_feats, masses.reshape(8, feat)], axis=0)
-    block = lax.optimization_barrier(block)
+    fixed = [pltpu.with_memory_space_constraint(a, pltpu.HBM) for a in (source_feats, target_feats, log_a, log_b)]
+    block = pl.pallas_call(
+        pack_kernel,
+        out_shape=pltpu.VMEM((s_dev + t_dev + 8, feat), jnp.float32),
+        in_specs=[pl.BlockSpec(memory_space=pltpu.HBM)] * 4,
+        out_specs=pl.BlockSpec(memory_space=pltpu.VMEM),
+        scratch_shapes=[
+            pltpu.VMEM((s_dev,), jnp.float32),
+            pltpu.VMEM((t_dev,), jnp.float32),
+            pltpu.SemaphoreType.DMA((4,)),
+        ],
+        compiler_params=pltpu.CompilerParams(vmem_limit_bytes=2 * 2**20),
+        name="pack",
+    )(*fixed)
     near_pieces, far_pieces = exchange(block, "src")
     sources, targets = n * s_dev, n * t_dev
     half_s, half_t = sources // 2, targets // 2

time: 62.3 us -> 61.6 us (0.989)
  other arithmetic: 1.6 us -> 0 us
  Pallas kernels: 39.9 us -> 40.8 us
    pallas_call x0 -> x1, Pallas kernels: none -> 0.91 us  [per_device_whole(): pl.pallas_call(pack_kernel, out_shape=pltpu.VMEM((s_dev + t_dev + 8, feat...]
    concatenate x1 -> x0, other arithmetic: 0.85 us -> none  [per_device_whole(): jnp.concatenate([source_feats, target_feats, masses.reshape(8, feat)], ax...]
    reshape x1 -> x0, other arithmetic: 0.75 us -> none  [per_device_whole(): masses.reshape(8, feat)]
where the time goes in v6:
time: 61.6 us; the launch traced here: 61.1 us
  Pallas kernels  40.8 us (66%)
  starting transfers between devices  12.1 us (20%)
  waiting for transfers between devices  7.54 us (12%)
  between operations  0.69 us (1%)
    pallas_call x1, Pallas kernels, per_device_whole(): pl.pallas_call(functools.partial(whole_group_kernel, n, s_dev, t_dev, blk...  38.4 us
    ppermute x15, starting transfers between devices, swap(): return lax.ppermute(a, axis, [(i, i ^ bits) for i in range(n)])  12.1 us
    ppermute x15, waiting for transfers between devices, swap(): return lax.ppermute(a, axis, [(i, i ^ bits) for i in range(n)])  7.54 us
    pallas_call x1, Pallas kernels, per_device_whole(): pl.pallas_call(functools.partial(near_kernel, s_dev, t_dev, blk), out_sha...  1.47 us
  transfers between devices with their start and end apart: 15, of which 5 were waited for; matrix products, arithmetic and copies ran while one was open for 0% of the time, Pallas kernels for 2%

profile of v6, /device:TPU:0, one launch (start us, length us, event | category | flops | bytes accessed | tf_op | source)
XLA Modules:
  0.0 61.1 jit_solution(13563094943271041114)
XLA Ops:
  0.6 0.9 %pack.1.refs_0_ = f32[232,128]{1,0:T(8,128)S(1)} custom-call(f32[96,128]{1,0:T(8,128)} %x_ref.1, f32[128,128]{1,0:T(8,128)} %y_ref.1, f32[96]{0:T(128)} %la_ref.1, f32[128]{0:T(128)} %lb_ref.1), custom_call_target="tpu_custom_call" | custom-call | tf_op jit(solution)/shard_map/pack/pallas_call | solution.py:365
  1.5 4.1 %collective-permute-start.1 = (f32[232,128]{1,0:T(8,128)S(1)}, f32[232,128]{1,0:T(8,128)S(1)}, u32[]{:S(2)}, u32[]{:S(2)}) collective-permute-start(f32[232,128]{1,0:T(8,128)S(1)} %pack.1.refs_0_), channel_id=1, source_target_pairs={{0,8},{1,9},{2,10},{3,11},{4,12},{5,13},{6,14},{7,15},{8,0},{9,1},... | collective-permute-start | bytes 356360 | tf_op jit(solution)/shard_map/ppermute | solution.py:325
  5.6 1.5 %collective-permute-start.7 = (f32[232,128]{1,0:T(8,128)S(1)}, f32[232,128]{1,0:T(8,128)S(1)}, u32[]{:S(2)}, u32[]{:S(2)}) collective-permute-start(f32[232,128]{1,0:T(8,128)S(1)} %pack.1.refs_0_), channel_id=1, source_target_pairs={{0,2},{1,3},{2,0},{3,1},{4,6},{5,7},{6,4},{7,5},{8,10},{9,11},{10,... | collective-permute-start | bytes 356360 | tf_op jit(solution)/shard_map/ppermute | solution.py:325
  7.2 1.6 %collective-permute-start = (f32[232,128]{1,0:T(8,128)S(1)}, f32[232,128]{1,0:T(8,128)S(1)}, u32[]{:S(2)}, u32[]{:S(2)}) collective-permute-start(f32[232,128]{1,0:T(8,128)S(1)} %pack.1.refs_0_), channel_id=1, source_target_pairs={{0,4},{1,5},{2,6},{3,7},{4,0},{5,1},{6,2},{7,3},{8,12},{9,13},{10,... | collective-permute-start | bytes 356360 | tf_op jit(solution)/shard_map/ppermute | solution.py:325
  8.7 0.0 collective-permute-start.3
  8.7 2.8 %collective-permute-done.1.refs_2_ = f32[232,128]{1,0:T(8,128)S(1)} collective-permute-done((f32[232,128]{1,0:T(8,128)S(1)}, f32[232,128]{1,0:T(8,128)S(1)}, u32[]{:S(2)}, u32[]{:S(2)}) %collective-permute-start.1) | collective-permute-done | bytes 118816 | tf_op jit(solution)/shard_map/ppermute | solution.py:325
  11.5 1.6 %collective-permute-start.9 = (f32[232,128]{1,0:T(8,128)S(1)}, f32[232,128]{1,0:T(8,128)S(1)}, u32[]{:S(2)}, u32[]{:S(2)}) collective-permute-start(f32[232,128]{1,0:T(8,128)S(1)} %collective-permute-done.1.refs_2_), channel_id=1, source_target_pairs={{0,2},{1,3},{2,0},{3,1},{4,6},{5,7},{6,4},{7,5},{8,10},{9,11},{10,... | collective-permute-start | bytes 356360 | tf_op jit(solution)/shard_map/ppermute | solution.py:325
  13.1 0.6 collective-permute-start.2
  13.7 0.0 collective-permute-done.7.refs_8_
  13.7 0.0 collective-permute-start.5
  13.7 0.0 collective-permute-done.refs_1_
  13.7 0.6 %collective-permute-start.8 = (f32[232,128]{1,0:T(8,128)S(1)}, f32[232,128]{1,0:T(8,128)S(1)}, u32[]{:S(2)}, u32[]{:S(2)}) collective-permute-start(f32[232,128]{1,0:T(8,128)S(1)} %collective-permute-done.refs_1_), channel_id=1, source_target_pairs={{0,2},{1,3},{2,0},{3,1},{4,6},{5,7},{6,4},{7,5},{8,10},{9,11},{10,... | collective-permute-start | bytes 356360 | tf_op jit(solution)/shard_map/ppermute | solution.py:325
  14.3 0.0 collective-permute-done.3.refs_4_
  14.3 0.2 collective-permute-start.4
  14.5 1.9 %collective-permute-done.9.refs_10_ = f32[232,128]{1,0:T(8,128)S(1)} collective-permute-done((f32[232,128]{1,0:T(8,128)S(1)}, f32[232,128]{1,0:T(8,128)S(1)}, u32[]{:S(2)}, u32[]{:S(2)}) %collective-permute-start.9) | collective-permute-done | bytes 118816 | tf_op jit(solution)/shard_map/ppermute | solution.py:325
  16.4 1.0 %collective-permute-start.10 = (f32[232,128]{1,0:T(8,128)S(1)}, f32[232,128]{1,0:T(8,128)S(1)}, u32[]{:S(2)}, u32[]{:S(2)}) collective-permute-start(f32[232,128]{1,0:T(8,128)S(1)} %collective-permute-done.9.refs_10_), channel_id=1, source_target_pairs={{0,4},{1,5},{2,6},{3,7},{4,0},{5,1},{6,2},{7,3},{8,12},{9,13},{10,... | collective-permute-start | bytes 356360 | tf_op jit(solution)/shard_map/ppermute | solution.py:325
  17.3 1.2 %collective-permute-done.2.refs_3_ = f32[232,128]{1,0:T(8,128)S(1)} collective-permute-done((f32[232,128]{1,0:T(8,128)S(1)}, f32[232,128]{1,0:T(8,128)S(1)}, u32[]{:S(2)}, u32[]{:S(2)}) %collective-permute-start.2) | collective-permute-done | bytes 118816 | tf_op jit(solution)/shard_map/ppermute | solution.py:325
  18.5 0.0 collective-permute-start.6
  18.5 0.0 collective-permute-done.5.refs_6_
  18.5 0.5 collective-permute-start.11
  19.0 0.3 collective-permute-done.8.refs_9_
  19.3 0.0 collective-permute-start.13
  19.3 0.0 collective-permute-done.4.refs_5_
  19.3 0.5 collective-permute-start.12
  19.8 1.4 %collective-permute-done.10.refs_11_ = f32[232,128]{1,0:T(8,128)S(1)} collective-permute-done((f32[232,128]{1,0:T(8,128)S(1)}, f32[232,128]{1,0:T(8,128)S(1)}, u32[]{:S(2)}, u32[]{:S(2)}) %collective-permute-start.10) | collective-permute-done | bytes 118816 | tf_op jit(solution)/shard_map/ppermute | solution.py:325
  21.2 0.0 collective-permute-start.14
  21.2 0.0 collective-permute-done.6.refs_7_
  21.2 1.5 %near.1 = (f32[768,1024]{1,0:T(8,128)S(1)}, bf16[768,512]{1,0:T(8,128)(2,1)S(1)}, bf16[1024,512]{1,0:T(8,128)(2,1)S(1)}, f32[768,1]{1,0:T(8,128)S(1)}, f32[1,1024]{1,0:T(1,128)S(1)}, /*index=5*/f32[8,128]{1,0:T(8,128)S(1)}) custom-call(f32[232,128]{1,0:T(8,128)S(1)} %pack.1.refs_0_, f32[232,128]{1,0:T(8,128)S(1)} %collective-permute-done.refs_1_, ...), custom_call_target="tpu_custom_call" | custom-call | flops 805306368 | bytes 8388608 | tf_op jit(solution)/shard_map/near/pallas_call | solution.py:384
  22.7 0.0 collective-permute-done.11.refs_12_
  22.7 0.0 collective-permute-done.13.refs_14_
  22.7 0.0 collective-permute-done.12.refs_13_
  22.7 0.0 collective-permute-done.14.refs_15_
  22.7 38.4 %whole_group.1 = (f32[1,96]{1,0:T(1,128)}, f32[1,128]{1,0:T(1,128)}, f32[96,128]{1,0:T(8,128)}, f32[128,128]{1,0:T(8,128)}) custom-call(f32[232,128]{1,0:T(8,128)S(1)} %pack.1.refs_0_, f32[232,128]{1,0:T(8,128)S(1)} %collective-permute-done.refs_1_, f32[232,128]{1,0:T(8,128)S(1)} %collective-permute-done.1.refs_2_, ...), custom_call_target="tpu_custom_call" | custom-call | tf_op jit(solution)/shard_map/whole_group/pallas_call | solution.py:404
Async XLA Ops:
  1.5 10.0 %collective-permute-start.1 = (f32[232,128]{1,0:T(8,128)S(1)}, f32[232,128]{1,0:T(8,128)S(1)}, u32[]{:S(2)}, u32[]{:S(2)}) collective-permute-start(f32[232,128]{1,0:T(8,128)S(1)} %pack.1.refs_0_), channel_id=1, source_target_pairs={{0,8},{1,9},{2,10},{3,11},{4,12},{5,13},{6,14},{7,15},{8,0},{9,1},... | collective-permute-start | bytes 356360 | tf_op jit(solution)/shard_map/ppermute | solution.py:325
  5.6 8.0 %collective-permute-start.7 = (f32[232,128]{1,0:T(8,128)S(1)}, f32[232,128]{1,0:T(8,128)S(1)}, u32[]{:S(2)}, u32[]{:S(2)}) collective-permute-start(f32[232,128]{1,0:T(8,128)S(1)} %pack.1.refs_0_), channel_id=1, source_target_pairs={{0,2},{1,3},{2,0},{3,1},{4,6},{5,7},{6,4},{7,5},{8,10},{9,11},{10,... | collective-permute-start | bytes 356360 | tf_op jit(solution)/shard_map/ppermute | solution.py:325
  7.2 6.5 %collective-permute-start = (f32[232,128]{1,0:T(8,128)S(1)}, f32[232,128]{1,0:T(8,128)S(1)}, u32[]{:S(2)}, u32[]{:S(2)}) collective-permute-start(f32[232,128]{1,0:T(8,128)S(1)} %pack.1.refs_0_), channel_id=1, source_target_pairs={{0,4},{1,5},{2,6},{3,7},{4,0},{5,1},{6,2},{7,3},{8,12},{9,13},{10,... | collective-permute-start | bytes 356360 | tf_op jit(solution)/shard_map/ppermute | solution.py:325
  8.7 5.6 %collective-permute-start.3 = (f32[232,128]{1,0:T(8,128)S(1)}, f32[232,128]{1,0:T(8,128)S(1)}, u32[]{:S(2)}, u32[]{:S(2)}) collective-permute-start(f32[232,128]{1,0:T(8,128)S(1)} %pack.1.refs_0_), channel_id=1, source_target_pairs={{0,1},{1,0},{2,3},{3,2},{4,5},{5,4},{6,7},{7,6},{8,9},{9,8},{10,11... | collective-permute-start | bytes 356360 | tf_op jit(solution)/shard_map/ppermute | solution.py:325
  11.5 4.8 %collective-permute-start.9 = (f32[232,128]{1,0:T(8,128)S(1)}, f32[232,128]{1,0:T(8,128)S(1)}, u32[]{:S(2)}, u32[]{:S(2)}) collective-permute-start(f32[232,128]{1,0:T(8,128)S(1)} %collective-permute-done.1.refs_2_), channel_id=1, source_target_pairs={{0,2},{1,3},{2,0},{3,1},{4,6},{5,7},{6,4},{7,5},{8,10},{9,11},{10,... | collective-permute-start | bytes 356360 | tf_op jit(solution)/shard_map/ppermute | solution.py:325
  13.1 5.4 %collective-permute-start.2 = (f32[232,128]{1,0:T(8,128)S(1)}, f32[232,128]{1,0:T(8,128)S(1)}, u32[]{:S(2)}, u32[]{:S(2)}) collective-permute-start(f32[232,128]{1,0:T(8,128)S(1)} %collective-permute-done.1.refs_2_), channel_id=1, source_target_pairs={{0,4},{1,5},{2,6},{3,7},{4,0},{5,1},{6,2},{7,3},{8,12},{9,13},{10,... | collective-permute-start | bytes 356360 | tf_op jit(solution)/shard_map/ppermute | solution.py:325
  13.7 4.8 %collective-permute-start.5 = (f32[232,128]{1,0:T(8,128)S(1)}, f32[232,128]{1,0:T(8,128)S(1)}, u32[]{:S(2)}, u32[]{:S(2)}) collective-permute-start(f32[232,128]{1,0:T(8,128)S(1)} %collective-permute-done.1.refs_2_), channel_id=1, source_target_pairs={{0,1},{1,0},{2,3},{3,2},{4,5},{5,4},{6,7},{7,6},{8,9},{9,8},{10,11... | collective-permute-start | bytes 356360 | tf_op jit(solution)/shard_map/ppermute | solution.py:325
  13.7 5.6 %collective-permute-start.8 = (f32[232,128]{1,0:T(8,128)S(1)}, f32[232,128]{1,0:T(8,128)S(1)}, u32[]{:S(2)}, u32[]{:S(2)}) collective-permute-start(f32[232,128]{1,0:T(8,128)S(1)} %collective-permute-done.refs_1_), channel_id=1, source_target_pairs={{0,2},{1,3},{2,0},{3,1},{4,6},{5,7},{6,4},{7,5},{8,10},{9,11},{10,... | collective-permute-start | bytes 356360 | tf_op jit(solution)/shard_map/ppermute | solution.py:325
  14.3 5.0 %collective-permute-start.4 = (f32[232,128]{1,0:T(8,128)S(1)}, f32[232,128]{1,0:T(8,128)S(1)}, u32[]{:S(2)}, u32[]{:S(2)}) collective-permute-start(f32[232,128]{1,0:T(8,128)S(1)} %collective-permute-done.refs_1_), channel_id=1, source_target_pairs={{0,1},{1,0},{2,3},{3,2},{4,5},{5,4},{6,7},{7,6},{8,9},{9,8},{10,11... | collective-permute-start | bytes 356360 | tf_op jit(solution)/shard_map/ppermute | solution.py:325
  16.4 4.8 %collective-permute-start.10 = (f32[232,128]{1,0:T(8,128)S(1)}, f32[232,128]{1,0:T(8,128)S(1)}, u32[]{:S(2)}, u32[]{:S(2)}) collective-permute-start(f32[232,128]{1,0:T(8,128)S(1)} %collective-permute-done.9.refs_10_), channel_id=1, source_target_pairs={{0,4},{1,5},{2,6},{3,7},{4,0},{5,1},{6,2},{7,3},{8,12},{9,13},{10,... | collective-permute-start | bytes 356360 | tf_op jit(solution)/shard_map/ppermute | solution.py:325
  18.5 2.7 %collective-permute-start.6 = (f32[232,128]{1,0:T(8,128)S(1)}, f32[232,128]{1,0:T(8,128)S(1)}, u32[]{:S(2)}, u32[]{:S(2)}) collective-permute-start(f32[232,128]{1,0:T(8,128)S(1)} %collective-permute-done.2.refs_3_), channel_id=1, source_target_pairs={{0,1},{1,0},{2,3},{3,2},{4,5},{5,4},{6,7},{7,6},{8,9},{9,8},{10,11... | collective-permute-start | bytes 356360 | tf_op jit(solution)/shard_map/ppermute | solution.py:325
  18.5 4.2 %collective-permute-start.11 = (f32[232,128]{1,0:T(8,128)S(1)}, f32[232,128]{1,0:T(8,128)S(1)}, u32[]{:S(2)}, u32[]{:S(2)}) collective-permute-start(f32[232,128]{1,0:T(8,128)S(1)} %collective-permute-done.7.refs_8_), channel_id=1, source_target_pairs={{0,1},{1,0},{2,3},{3,2},{4,5},{5,4},{6,7},{7,6},{8,9},{9,8},{10,11... | collective-permute-start | bytes 356360 | tf_op jit(solution)/shard_map/ppermute | solution.py:325
  19.3 3.4 %collective-permute-start.13 = (f32[232,128]{1,0:T(8,128)S(1)}, f32[232,128]{1,0:T(8,128)S(1)}, u32[]{:S(2)}, u32[]{:S(2)}) collective-permute-start(f32[232,128]{1,0:T(8,128)S(1)} %collective-permute-done.9.refs_10_), channel_id=1, source_target_pairs={{0,1},{1,0},{2,3},{3,2},{4,5},{5,4},{6,7},{7,6},{8,9},{9,8},{10,11... | collective-permute-start | bytes 356360 | tf_op jit(solution)/shard_map/ppermute | solution.py:325
  19.3 3.4 %collective-permute-start.12 = (f32[232,128]{1,0:T(8,128)S(1)}, f32[232,128]{1,0:T(8,128)S(1)}, u32[]{:S(2)}, u32[]{:S(2)}) collective-permute-start(f32[232,128]{1,0:T(8,128)S(1)} %collective-permute-done.8.refs_9_), channel_id=1, source_target_pairs={{0,1},{1,0},{2,3},{3,2},{4,5},{5,4},{6,7},{7,6},{8,9},{9,8},{10,11... | collective-permute-start | bytes 356360 | tf_op jit(solution)/shard_map/ppermute | solution.py:325
  21.2 1.5 %collective-permute-start.14 = (f32[232,128]{1,0:T(8,128)S(1)}, f32[232,128]{1,0:T(8,128)S(1)}, u32[]{:S(2)}, u32[]{:S(2)}) collective-permute-start(f32[232,128]{1,0:T(8,128)S(1)} %collective-permute-done.10.refs_11_), channel_id=1, source_target_pairs={{0,1},{1,0},{2,3},{3,2},{4,5},{5,4},{6,7},{7,6},{8,9},{9,8},{10,11... | collective-permute-start | bytes 356360 | tf_op jit(solution)/shard_map/ppermute | solution.py:325

commit v7 on v6

--- a/solution.py
+++ b/solution.py
@@ -225,7 +225,6 @@
             kept, s = halves(i)
             e0, e1 = kept[0][s, :], kept[1][s, :]
             r = jnp.sum(e0 * v[0] + e1 * v[1], axis=1, keepdims=True)
-            sums.extend(r[p * sub : (p + 1) * sub, :] for p in range(parts))
             u = la_col[i * blk : (i + 1) * blk, :] / r
             acc0[...] += column_part(e0, u)
             acc1[...] += column_part(e1, u)
@@ -247,7 +246,7 @@
     put_sources((e11[0:s_dev, :] * v[0], e12[0:s_dev, :] * v[1]))
 
     low_r, high_r, low_c, high_c = least(sums), most(sums), least(ends), most(ends)
-    bad = jnp.max(jnp.where((low_r < 1.0 / SAFE) | (high_r > WIDE), 1.0, 0.0)) + jnp.max(
+    bad = jnp.max(jnp.where((low_r < 1.0) | (high_r > WIDE), 1.0, 0.0)) + jnp.max(
         jnp.where((low_c < 1.0 / SAFE) | (high_c > SAFE), 1.0, 0.0)
     )
     finite = (jnp.max(high_r) < WIDE) & (jnp.max(high_c) < SAFE)

time: 61.6 us -> 61.5 us (level)
  no operation moved by 1% of the time
where the time goes in v7:
time: 61.5 us; the launch traced here: 61 us
  Pallas kernels  40.7 us (66%)
  starting transfers between devices  12.1 us (20%)
  waiting for transfers between devices  7.54 us (12%)
  between operations  0.69 us (1%)
    pallas_call x1, Pallas kernels, per_device_whole(): pl.pallas_call(functools.partial(whole_group_kernel, n, s_dev, t_dev, blk...  38.3 us
    ppermute x15, starting transfers between devices, swap(): return lax.ppermute(a, axis, [(i, i ^ bits) for i in range(n)])  12.1 us
    ppermute x15, waiting for transfers between devices, swap(): return lax.ppermute(a, axis, [(i, i ^ bits) for i in range(n)])  7.54 us
    pallas_call x1, Pallas kernels, per_device_whole(): pl.pallas_call(functools.partial(near_kernel, s_dev, t_dev, blk), out_sha...  1.47 us
  transfers between devices with their start and end apart: 15, of which 5 were waited for; matrix products, arithmetic and copies ran while one was open for 0% of the time, Pallas kernels for 2%

profile of v7, /device:TPU:0, one launch (start us, length us, event | category | flops | bytes accessed | tf_op | source)
XLA Modules:
  0.0 61.0 jit_solution(5205534437541265602)
XLA Ops:
  0.6 0.9 %pack.1.refs_0_ = f32[232,128]{1,0:T(8,128)S(1)} custom-call(f32[96,128]{1,0:T(8,128)} %x_ref.1, f32[128,128]{1,0:T(8,128)} %y_ref.1, f32[96]{0:T(128)} %la_ref.1, f32[128]{0:T(128)} %lb_ref.1), custom_call_target="tpu_custom_call" | custom-call | tf_op jit(solution)/shard_map/pack/pallas_call | solution.py:364
  1.5 4.1 %collective-permute-start.1 = (f32[232,128]{1,0:T(8,128)S(1)}, f32[232,128]{1,0:T(8,128)S(1)}, u32[]{:S(2)}, u32[]{:S(2)}) collective-permute-start(f32[232,128]{1,0:T(8,128)S(1)} %pack.1.refs_0_), channel_id=1, source_target_pairs={{0,8},{1,9},{2,10},{3,11},{4,12},{5,13},{6,14},{7,15},{8,0},{9,1},... | collective-permute-start | bytes 356360 | tf_op jit(solution)/shard_map/ppermute | solution.py:324
  5.6 1.5 %collective-permute-start.7 = (f32[232,128]{1,0:T(8,128)S(1)}, f32[232,128]{1,0:T(8,128)S(1)}, u32[]{:S(2)}, u32[]{:S(2)}) collective-permute-start(f32[232,128]{1,0:T(8,128)S(1)} %pack.1.refs_0_), channel_id=1, source_target_pairs={{0,2},{1,3},{2,0},{3,1},{4,6},{5,7},{6,4},{7,5},{8,10},{9,11},{10,... | collective-permute-start | bytes 356360 | tf_op jit(solution)/shard_map/ppermute | solution.py:324
  7.2 1.6 %collective-permute-start = (f32[232,128]{1,0:T(8,128)S(1)}, f32[232,128]{1,0:T(8,128)S(1)}, u32[]{:S(2)}, u32[]{:S(2)}) collective-permute-start(f32[232,128]{1,0:T(8,128)S(1)} %pack.1.refs_0_), channel_id=1, source_target_pairs={{0,4},{1,5},{2,6},{3,7},{4,0},{5,1},{6,2},{7,3},{8,12},{9,13},{10,... | collective-permute-start | bytes 356360 | tf_op jit(solution)/shard_map/ppermute | solution.py:324
  8.7 0.0 collective-permute-start.3
  8.7 2.8 %collective-permute-done.1.refs_2_ = f32[232,128]{1,0:T(8,128)S(1)} collective-permute-done((f32[232,128]{1,0:T(8,128)S(1)}, f32[232,128]{1,0:T(8,128)S(1)}, u32[]{:S(2)}, u32[]{:S(2)}) %collective-permute-start.1) | collective-permute-done | bytes 118816 | tf_op jit(solution)/shard_map/ppermute | solution.py:324
  11.5 1.6 %collective-permute-start.9 = (f32[232,128]{1,0:T(8,128)S(1)}, f32[232,128]{1,0:T(8,128)S(1)}, u32[]{:S(2)}, u32[]{:S(2)}) collective-permute-start(f32[232,128]{1,0:T(8,128)S(1)} %collective-permute-done.1.refs_2_), channel_id=1, source_target_pairs={{0,2},{1,3},{2,0},{3,1},{4,6},{5,7},{6,4},{7,5},{8,10},{9,11},{10,... | collective-permute-start | bytes 356360 | tf_op jit(solution)/shard_map/ppermute | solution.py:324
  13.1 0.6 collective-permute-start.2
  13.7 0.0 collective-permute-done.7.refs_8_
  13.7 0.0 collective-permute-start.5
  13.7 0.0 collective-permute-done.refs_1_
  13.7 0.6 %collective-permute-start.8 = (f32[232,128]{1,0:T(8,128)S(1)}, f32[232,128]{1,0:T(8,128)S(1)}, u32[]{:S(2)}, u32[]{:S(2)}) collective-permute-start(f32[232,128]{1,0:T(8,128)S(1)} %collective-permute-done.refs_1_), channel_id=1, source_target_pairs={{0,2},{1,3},{2,0},{3,1},{4,6},{5,7},{6,4},{7,5},{8,10},{9,11},{10,... | collective-permute-start | bytes 356360 | tf_op jit(solution)/shard_map/ppermute | solution.py:324
  14.3 0.0 collective-permute-done.3.refs_4_
  14.3 0.2 collective-permute-start.4
  14.5 1.9 %collective-permute-done.9.refs_10_ = f32[232,128]{1,0:T(8,128)S(1)} collective-permute-done((f32[232,128]{1,0:T(8,128)S(1)}, f32[232,128]{1,0:T(8,128)S(1)}, u32[]{:S(2)}, u32[]{:S(2)}) %collective-permute-start.9) | collective-permute-done | bytes 118816 | tf_op jit(solution)/shard_map/ppermute | solution.py:324
  16.4 1.0 %collective-permute-start.10 = (f32[232,128]{1,0:T(8,128)S(1)}, f32[232,128]{1,0:T(8,128)S(1)}, u32[]{:S(2)}, u32[]{:S(2)}) collective-permute-start(f32[232,128]{1,0:T(8,128)S(1)} %collective-permute-done.9.refs_10_), channel_id=1, source_target_pairs={{0,4},{1,5},{2,6},{3,7},{4,0},{5,1},{6,2},{7,3},{8,12},{9,13},{10,... | collective-permute-start | bytes 356360 | tf_op jit(solution)/shard_map/ppermute | solution.py:324
  17.3 1.2 %collective-permute-done.2.refs_3_ = f32[232,128]{1,0:T(8,128)S(1)} collective-permute-done((f32[232,128]{1,0:T(8,128)S(1)}, f32[232,128]{1,0:T(8,128)S(1)}, u32[]{:S(2)}, u32[]{:S(2)}) %collective-permute-start.2) | collective-permute-done | bytes 118816 | tf_op jit(solution)/shard_map/ppermute | solution.py:324
  18.5 0.0 collective-permute-start.6
  18.5 0.0 collective-permute-done.5.refs_6_
  18.5 0.5 collective-permute-start.11
  19.0 0.3 collective-permute-done.8.refs_9_
  19.3 0.0 collective-permute-start.13
  19.3 0.0 collective-permute-done.4.refs_5_
  19.3 0.5 collective-permute-start.12
  19.8 1.4 %collective-permute-done.10.refs_11_ = f32[232,128]{1,0:T(8,128)S(1)} collective-permute-done((f32[232,128]{1,0:T(8,128)S(1)}, f32[232,128]{1,0:T(8,128)S(1)}, u32[]{:S(2)}, u32[]{:S(2)}) %collective-permute-start.10) | collective-permute-done | bytes 118816 | tf_op jit(solution)/shard_map/ppermute | solution.py:324
  21.2 0.0 collective-permute-start.14
  21.2 0.0 collective-permute-done.6.refs_7_
  21.2 1.5 %near.1 = (f32[768,1024]{1,0:T(8,128)S(1)}, bf16[768,512]{1,0:T(8,128)(2,1)S(1)}, bf16[1024,512]{1,0:T(8,128)(2,1)S(1)}, f32[768,1]{1,0:T(8,128)S(1)}, f32[1,1024]{1,0:T(1,128)S(1)}, /*index=5*/f32[8,128]{1,0:T(8,128)S(1)}) custom-call(f32[232,128]{1,0:T(8,128)S(1)} %pack.1.refs_0_, f32[232,128]{1,0:T(8,128)S(1)} %collective-permute-done.refs_1_, ...), custom_call_target="tpu_custom_call" | custom-call | flops 805306368 | bytes 8388608 | tf_op jit(solution)/shard_map/near/pallas_call | solution.py:383
  22.7 0.0 collective-permute-done.11.refs_12_
  22.7 0.0 collective-permute-done.13.refs_14_
  22.7 0.0 collective-permute-done.12.refs_13_
  22.7 0.0 collective-permute-done.14.refs_15_
  22.7 38.3 %whole_group.1 = (f32[1,96]{1,0:T(1,128)}, f32[1,128]{1,0:T(1,128)}, f32[96,128]{1,0:T(8,128)}, f32[128,128]{1,0:T(8,128)}) custom-call(f32[232,128]{1,0:T(8,128)S(1)} %pack.1.refs_0_, f32[232,128]{1,0:T(8,128)S(1)} %collective-permute-done.refs_1_, f32[232,128]{1,0:T(8,128)S(1)} %collective-permute-done.1.refs_2_, ...), custom_call_target="tpu_custom_call" | custom-call | tf_op jit(solution)/shard_map/whole_group/pallas_call | solution.py:403
Async XLA Ops:
  1.5 10.0 %collective-permute-start.1 = (f32[232,128]{1,0:T(8,128)S(1)}, f32[232,128]{1,0:T(8,128)S(1)}, u32[]{:S(2)}, u32[]{:S(2)}) collective-permute-start(f32[232,128]{1,0:T(8,128)S(1)} %pack.1.refs_0_), channel_id=1, source_target_pairs={{0,8},{1,9},{2,10},{3,11},{4,12},{5,13},{6,14},{7,15},{8,0},{9,1},... | collective-permute-start | bytes 356360 | tf_op jit(solution)/shard_map/ppermute | solution.py:324
  5.6 8.0 %collective-permute-start.7 = (f32[232,128]{1,0:T(8,128)S(1)}, f32[232,128]{1,0:T(8,128)S(1)}, u32[]{:S(2)}, u32[]{:S(2)}) collective-permute-start(f32[232,128]{1,0:T(8,128)S(1)} %pack.1.refs_0_), channel_id=1, source_target_pairs={{0,2},{1,3},{2,0},{3,1},{4,6},{5,7},{6,4},{7,5},{8,10},{9,11},{10,... | collective-permute-start | bytes 356360 | tf_op jit(solution)/shard_map/ppermute | solution.py:324
  7.2 6.5 %collective-permute-start = (f32[232,128]{1,0:T(8,128)S(1)}, f32[232,128]{1,0:T(8,128)S(1)}, u32[]{:S(2)}, u32[]{:S(2)}) collective-permute-start(f32[232,128]{1,0:T(8,128)S(1)} %pack.1.refs_0_), channel_id=1, source_target_pairs={{0,4},{1,5},{2,6},{3,7},{4,0},{5,1},{6,2},{7,3},{8,12},{9,13},{10,... | collective-permute-start | bytes 356360 | tf_op jit(solution)/shard_map/ppermute | solution.py:324
  8.7 5.6 %collective-permute-start.3 = (f32[232,128]{1,0:T(8,128)S(1)}, f32[232,128]{1,0:T(8,128)S(1)}, u32[]{:S(2)}, u32[]{:S(2)}) collective-permute-start(f32[232,128]{1,0:T(8,128)S(1)} %pack.1.refs_0_), channel_id=1, source_target_pairs={{0,1},{1,0},{2,3},{3,2},{4,5},{5,4},{6,7},{7,6},{8,9},{9,8},{10,11... | collective-permute-start | bytes 356360 | tf_op jit(solution)/shard_map/ppermute | solution.py:324
  11.5 4.8 %collective-permute-start.9 = (f32[232,128]{1,0:T(8,128)S(1)}, f32[232,128]{1,0:T(8,128)S(1)}, u32[]{:S(2)}, u32[]{:S(2)}) collective-permute-start(f32[232,128]{1,0:T(8,128)S(1)} %collective-permute-done.1.refs_2_), channel_id=1, source_target_pairs={{0,2},{1,3},{2,0},{3,1},{4,6},{5,7},{6,4},{7,5},{8,10},{9,11},{10,... | collective-permute-start | bytes 356360 | tf_op jit(solution)/shard_map/ppermute | solution.py:324
  13.1 5.4 %collective-permute-start.2 = (f32[232,128]{1,0:T(8,128)S(1)}, f32[232,128]{1,0:T(8,128)S(1)}, u32[]{:S(2)}, u32[]{:S(2)}) collective-permute-start(f32[232,128]{1,0:T(8,128)S(1)} %collective-permute-done.1.refs_2_), channel_id=1, source_target_pairs={{0,4},{1,5},{2,6},{3,7},{4,0},{5,1},{6,2},{7,3},{8,12},{9,13},{10,... | collective-permute-start | bytes 356360 | tf_op jit(solution)/shard_map/ppermute | solution.py:324
  13.7 4.8 %collective-permute-start.5 = (f32[232,128]{1,0:T(8,128)S(1)}, f32[232,128]{1,0:T(8,128)S(1)}, u32[]{:S(2)}, u32[]{:S(2)}) collective-permute-start(f32[232,128]{1,0:T(8,128)S(1)} %collective-permute-done.1.refs_2_), channel_id=1, source_target_pairs={{0,1},{1,0},{2,3},{3,2},{4,5},{5,4},{6,7},{7,6},{8,9},{9,8},{10,11... | collective-permute-start | bytes 356360 | tf_op jit(solution)/shard_map/ppermute | solution.py:324
  13.7 5.6 %collective-permute-start.8 = (f32[232,128]{1,0:T(8,128)S(1)}, f32[232,128]{1,0:T(8,128)S(1)}, u32[]{:S(2)}, u32[]{:S(2)}) collective-permute-start(f32[232,128]{1,0:T(8,128)S(1)} %collective-permute-done.refs_1_), channel_id=1, source_target_pairs={{0,2},{1,3},{2,0},{3,1},{4,6},{5,7},{6,4},{7,5},{8,10},{9,11},{10,... | collective-permute-start | bytes 356360 | tf_op jit(solution)/shard_map/ppermute | solution.py:324
  14.3 5.0 %collective-permute-start.4 = (f32[232,128]{1,0:T(8,128)S(1)}, f32[232,128]{1,0:T(8,128)S(1)}, u32[]{:S(2)}, u32[]{:S(2)}) collective-permute-start(f32[232,128]{1,0:T(8,128)S(1)} %collective-permute-done.refs_1_), channel_id=1, source_target_pairs={{0,1},{1,0},{2,3},{3,2},{4,5},{5,4},{6,7},{7,6},{8,9},{9,8},{10,11... | collective-permute-start | bytes 356360 | tf_op jit(solution)/shard_map/ppermute | solution.py:324
  16.4 4.8 %collective-permute-start.10 = (f32[232,128]{1,0:T(8,128)S(1)}, f32[232,128]{1,0:T(8,128)S(1)}, u32[]{:S(2)}, u32[]{:S(2)}) collective-permute-start(f32[232,128]{1,0:T(8,128)S(1)} %collective-permute-done.9.refs_10_), channel_id=1, source_target_pairs={{0,4},{1,5},{2,6},{3,7},{4,0},{5,1},{6,2},{7,3},{8,12},{9,13},{10,... | collective-permute-start | bytes 356360 | tf_op jit(solution)/shard_map/ppermute | solution.py:324
  18.5 2.7 %collective-permute-start.6 = (f32[232,128]{1,0:T(8,128)S(1)}, f32[232,128]{1,0:T(8,128)S(1)}, u32[]{:S(2)}, u32[]{:S(2)}) collective-permute-start(f32[232,128]{1,0:T(8,128)S(1)} %collective-permute-done.2.refs_3_), channel_id=1, source_target_pairs={{0,1},{1,0},{2,3},{3,2},{4,5},{5,4},{6,7},{7,6},{8,9},{9,8},{10,11... | collective-permute-start | bytes 356360 | tf_op jit(solution)/shard_map/ppermute | solution.py:324
  18.5 4.2 %collective-permute-start.11 = (f32[232,128]{1,0:T(8,128)S(1)}, f32[232,128]{1,0:T(8,128)S(1)}, u32[]{:S(2)}, u32[]{:S(2)}) collective-permute-start(f32[232,128]{1,0:T(8,128)S(1)} %collective-permute-done.7.refs_8_), channel_id=1, source_target_pairs={{0,1},{1,0},{2,3},{3,2},{4,5},{5,4},{6,7},{7,6},{8,9},{9,8},{10,11... | collective-permute-start | bytes 356360 | tf_op jit(solution)/shard_map/ppermute | solution.py:324
  19.3 3.4 %collective-permute-start.13 = (f32[232,128]{1,0:T(8,128)S(1)}, f32[232,128]{1,0:T(8,128)S(1)}, u32[]{:S(2)}, u32[]{:S(2)}) collective-permute-start(f32[232,128]{1,0:T(8,128)S(1)} %collective-permute-done.9.refs_10_), channel_id=1, source_target_pairs={{0,1},{1,0},{2,3},{3,2},{4,5},{5,4},{6,7},{7,6},{8,9},{9,8},{10,11... | collective-permute-start | bytes 356360 | tf_op jit(solution)/shard_map/ppermute | solution.py:324
  19.3 3.4 %collective-permute-start.12 = (f32[232,128]{1,0:T(8,128)S(1)}, f32[232,128]{1,0:T(8,128)S(1)}, u32[]{:S(2)}, u32[]{:S(2)}) collective-permute-start(f32[232,128]{1,0:T(8,128)S(1)} %collective-permute-done.8.refs_9_), channel_id=1, source_target_pairs={{0,1},{1,0},{2,3},{3,2},{4,5},{5,4},{6,7},{7,6},{8,9},{9,8},{10,11... | collective-permute-start | bytes 356360 | tf_op jit(solution)/shard_map/ppermute | solution.py:324
  21.2 1.5 %collective-permute-start.14 = (f32[232,128]{1,0:T(8,128)S(1)}, f32[232,128]{1,0:T(8,128)S(1)}, u32[]{:S(2)}, u32[]{:S(2)}) collective-permute-start(f32[232,128]{1,0:T(8,128)S(1)} %collective-permute-done.10.refs_11_), channel_id=1, source_target_pairs={{0,1},{1,0},{2,3},{3,2},{4,5},{5,4},{6,7},{7,6},{8,9},{9,8},{10,11... | collective-permute-start | bytes 356360 | tf_op jit(solution)/shard_map/ppermute | solution.py:324
